TPU v7x, 256 devices: a whole 4x4x8 slice. The times are simulated.
256 devices in a mesh: bands: 8 (over z_hi, core), gy: 4 (over x), gz: 8 (over z_lo, y).
Axes of the slice: x: 4, y: 4, z: 8 (z_hi: 4, z_lo: 2; z = z_hi * 2 + z_lo), core: 2. Of those that a mesh axis runs over, the one named last changes fastest.
Arguments:
- orbitals: float32 [16, 64, 128, 128], P('bands', 'gy', 'gz'), may hold values from -6 to 6
- orbital_shift: float32 [16], P('bands'), may hold values from 0.1 to 1
- occupation: float32 [16], P('bands'), may hold values from 0.03125 to 0.125
- potential: float32 [64, 128, 128], P('gy', 'gz'), may hold values from 0.1 to 2
- perturbation: float32 [64, 128, 128], P('gy', 'gz'), may hold values from -6 to 6
- kernel: float32 [64, 128, 128], P('gy', 'gz'), may hold values from 0.2 to 1
Outputs:
- response: float32 [16, 64, 128, 128], P('bands', 'gy', 'gz')
- density: float32 [64, 128, 128], P('gy', 'gz', 'bands')
All inputs are finite; a program needn't handle non-finite values.
Results may differ from a plain program's by a relative error of at most 0.00002.
Values sent between devices are 32-bit elements; how exact they have to be, the bound alone decides.
No kernel may reach another device: no remote copies, remote signals or barrier semaphores. Data moves between devices by JAX's collectives and lax.ppermute only.
A program may use at most 64 MiB of HBM per device.

v0:
```python
import jax
import jax.numpy as jnp
from jax import lax
from jax.sharding import PartitionSpec as P

SWEEPS = 4
OUTER = 2


relax_factor = 0.8


def extended(cells, sides, width):
    for axis, dim in sides:
        count = lax.axis_size(axis)
        head = lax.slice_in_dim(cells, 0, width, axis=dim)
        tail = lax.slice_in_dim(cells, cells.shape[dim] - width, cells.shape[dim], axis=dim)
        cells = jnp.concatenate(
            [
                lax.ppermute(tail, axis, [(i, (i + 1) % count) for i in range(count)]),
                cells,
                lax.ppermute(head, axis, [((i + 1) % count, i) for i in range(count)]),
            ],
            axis=dim,
        )
    return cells


def copy_for_each(value, axis):
    peers = lax.axis_size(axis)
    return lax.all_to_all(
        jnp.broadcast_to(value[None], (peers, *value.shape)), axis, 0, 0, tiled=True
    )


def taken_together(value, axis):
    return copy_for_each(value, axis).sum(axis=0)


def in_blocks(value, dim, peers):
    before, after = (value.shape[:dim], value.shape[dim + 1 :])
    return jnp.moveaxis(value.reshape(*before, peers, -1, *after), dim, 0)


def sum_at_owner(value, axis, dim):
    peers = lax.axis_size(axis)
    blocks = lax.all_to_all(in_blocks(value, dim, peers), axis, 0, 0, tiled=True)
    return jnp.sum(blocks, axis=0)


def roll_sum(field):
    return jnp.roll(field, 1, -1) + jnp.roll(field, -1, -1)


def laplace_parts(padded):
    centre = padded[..., 1:-1, 1:-1, :]
    along_y = padded[..., 2:, 1:-1, :] + padded[..., :-2, 1:-1, :]
    along_z = padded[..., 1:-1, 2:, :] + padded[..., 1:-1, :-2, :]
    plane_corners = (
        padded[..., 2:, 2:, :]
        + padded[..., 2:, :-2, :]
        + padded[..., :-2, 2:, :]
        + padded[..., :-2, :-2, :]
    )
    face_sum = roll_sum(centre) + along_y + along_z
    edge_sum = roll_sum(along_y) + roll_sum(along_z) + plane_corners
    corner_sum = roll_sum(plane_corners)
    laplacian = (-128.0 * centre + 14.0 * face_sum + 3.0 * edge_sum + corner_sum) / 30.0
    return (centre, laplacian)


def mehrstellen(padded):
    centre = padded[..., 1:-1, 1:-1, :]
    along_y = padded[..., 2:, 1:-1, :] + padded[..., :-2, 1:-1, :]
    along_z = padded[..., 1:-1, 2:, :] + padded[..., 1:-1, :-2, :]
    return 0.5 * centre + (roll_sum(centre) + along_y + along_z) / 12.0


def relax(padded, weight, source):
    centre, laplacian = laplace_parts(padded)
    diagonal = 32.0 / 15.0 + weight
    applied = -0.5 * laplacian + weight * centre
    return centre + relax_factor * (source - applied) / diagonal


def shrink(field, margin):
    if margin == 0:
        return field
    return field[..., margin:-margin, margin:-margin, :]


def on_device(orbitals, orbital_shift, occupation, potential, perturbation, kernel):
    shifts = orbital_shift[:, None, None, None]
    response = jnp.zeros_like(orbitals)
    change = perturbation
    orbital_count = orbitals.shape[0]
    widened = extended(potential, (("gy", 0), ("gz", 1)), SWEEPS - 1)
    weight_wide = widened[None] + shifts
    for update in range(OUTER):
        product = change[None] * orbitals
        stacked = extended(jnp.concatenate([response, product], 0), (("gy", 1), ("gz", 2)), SWEEPS)
        current = stacked[:orbital_count]
        source = -mehrstellen(stacked[orbital_count:])
        for sweep_index in range(SWEEPS):
            current = relax(current, shrink(weight_wide, sweep_index), shrink(source, sweep_index))
        response = current
        partial_value = jnp.sum(occupation[:, None, None, None] * orbitals * response, 0)
        if update + 1 < OUTER:
            total = taken_together(partial_value, "bands")
            change = perturbation + kernel * total
        else:
            density = sum_at_owner(partial_value, "bands", 2)
    return (response, density)


def solution(mesh):
    placed = (
        P("bands", "gy", "gz", None),
        P("bands"),
        P("bands"),
        P("gy", "gz", None),
        P("gy", "gz", None),
        P("gy", "gz", None),
    )
    return jax.shard_map(
        on_device,
        mesh=mesh,
        in_specs=placed,
        out_specs=(P("bands", "gy", "gz", None), P("gy", "gz", "bands")),
        check_vma=False,
    )
```

profile of v0, /device:TPU:6, one launch (start us, length us, event | category | flops | bytes accessed | tf_op | source)
XLA Modules:
  0.0 120.6 jit_solution(13091732145735517693)
XLA Ops:
  0.6 0.8 fusion.193
  1.4 2.2 %collective-permute-start.4 = (f32[3,16,128]{2,1,0:T(8,128)S(1)}, f32[3,16,128]{2,1,0:T(8,128)S(1)}, u32[]{:S(2)}, u32[]{:S(2)}) collective-permute-start(f32[3,16,128]{2,1,0:T(8,128)S(1)} %get-tuple-element.181), channel_id=1, source_target_pairs={{0,8},{8,16},{16,24},{24,0},{1,9},{9,17},{17,25},{25,1},{2,10},{10... | collective-permute-start | bytes 73736 | tf_op jit(solution)/shard_map/ppermute | solution.py:20
  3.6 1.0 broadcast_multiply_fusion.1
  4.6 0.6 collective-permute-done.4
  5.2 0.9 constant_dynamic-update-slice_fusion.1
  6.1 2.5 %collective-permute-done.5 = f32[3,16,128]{2,1,0:T(8,128)S(1)} collective-permute-done((f32[3,16,128]{2,1,0:T(8,128)S(1)}, f32[3,16,128]{2,1,0:T(8,128)S(1)}, u32[]{:S(2)}, u32[]{:S(2)}) %collective-permute-start.5) | collective-permute-done | bytes 24608 | tf_op jit(solution)/shard_map/ppermute | solution.py:22
  8.8 4.1 %collective-permute-start.7 = (f32[22,3,128]{2,1,0:T(4,128)S(1)}, f32[22,3,128]{2,1,0:T(4,128)S(1)}, u32[]{:S(2)}, u32[]{:S(2)}) collective-permute-start(f32[22,3,128]{2,1,0:T(4,128)S(1)} %get-tuple-element.179), channel_id=1, source_target_pairs={{1,0},{2,1},{3,2},{4,3},{5,4},{6,5},{7,6},{0,7},{9,8},{10,9},{11,1... | collective-permute-start | bytes 101384 | tf_op jit(solution)/shard_map/ppermute | solution.py:22
  12.9 1.0 collective-permute-start
  13.9 1.1 collective-permute-start.1
  15.1 2.8 %collective-permute-done = f32[4,4,16,128]{3,2,1,0:T(8,128)S(1)} collective-permute-done((f32[4,4,16,128]{3,2,1,0:T(8,128)S(1)}, f32[4,4,16,128]{3,2,1,0:T(8,128)S(1)}, u32[]{:S(2)}, u32[]{:S(2)}) %collective-permute-start) | collective-permute-done | bytes 131104 | tf_op jit(solution)/shard_map/ppermute | solution.py:20
  17.9 2.2 %collective-permute-done.1 = f32[4,4,16,128]{3,2,1,0:T(8,128)S(1)} collective-permute-done((f32[4,4,16,128]{3,2,1,0:T(8,128)S(1)}, f32[4,4,16,128]{3,2,1,0:T(8,128)S(1)}, u32[]{:S(2)}, u32[]{:S(2)}) %collective-permute-start.1) | collective-permute-done | bytes 131104 | tf_op jit(solution)/shard_map/ppermute | solution.py:22
  20.3 4.1 %collective-permute-start.3 = (f32[4,24,4,128]{3,2,1,0:T(4,128)S(1)}, f32[4,24,4,128]{3,2,1,0:T(4,128)S(1)}, u32[]{:S(2)}, u32[]{:S(2)}) collective-permute-start(f32[4,24,4,128]{3,2,1,0:T(4,128)S(1)} %get-tuple-element.35), channel_id=1, source_target_pairs={{1,0},{2,1},{3,2},{4,3},{5,4},{6,5},{7,6},{0,7},{9,8},{10,9},{11,1... | collective-permute-start | bytes 589832 | tf_op jit(solution)/shard_map/ppermute | solution.py:22
  24.5 3.5 %collective-permute-done.2 = f32[4,24,4,128]{3,2,1,0:T(4,128)S(1)} collective-permute-done((f32[4,24,4,128]{3,2,1,0:T(4,128)S(1)}, f32[4,24,4,128]{3,2,1,0:T(4,128)S(1)}, u32[]{:S(2)}, u32[]{:S(2)}) %collective-permute-start.2) | collective-permute-done | bytes 196640 | tf_op jit(solution)/shard_map/ppermute | solution.py:20
  29.6 0.5 fusion.131
  30.2 2.0 %fusion.2 = (f32[2,22,22,128]{3,2,1,0:T(8,128)S(1)}, f32[2,22,22,128]{3,2,1,0:T(8,128)S(1)}) fusion(f32[2,22,22,128]{3,2,1,0:T(8,128)S(1)} %get-tuple-element.31, f32[2,22,22,128]{3,2,1,0:T(8,128)S(1)} %get-tuple-element.30, f32[2,22,22,127]{3,2,1,0:T(8,128)S(1)} %get-tuple-element.26, f32[2,22,22,1]{3,2,1,0:T(8,128)S(1)} %get-tuple-element.22, ...), kind=kLoop, calls=%fused_computation.7 | loop fusion | flops 5203968 | bytes 10655752 | tf_op jit(solution)/shard_map/add | solution.py:83
  33.9 1.5 %fusion.45 = f32[2,20,20,128]{3,2,1,0:T(8,128)S(1)} fusion(f32[2,22,22,128]{3,2,1,0:T(8,128)S(1)} %get-tuple-element.9, f32[2,20,20,128]{3,2,1,0:T(8,128)S(1)} %get-tuple-element.57, f32[2,20,20,128]{3,2,1,0:T(8,128)S(1)} %get-tuple-element.56, f32[2,20,20,127]{3,2,1,0:T(8,128)S(1)} %get-tuple-element.59, f32[2,20,20,1]{3,2,1,0:T(8,128)S(1)} %get-tuple-element.61, ...), kind=kLoop, calls=%fused_computation.88 | loop fusion | flops 3072000 | bytes 6144000 | tf_op jit(solution)/shard_map/add | solution.py:83
  37.1 1.4 %fusion.73 = f32[2,18,18,128]{3,2,1,0:T(8,128)S(1)} fusion(f32[2,22,22,128]{3,2,1,0:T(8,128)S(1)} %get-tuple-element.9, f32[2,18,18,128]{3,2,1,0:T(8,128)S(1)} %get-tuple-element.97, f32[2,18,18,128]{3,2,1,0:T(8,128)S(1)} %get-tuple-element.96, f32[2,18,18,127]{3,2,1,0:T(8,128)S(1)} %get-tuple-element.99, f32[2,18,18,1]{3,2,1,0:T(8,128)S(1)} %get-tuple-element.101, ...), kind=kLoop, calls=%fused_computation.136 | loop fusion | flops 2488320 | bytes 4976640 | tf_op jit(solution)/shard_map/add | solution.py:83
  39.8 0.7 copy-done
  40.5 0.7 multiply_reduce_fusion.1
  41.3 36.0 %all_to_all.10 = f32[8,16,16,128]{3,2,1,0:T(8,128)S(1)} all-to-all(f32[8,16,16,128]{3,2,1,0:T(8,128)S(1)} %broadcast_in_dim.2), channel_id=1, replica_groups=mesh['bands'=8,'gy'=4,'gz'=8] {'bands'}, dimensions={0} | all-to-all | bytes 2097152 | tf_op jit(solution)/shard_map/all_to_all | solution.py:31
  77.5 2.0 %collective-permute-start.9 = (f32[4,4,16,128]{3,2,1,0:T(8,128)S(1)}, f32[4,4,16,128]{3,2,1,0:T(8,128)S(1)}, u32[]{:S(2)}, u32[]{:S(2)}) collective-permute-start(f32[4,4,16,128]{3,2,1,0:T(8,128)S(1)} %get-tuple-element.75), channel_id=1, source_target_pairs={{8,0},{16,8},{24,16},{0,24},{9,1},{17,9},{25,17},{1,25},{10,2},{18... | collective-permute-start | bytes 393224 | tf_op jit(solution)/shard_map/ppermute | solution.py:22
  79.6 2.9 %collective-permute-done.8 = f32[4,4,16,128]{3,2,1,0:T(8,128)S(1)} collective-permute-done((f32[4,4,16,128]{3,2,1,0:T(8,128)S(1)}, f32[4,4,16,128]{3,2,1,0:T(8,128)S(1)}, u32[]{:S(2)}, u32[]{:S(2)}) %collective-permute-start.8) | collective-permute-done | bytes 131104 | tf_op jit(solution)/shard_map/ppermute | solution.py:20
  82.5 1.3 %collective-permute-done.9 = f32[4,4,16,128]{3,2,1,0:T(8,128)S(1)} collective-permute-done((f32[4,4,16,128]{3,2,1,0:T(8,128)S(1)}, f32[4,4,16,128]{3,2,1,0:T(8,128)S(1)}, u32[]{:S(2)}, u32[]{:S(2)}) %collective-permute-start.9) | collective-permute-done | bytes 131104 | tf_op jit(solution)/shard_map/ppermute | solution.py:22
  84.0 4.4 %collective-permute-start.11 = (f32[4,24,4,128]{3,2,1,0:T(4,128)S(1)}, f32[4,24,4,128]{3,2,1,0:T(4,128)S(1)}, u32[]{:S(2)}, u32[]{:S(2)}) collective-permute-start(f32[4,24,4,128]{3,2,1,0:T(4,128)S(1)} %get-tuple-element.33), channel_id=1, source_target_pairs={{1,0},{2,1},{3,2},{4,3},{5,4},{6,5},{7,6},{0,7},{9,8},{10,9},{11,1... | collective-permute-start | bytes 589832 | tf_op jit(solution)/shard_map/ppermute | solution.py:22
  88.4 3.4 %collective-permute-done.10 = f32[4,24,4,128]{3,2,1,0:T(4,128)S(1)} collective-permute-done((f32[4,24,4,128]{3,2,1,0:T(4,128)S(1)}, f32[4,24,4,128]{3,2,1,0:T(4,128)S(1)}, u32[]{:S(2)}, u32[]{:S(2)}) %collective-permute-start.10) | collective-permute-done | bytes 196640 | tf_op jit(solution)/shard_map/ppermute | solution.py:20
  94.1 2.0 %fusion.3 = (f32[2,22,22,128]{3,2,1,0:T(8,128)S(1)}, f32[2,22,22,128]{3,2,1,0:T(8,128)S(1)}) fusion(f32[2,22,22,128]{3,2,1,0:T(8,128)S(1)} %get-tuple-element.20, f32[2,22,22,128]{3,2,1,0:T(8,128)S(1)} %get-tuple-element.19, f32[2,22,22,127]{3,2,1,0:T(8,128)S(1)} %get-tuple-element.15, f32[2,22,22,1]{3,2,1,0:T(8,128)S(1)} %get-tuple-element.11, ...), kind=kLoop, calls=%fused_computation.8 | loop fusion | flops 5203968 | bytes 10655752 | tf_op jit(solution)/shard_map/add | solution.py:83
  97.9 1.5 %fusion.42 = f32[2,20,20,128]{3,2,1,0:T(8,128)S(1)} fusion(f32[2,22,22,128]{3,2,1,0:T(8,128)S(1)} %get-tuple-element.5, f32[2,20,20,128]{3,2,1,0:T(8,128)S(1)} %get-tuple-element.38, f32[2,20,20,128]{3,2,1,0:T(8,128)S(1)} %get-tuple-element.37, f32[2,20,20,127]{3,2,1,0:T(8,128)S(1)} %get-tuple-element.40, f32[2,20,20,1]{3,2,1,0:T(8,128)S(1)} %get-tuple-element.42, ...), kind=kLoop, calls=%fused_computation.79 | loop fusion | flops 3072000 | bytes 6144000 | tf_op jit(solution)/shard_map/add | solution.py:83
  101.1 1.4 %fusion.70 = f32[2,18,18,128]{3,2,1,0:T(8,128)S(1)} fusion(f32[2,22,22,128]{3,2,1,0:T(8,128)S(1)} %get-tuple-element.5, f32[2,18,18,128]{3,2,1,0:T(8,128)S(1)} %get-tuple-element.78, f32[2,18,18,128]{3,2,1,0:T(8,128)S(1)} %get-tuple-element.77, f32[2,18,18,127]{3,2,1,0:T(8,128)S(1)} %get-tuple-element.80, f32[2,18,18,1]{3,2,1,0:T(8,128)S(1)} %get-tuple-element.82, ...), kind=kLoop, calls=%fused_computation.127 | loop fusion | flops 2488320 | bytes 4976640 | tf_op jit(solution)/shard_map/add | solution.py:83
  103.7 1.4 %multiply_reduce_fusion = (f32[16,16,128]{2,1,0:T(8,128)S(1)}, f32[2,16,16,128]{3,2,1,0:T(8,128)}) fusion(f32[2,16,16,128]{3,2,1,0:T(8,128)S(1)} %copy-done, f32[2]{0:T(128)S(1)} %copy-done.4, f32[2,22,22,128]{3,2,1,0:T(8,128)S(1)} %broadcast_add_fusion, f32[2,16,16,1]{3,2,1,0:T(8,128)S(1)} %get-tuple-element.161, ...), kind=kLoop, calls=%fused_computation.217 | loop fusion | flops 2129920 | bytes 4325384 | tf_op jit(solution)/shard_map/reduce_sum | solution.py:107
  106.0 12.0 %all_to_all.11 = f32[8,1,4096]{2,1,0:T(1,128)S(1)} all-to-all(f32[8,1,4096]{2,1,0:T(1,128)S(1)} %reshape.14), channel_id=1, replica_groups=mesh['bands'=8,'gy'=4,'gz'=8] {'bands'}, dimensions={0} | all-to-all | bytes 262144 | tf_op jit(solution)/shard_map/all_to_all | solution.py:47
  118.5 1.0 reduce
  119.9 0.7 reduce_sum.39
  (106 shorter events, 15.7 us)
Async XLA Ops:
  1.4 3.8 %collective-permute-start.4 = (f32[3,16,128]{2,1,0:T(8,128)S(1)}, f32[3,16,128]{2,1,0:T(8,128)S(1)}, u32[]{:S(2)}, u32[]{:S(2)}) collective-permute-start(f32[3,16,128]{2,1,0:T(8,128)S(1)} %get-tuple-element.181), channel_id=1, source_target_pairs={{0,8},{8,16},{16,24},{24,0},{1,9},{9,17},{17,25},{25,1},{2,10},{10... | collective-permute-start | bytes 73736 | tf_op jit(solution)/shard_map/ppermute | solution.py:20
  3.6 5.0 %collective-permute-start.5 = (f32[3,16,128]{2,1,0:T(8,128)S(1)}, f32[3,16,128]{2,1,0:T(8,128)S(1)}, u32[]{:S(2)}, u32[]{:S(2)}) collective-permute-start(f32[3,16,128]{2,1,0:T(8,128)S(1)} %get-tuple-element.180), channel_id=1, source_target_pairs={{8,0},{16,8},{24,16},{0,24},{9,1},{17,9},{25,17},{1,25},{10,2},{18... | collective-permute-start | bytes 73736 | tf_op jit(solution)/shard_map/ppermute | solution.py:22
  8.7 6.4 %collective-permute-start.6 = (f32[22,3,128]{2,1,0:T(4,128)S(1)}, f32[22,3,128]{2,1,0:T(4,128)S(1)}, u32[]{:S(2)}, u32[]{:S(2)}) collective-permute-start(f32[22,3,128]{2,1,0:T(4,128)S(1)} %get-tuple-element.178), channel_id=1, source_target_pairs={{0,1},{1,2},{2,3},{3,4},{4,5},{5,6},{6,7},{7,0},{8,9},{9,10},{10,1... | collective-permute-start | bytes 101384 | tf_op jit(solution)/shard_map/ppermute | solution.py:20
  8.8 6.3 %collective-permute-start.7 = (f32[22,3,128]{2,1,0:T(4,128)S(1)}, f32[22,3,128]{2,1,0:T(4,128)S(1)}, u32[]{:S(2)}, u32[]{:S(2)}) collective-permute-start(f32[22,3,128]{2,1,0:T(4,128)S(1)} %get-tuple-element.179), channel_id=1, source_target_pairs={{1,0},{2,1},{3,2},{4,3},{5,4},{6,5},{7,6},{0,7},{9,8},{10,9},{11,1... | collective-permute-start | bytes 101384 | tf_op jit(solution)/shard_map/ppermute | solution.py:22
  12.9 5.0 %collective-permute-start = (f32[4,4,16,128]{3,2,1,0:T(8,128)S(1)}, f32[4,4,16,128]{3,2,1,0:T(8,128)S(1)}, u32[]{:S(2)}, u32[]{:S(2)}) collective-permute-start(f32[4,4,16,128]{3,2,1,0:T(8,128)S(1)} %get-tuple-element.176), channel_id=1, source_target_pairs={{0,8},{8,16},{16,24},{24,0},{1,9},{9,17},{17,25},{25,1},{2,10},{10... | collective-permute-start | bytes 393224 | tf_op jit(solution)/shard_map/ppermute | solution.py:20
  13.9 10.5 %copy-start.3 = (f32[2]{0:T(128)S(1)}, f32[2]{0:T(128)}, u32[]{:S(2)}) copy-start(f32[2]{0:T(128)} %param.7) | copy-start | bytes 28
  13.9 6.2 %collective-permute-start.1 = (f32[4,4,16,128]{3,2,1,0:T(8,128)S(1)}, f32[4,4,16,128]{3,2,1,0:T(8,128)S(1)}, u32[]{:S(2)}, u32[]{:S(2)}) collective-permute-start(f32[4,4,16,128]{3,2,1,0:T(8,128)S(1)} %get-tuple-element.177), channel_id=1, source_target_pairs={{8,0},{16,8},{24,16},{0,24},{9,1},{17,9},{25,17},{1,25},{10,2},{18... | collective-permute-start | bytes 393224 | tf_op jit(solution)/shard_map/ppermute | solution.py:22
  20.2 7.9 %collective-permute-start.2 = (f32[4,24,4,128]{3,2,1,0:T(4,128)S(1)}, f32[4,24,4,128]{3,2,1,0:T(4,128)S(1)}, u32[]{:S(2)}, u32[]{:S(2)}) collective-permute-start(f32[4,24,4,128]{3,2,1,0:T(4,128)S(1)} %get-tuple-element.34), channel_id=1, source_target_pairs={{0,1},{1,2},{2,3},{3,4},{4,5},{5,6},{6,7},{7,0},{8,9},{9,10},{10,1... | collective-permute-start | bytes 589832 | tf_op jit(solution)/shard_map/ppermute | solution.py:20
  20.3 7.8 %collective-permute-start.3 = (f32[4,24,4,128]{3,2,1,0:T(4,128)S(1)}, f32[4,24,4,128]{3,2,1,0:T(4,128)S(1)}, u32[]{:S(2)}, u32[]{:S(2)}) collective-permute-start(f32[4,24,4,128]{3,2,1,0:T(4,128)S(1)} %get-tuple-element.35), channel_id=1, source_target_pairs={{1,0},{2,1},{3,2},{4,3},{5,4},{6,5},{7,6},{0,7},{9,8},{10,9},{11,1... | collective-permute-start | bytes 589832 | tf_op jit(solution)/shard_map/ppermute | solution.py:22
  39.5 1.0 copy-start
  39.5 0.9 copy-start.4
  41.3 36.1 %copy-start.1 = (f32[16,16,128]{2,1,0:T(8,128)S(1)}, f32[16,16,128]{2,1,0:T(8,128)}, u32[]{:S(2)}) copy-start(f32[16,16,128]{2,1,0:T(8,128)} %param.10) | copy-start | bytes 393220
  41.3 36.1 %copy-start.2 = (f32[16,16,128]{2,1,0:T(8,128)S(1)}, f32[16,16,128]{2,1,0:T(8,128)}, u32[]{:S(2)}) copy-start(f32[16,16,128]{2,1,0:T(8,128)} %param.11) | copy-start | bytes 393220
  77.5 5.0 %collective-permute-start.8 = (f32[4,4,16,128]{3,2,1,0:T(8,128)S(1)}, f32[4,4,16,128]{3,2,1,0:T(8,128)S(1)}, u32[]{:S(2)}, u32[]{:S(2)}) collective-permute-start(f32[4,4,16,128]{3,2,1,0:T(8,128)S(1)} %get-tuple-element.74), channel_id=1, source_target_pairs={{0,8},{8,16},{16,24},{24,0},{1,9},{9,17},{17,25},{25,1},{2,10},{10... | collective-permute-start | bytes 393224 | tf_op jit(solution)/shard_map/ppermute | solution.py:20
  77.5 6.3 %collective-permute-start.9 = (f32[4,4,16,128]{3,2,1,0:T(8,128)S(1)}, f32[4,4,16,128]{3,2,1,0:T(8,128)S(1)}, u32[]{:S(2)}, u32[]{:S(2)}) collective-permute-start(f32[4,4,16,128]{3,2,1,0:T(8,128)S(1)} %get-tuple-element.75), channel_id=1, source_target_pairs={{8,0},{16,8},{24,16},{0,24},{9,1},{17,9},{25,17},{1,25},{10,2},{18... | collective-permute-start | bytes 393224 | tf_op jit(solution)/shard_map/ppermute | solution.py:22
  83.9 7.9 %collective-permute-start.10 = (f32[4,24,4,128]{3,2,1,0:T(4,128)S(1)}, f32[4,24,4,128]{3,2,1,0:T(4,128)S(1)}, u32[]{:S(2)}, u32[]{:S(2)}) collective-permute-start(f32[4,24,4,128]{3,2,1,0:T(4,128)S(1)} %get-tuple-element.32), channel_id=1, source_target_pairs={{0,1},{1,2},{2,3},{3,4},{4,5},{5,6},{6,7},{7,0},{8,9},{9,10},{10,1... | collective-permute-start | bytes 589832 | tf_op jit(solution)/shard_map/ppermute | solution.py:20
  84.0 7.8 %collective-permute-start.11 = (f32[4,24,4,128]{3,2,1,0:T(4,128)S(1)}, f32[4,24,4,128]{3,2,1,0:T(4,128)S(1)}, u32[]{:S(2)}, u32[]{:S(2)}) collective-permute-start(f32[4,24,4,128]{3,2,1,0:T(4,128)S(1)} %get-tuple-element.33), channel_id=1, source_target_pairs={{1,0},{2,1},{3,2},{4,3},{5,4},{6,5},{7,6},{0,7},{9,8},{10,9},{11,1... | collective-permute-start | bytes 589832 | tf_op jit(solution)/shard_map/ppermute | solution.py:22
where the time goes:
time: 122 us; the launch traced here: 121 us
  blocking collectives  47.9 us (39%)
  starting transfers between devices  19.3 us (16%)
  waiting for transfers between devices  19.3 us (16%)
  other arithmetic  16.5 us (14%)
  local copies, waits for them, and re-layouts  16.4 us (13%)
    all_to_all x1, blocking collectives, copy_for_each(): lax.all_to_all(jnp.broadcast_to(value[None], (peers, *value.shape)), axis...  36 us
    ppermute x6, starting transfers between devices, extended(): lax.ppermute(head, axis, [((i + 1) % count, i) for i in range(count)])  15.7 us
    ppermute x6, waiting for transfers between devices, extended(): lax.ppermute(tail, axis, [(i, (i + 1) % count) for i in range(count)])  13.3 us
    slice x60, local copies, waits for them, and re-layouts, roll_sum(): return jnp.roll(field, 1, -1) + jnp.roll(field, -1, -1)  12.2 us
    all_to_all x1, blocking collectives, sum_at_owner(): lax.all_to_all(in_blocks(value, dim, peers), axis, 0, 0, tiled=True)  12 us
    add x6, other arithmetic, relax(): return centre + relax_factor * (source - applied) / diagonal  9.91 us
    ppermute x6, waiting for transfers between devices, extended(): lax.ppermute(head, axis, [((i + 1) % count, i) for i in range(count)])  5.97 us
    ppermute x6, starting transfers between devices, extended(): lax.ppermute(tail, axis, [(i, (i + 1) % count) for i in range(count)])  3.57 us
  transfers between devices with their start and end apart: 12, of which 8 were waited for; matrix products, arithmetic and copies ran while one was open for 2% of the time, Pallas kernels for 0%

commit v1 on v0

v1 whole, which is shorter than its diff:
```python
import jax
import jax.numpy as jnp
from jax import lax
from jax.experimental import pallas as pl
from jax.experimental.pallas import tpu as pltpu
from jax.sharding import PartitionSpec as P

RELAX = 0.8
HALO = 4
VMEM = pl.BlockSpec(memory_space=pltpu.VMEM)
SMEM = pl.BlockSpec(memory_space=pltpu.SMEM)


def call(body, outs, *args, scratch=(), smem=0):
    return pl.pallas_call(
        body,
        out_shape=outs,
        in_specs=[VMEM] * (len(args) - smem) + [SMEM] * smem,
        out_specs=jax.tree.map(lambda _: VMEM, outs),
        scratch_shapes=list(scratch),
        compiler_params=pltpu.CompilerParams(vmem_limit_bytes=48 * 2**20),
    )(*args)


def f32(*shape):
    return jax.ShapeDtypeStruct(shape, jnp.float32)


def low_half():
    return lax.broadcasted_iota(jnp.int32, (8, 128), 0) < 4


def pack_z(row, head_ref, tail_ref, field):
    low = low_half()
    for j in range(12):
        a, b = row(j), row(j + 12)
        head_ref[field, j] = jnp.where(low, a[:8], pltpu.roll(b[:8], 4, 0))
        tail_ref[field, j] = jnp.where(low, pltpu.roll(b[8:], 4, 0), a[8:])


def padded_row(centre_ref, lo_ref, hi_ref, field):
    def row(r):
        if r < 4:
            return lo_ref[field, r]
        if r < 20:
            return centre_ref[field, r - 4]
        return hi_ref[field, r - 20]

    return row


def pack_kernel(centre_ref, lo_ref, hi_ref, head_ref, tail_ref):
    for field in range(centre_ref.shape[0]):
        pack_z(padded_row(centre_ref, lo_ref, hi_ref, field), head_ref, tail_ref, field)


def assemble(row, above_ref, below_ref, field, dest_ref, at):
    low = low_half()
    for r in range(24):
        dest_ref[at, r, 0:16] = row(r)
    for j in range(12):
        above, below = above_ref[field, j], below_ref[field, j]
        dest_ref[at, j, 16:24] = jnp.where(low, above, below)
        dest_ref[at, j + 12, 16:24] = pltpu.roll(jnp.where(low, below, above), 4, 0)


def shifts_z(u):
    return pltpu.roll(u, 1, u.ndim - 2) + pltpu.roll(u, 23, u.ndim - 2)


def shifts_x(u):
    return pltpu.roll(u, 1, u.ndim - 1) + pltpu.roll(u, 127, u.ndim - 1)


def by_rows(first, last, load, emit, step=2):
    def body(i, carry):
        before, at = carry
        r = first + step * i
        for k in range(step):
            after = load(r + k + 1)
            emit(r + k, before, at, after)
            before, at = at, after
        return before, at

    lax.fori_loop(0, (last - first) // step, body, (load(first - 1), load(first)))


def sources(p_ref, scale_ref, sc_ref, o):
    def load(r):
        return p_ref[o, r]

    def emit(r, before, at, after):
        faces = shifts_x(at) + shifts_z(at) + (before + after)
        sc_ref[o, r] = scale_ref[o, r] * (-30.0 * at - 5.0 * faces)

    by_rows(1, 23, load, emit)


def sweep(src_ref, scale_ref, sc_ref, o, margin, store):
    def load(r):
        u = src_ref[o, r]
        return u, shifts_z(u)

    def emit(r, before, at, after):
        u, along_z = at
        across = before[1] + after[1]
        m = before[0] + after[0] + along_z
        n = 3.0 * m + across
        total = shifts_x(14.0 * u + n) + (3.0 * n + 5.0 * m)
        store(r, 0.2 * u + sc_ref[o, r] + scale_ref[o, r] * total)

    by_rows(margin, 24 - margin, load, emit)


def into(dest_ref, o):
    def store(r, new):
        dest_ref[o, r] = new

    return store


def last_sweep(src_ref, scale_ref, sc_ref, o, orb_ref, occ_ref, resp_ref, dens_ref):
    occupation = occ_ref[o]

    def store(r, new):
        own = new[:16]
        resp_ref[o, r - 4] = own
        term = occupation * orb_ref[o, r - 4] * own
        dens_ref[r - 4] = term if o == 0 else dens_ref[r - 4] + term

    sweep(src_ref, scale_ref, sc_ref, o, 4, store)


def first_kernel(
    centre_ref, lo_ref, hi_ref, above_ref, below_ref, orb_ref, shift_ref, occ_ref,
    resp_ref, dens_ref, scale_ref, p_ref, sc_ref, a_ref, b_ref,
):
    for field in range(2):
        assemble(padded_row(centre_ref, lo_ref, hi_ref, field), above_ref, below_ref, field, p_ref, field)
    assemble(padded_row(centre_ref, lo_ref, hi_ref, 2), above_ref, below_ref, 2, a_ref, 0)
    for o in range(2):
        base = 32.0 / 15.0 + shift_ref[o]

        def scales(r, _):
            scale_ref[o, r] = (RELAX / 60.0) / (base + a_ref[0, r])
            return 0

        lax.fori_loop(1, 23, scales, 0)
    for o in range(2):
        sources(p_ref, scale_ref, sc_ref, o)
    for o in range(2):
        sweep(sc_ref, scale_ref, sc_ref, o, 2, into(a_ref, o))
        sweep(a_ref, scale_ref, sc_ref, o, 3, into(b_ref, o))
        last_sweep(b_ref, scale_ref, sc_ref, o, orb_ref, occ_ref, resp_ref, dens_ref)


def change_kernel(own_ref, other_ref, pert_ref, kern_ref, orb_ref, resp_ref, core_ref, centre_ref, up_ref, down_ref):
    first_core = core_ref[0] == 0
    for y in range(16):
        mine, theirs = own_ref[y % 8], other_ref[y % 8]
        total = jnp.where(first_core, mine, theirs) if y < 8 else jnp.where(first_core, theirs, mine)
        change = pert_ref[y] + kern_ref[y] * total
        for o in range(2):
            product, response = change * orb_ref[o, y], resp_ref[o, y]
            centre_ref[o, y] = product
            centre_ref[2 + o, y] = response
            if y < 4:
                down_ref[o, y] = product
                down_ref[2 + o, y] = response
            if y >= 12:
                up_ref[o, y - 12] = product
                up_ref[2 + o, y - 12] = response


def swap_blocks(rows):
    block = lax.broadcasted_iota(jnp.int32, rows[0].shape, rows[0].ndim - 1) // 16
    for d in (1, 2, 4):
        keep = (block // d) % 2 == 0
        out = list(rows)
        for k in range(8):
            if k & d == 0:
                a, b = rows[k], rows[k + d]
                out[k] = jnp.where(keep, a, pltpu.roll(b, 16 * d, 1))
                out[k + d] = jnp.where(keep, pltpu.roll(a, 128 - 16 * d, 1), b)
        rows = out
    return rows


def second_kernel(
    centre_ref, lo_ref, hi_ref, above_ref, below_ref, scale_ref, orb_ref, occ_ref,
    resp_ref, out_ref, p_ref, u_ref, sc_ref, a_ref, b_ref, dens_ref,
):
    for o in range(2):
        assemble(padded_row(centre_ref, lo_ref, hi_ref, o), above_ref, below_ref, o, p_ref, o)
        assemble(padded_row(centre_ref, lo_ref, hi_ref, 2 + o), above_ref, below_ref, 2 + o, u_ref, o)
    for o in range(2):
        sources(p_ref, scale_ref, sc_ref, o)
        sweep(u_ref, scale_ref, sc_ref, o, 1, into(a_ref, o))
        sweep(a_ref, scale_ref, sc_ref, o, 2, into(b_ref, o))
        sweep(b_ref, scale_ref, sc_ref, o, 3, into(a_ref, o))
        last_sweep(a_ref, scale_ref, sc_ref, o, orb_ref, occ_ref, resp_ref, dens_ref)
    for part in range(4):
        y, z = part // 2, 8 * (part % 2)
        blocks = swap_blocks([dens_ref[2 * k + y, z : z + 8] for k in range(8)])
        for b in range(8):
            out_ref[b, part] = blocks[b]


def final_kernel(own_ref, one_ref, two_ref, three_ref, dens_ref):
    for part in range(4):
        y, z = part // 2, 8 * (part % 2)
        total = (own_ref[part] + one_ref[part]) + (two_ref[part] + three_ref[part])
        for k in range(8):
            moved = total if k == 0 else pltpu.roll(total, 128 - 16 * k, 1)
            dens_ref[2 * k + y, z : z + 8, :] = moved[:, :16]


def ring(axis, step):
    count = lax.axis_size(axis)
    return [(i, (i + step) % count) for i in range(count)]


def exchange_y(up, down):
    return lax.ppermute(up, "gy", ring("gy", 1)), lax.ppermute(down, "gy", ring("gy", -1))


def exchange_z(centre, lo, hi):
    fields = centre.shape[0]
    strip = f32(fields, 12, 8, 128)
    head, tail = call(pack_kernel, (strip, strip), centre, lo, hi)
    above = lax.ppermute(head, "gz", ring("gz", -1))
    below = lax.ppermute(tail, "gz", ring("gz", 1))
    return above, below


def partner(value, step):
    count = lax.axis_size("bands")
    return lax.ppermute(value, "bands", [(i, i ^ step) for i in range(count)])


def on_device(orbitals, orbital_shift, occupation, potential, perturbation, kernel):
    group = lax.axis_index("bands")
    core, far = group % 2, group // 2
    padded = f32(2, 24, 24, 128)
    wide = pltpu.VMEM((2, 24, 24, 128), jnp.float32)

    def fields(rows):
        return jnp.concatenate([perturbation[None, rows] * orbitals[:, rows], potential[None, rows]], 0)

    lo, hi = exchange_y(fields(slice(12, 16)), fields(slice(0, 4)))
    centre = fields(slice(0, 16))
    above, below = exchange_z(centre, lo, hi)
    response, partial, scale = call(
        first_kernel, (f32(2, 16, 16, 128), f32(16, 16, 128), padded),
        centre, lo, hi, above, below, orbitals, orbital_shift, occupation,
        scratch=[wide] * 4, smem=2,
    )

    own = lax.dynamic_slice_in_dim(partial, 8 * core, 8, 0)
    own = own + partner(lax.dynamic_slice_in_dim(partial, 8 * (1 - core), 8, 0), 1)
    own = own + partner(own, 2)
    own = own + partner(own, 6)
    other = partner(own, 1)
    centre, up, down = call(
        change_kernel, (f32(4, 16, 16, 128), f32(4, 4, 16, 128), f32(4, 4, 16, 128)),
        own, other, perturbation, kernel, orbitals, response, core[None].astype(jnp.int32), smem=1,
    )
    lo, hi = exchange_y(up, down)
    above, below = exchange_z(centre, lo, hi)
    response, blocks = call(
        second_kernel, (f32(2, 16, 16, 128), f32(8, 4, 8, 128)),
        centre, lo, hi, above, below, scale, orbitals, occupation,
        scratch=[wide] * 5 + [pltpu.VMEM((16, 16, 128), jnp.float32)], smem=1,
    )

    blocks = blocks.reshape(4, 2, 4, 8, 128)
    kept = lax.dynamic_index_in_dim(blocks, core, 1, keepdims=False)
    kept = kept + partner(lax.dynamic_index_in_dim(blocks, 1 - core, 1, keepdims=False), 1)

    def block_of(step):
        return lax.dynamic_index_in_dim(kept, far ^ step, 0, keepdims=False)

    two, one, three = (partner(block_of(step), 2 * step) for step in (2, 1, 3))
    density = call(final_kernel, f32(16, 16, 16), block_of(0), one, two, three)
    return response, density


def solution(mesh):
    placed = (
        P("bands", "gy", "gz", None),
        P("bands"),
        P("bands"),
        P("gy", "gz", None),
        P("gy", "gz", None),
        P("gy", "gz", None),
    )
    return jax.shard_map(
        on_device,
        mesh=mesh,
        in_specs=placed,
        out_specs=(P("bands", "gy", "gz", None), P("gy", "gz", "bands")),
        check_vma=False,
    )
```

time: 122 us -> 84.5 us (0.69)
  blocking collectives: 47.9 us -> 0 us
  waiting for transfers between devices: 19.3 us -> 38.7 us
  Pallas kernels: 0 us -> 18.8 us
  other arithmetic: 16.5 us -> 0.12 us
  local copies, waits for them, and re-layouts: 16.4 us -> 2.43 us
  starting transfers between devices: 19.3 us -> 23.4 us
    all_to_all x2 -> x0, blocking collectives: 47.9 us -> none  [the longest x1 36 us: copy_for_each(): lax.all_to_all(jnp.broadcast_to(value[None], (peers, *value.shape)), axis...]
    ppermute x12 -> x16, waiting for transfers between devices: 19.3 us -> 38.7 us  [the longest x8 14.6 us: partner(): return lax.ppermute(value, 'bands', [(i, i ^ step) for i in range(count)])]
    pallas_call x0 -> x6, Pallas kernels: none -> 18.8 us  [call(): pl.pallas_call(body, out_shape=outs, in_specs=[VMEM] * (len(args) - smem)...]
    slice x63 -> x1, local copies, waits for them, and re-layouts: 13 us -> 0.78 us  [fields(): perturbation[None, rows] * orbitals[:, rows]]
    add x16 -> x4, other arithmetic: 11 us -> 0.04 us  [the longest x1 0.01 us: on_device(): kept + partner(lax.dynamic_index_in_dim(blocks, 1 - core, 1, keepdims=Fal...]
    ppermute x12 -> x16, starting transfers between devices: 19.3 us -> 23.4 us  [the longest x8 14.1 us: partner(): return lax.ppermute(value, 'bands', [(i, i ^ step) for i in range(count)])]
    reduce_sum x4 -> x0, other arithmetic: 2.93 us -> none  [the longest x2 2.13 us: on_device(): jnp.sum(occupation[:, None, None, None] * orbitals * response, 0)]
    unnamed x14 -> x12, local copies, waits for them, and re-layouts: 2.34 us -> 0.79 us
  transfers between devices with their start and end apart: 12 -> 16, of which waited for: 8 -> 14; matrix products, arithmetic and copies ran while one was open for 2% -> 0% of each run, Pallas kernels for 0% -> 0%
where the time goes in v1:
time: 84.5 us; the launch traced here: 84.3 us
  waiting for transfers between devices  38.7 us (46%)
  starting transfers between devices  23.4 us (28%)
  Pallas kernels  18.8 us (22%)
  local copies, waits for them, and re-layouts  2.43 us (3%)
    pallas_call x6, Pallas kernels, call(): pl.pallas_call(body, out_shape=outs, in_specs=[VMEM] * (len(args) - smem)...  18.8 us
    ppermute x8, waiting for transfers between devices, partner(): return lax.ppermute(value, 'bands', [(i, i ^ step) for i in range(count)])  14.6 us
    ppermute x8, starting transfers between devices, partner(): return lax.ppermute(value, 'bands', [(i, i ^ step) for i in range(count)])  14.1 us
    ppermute x2, waiting for transfers between devices, exchange_z(): below = lax.ppermute(tail, 'gz', ring('gz', 1))  7.77 us
    ppermute x2, waiting for transfers between devices, exchange_z(): above = lax.ppermute(head, 'gz', ring('gz', -1))  6.56 us
    ppermute x2, waiting for transfers between devices, exchange_y(): lax.ppermute(up, 'gy', ring('gy', 1))  4.99 us
    ppermute x2, waiting for transfers between devices, exchange_y(): lax.ppermute(down, 'gy', ring('gy', -1))  4.82 us
    ppermute x2, starting transfers between devices, exchange_z(): above = lax.ppermute(head, 'gz', ring('gz', -1))  4.11 us
  transfers between devices with their start and end apart: 16, of which 14 were waited for; matrix products, arithmetic and copies ran while one was open for 0% of the time, Pallas kernels for 0%

profile of v1, /device:TPU:6, one launch (start us, length us, event | category | flops | bytes accessed | tf_op | source)
XLA Modules:
  0.0 84.3 jit_solution(12705189600764008109)
XLA Ops:
  0.6 0.8 slice_bitcast_fusion
  1.5 0.8 fusion
  2.3 2.3 %collective-permute-start = (f32[3,4,16,128]{3,2,1,0:T(8,128)S(1)}, f32[3,4,16,128]{3,2,1,0:T(8,128)S(1)}, u32[]{:S(2)}, u32[]{:S(2)}) collective-permute-start(f32[3,4,16,128]{3,2,1,0:T(8,128)S(1)} %pad_maximum_fusion.1), channel_id=1, source_target_pairs={{0,8},{8,16},{16,24},{24,0},{1,9},{9,17},{17,25},{25,1},{2,10},{10... | collective-permute-start | bytes 294920 | tf_op jit(solution)/shard_map/ppermute | solution.py:224
  4.7 0.8 copy-done.5
  5.5 1.5 %collective-permute-done.lo_ref = f32[3,4,16,128]{3,2,1,0:T(8,128)S(1)} collective-permute-done((f32[3,4,16,128]{3,2,1,0:T(8,128)S(1)}, f32[3,4,16,128]{3,2,1,0:T(8,128)S(1)}, u32[]{:S(2)}, u32[]{:S(2)}) %collective-permute-start) | collective-permute-done | bytes 98336 | tf_op jit(solution)/shard_map/ppermute | solution.py:224
  7.0 3.5 %collective-permute-done.1.hi_ref = f32[3,4,16,128]{3,2,1,0:T(8,128)S(1)} collective-permute-done((f32[3,4,16,128]{3,2,1,0:T(8,128)S(1)}, f32[3,4,16,128]{3,2,1,0:T(8,128)S(1)}, u32[]{:S(2)}, u32[]{:S(2)}) %collective-permute-start.1) | collective-permute-done | bytes 98336 | tf_op jit(solution)/shard_map/ppermute | solution.py:224
  10.5 2.7 %collective-permute-start.2 = (f32[3,12,8,128]{3,2,1,0:T(8,128)S(1)}, f32[3,12,8,128]{3,2,1,0:T(8,128)S(1)}, u32[]{:S(2)}, u32[]{:S(2)}) collective-permute-start(f32[3,12,8,128]{3,2,1,0:T(8,128)S(1)} %get-tuple-element.14), channel_id=1, source_target_pairs={{0,7},{1,0},{2,1},{3,2},{4,3},{5,4},{6,5},{7,6},{8,15},{9,8},{10,9... | collective-permute-start | bytes 442376 | tf_op jit(solution)/shard_map/ppermute | solution.py:231
  13.3 2.7 %collective-permute-done.2.above_ref = f32[3,12,8,128]{3,2,1,0:T(8,128)S(1)} collective-permute-done((f32[3,12,8,128]{3,2,1,0:T(8,128)S(1)}, f32[3,12,8,128]{3,2,1,0:T(8,128)S(1)}, u32[]{:S(2)}, u32[]{:S(2)}) %collective-permute-start.2) | collective-permute-done | bytes 147488 | tf_op jit(solution)/shard_map/ppermute | solution.py:231
  15.9 4.6 %collective-permute-done.3.below_ref = f32[3,12,8,128]{3,2,1,0:T(8,128)S(1)} collective-permute-done((f32[3,12,8,128]{3,2,1,0:T(8,128)S(1)}, f32[3,12,8,128]{3,2,1,0:T(8,128)S(1)}, u32[]{:S(2)}, u32[]{:S(2)}) %collective-permute-start.3) | collective-permute-done | bytes 147488 | tf_op jit(solution)/shard_map/ppermute | solution.py:232
  20.5 7.8 %shard_map.78 = (f32[2,16,16,128]{3,2,1,0:T(8,128)S(1)}, f32[16,16,128]{2,1,0:T(8,128)S(1)}, f32[2,24,24,128]{3,2,1,0:T(8,128)S(1)}) custom-call(f32[3,16,16,128]{3,2,1,0:T(8,128)S(1)} %pad_maximum_fusion.centre_ref, f32[3,4,16,128]{3,2,1,0:T(8,128)S(1)} %collective-permute-done.lo_ref, f32[3,4,16,128]{3,2,1,0:T(8,128)S(1)} %collective-permute-done.1.hi_ref, ...), custom_call_target="tpu_custom_call" | custom-call | tf_op jit(solution)/shard_map/pallas_call | solution.py:15
  28.3 0.1 collective-permute-start.4
  28.5 1.2 %collective-permute-done.4 = f32[8,16,128]{2,1,0:T(8,128)S(1)} collective-permute-done((f32[8,16,128]{2,1,0:T(8,128)S(1)}, f32[8,16,128]{2,1,0:T(8,128)S(1)}, u32[]{:S(2)}, u32[]{:S(2)}) %collective-permute-start.4) | collective-permute-done | bytes 65568 | tf_op jit(solution)/shard_map/ppermute | solution.py:238
  29.7 3.4 %collective-permute-start.5 = (f32[8,16,128]{2,1,0:T(8,128)S(1)}, f32[8,16,128]{2,1,0:T(8,128)S(1)}, u32[]{:S(2)}, u32[]{:S(2)}) collective-permute-start(f32[8,16,128]{2,1,0:T(8,128)S(1)} %dynamic-slice_add_fusion), channel_id=1, source_target_pairs={{0,64},{32,96},{64,0},{96,32},{128,192},{160,224},{192,128},{224,1... | collective-permute-start | bytes 196616 | tf_op jit(solution)/shard_map/ppermute | solution.py:238
  33.1 3.4 %collective-permute-done.5 = f32[8,16,128]{2,1,0:T(8,128)S(1)} collective-permute-done((f32[8,16,128]{2,1,0:T(8,128)S(1)}, f32[8,16,128]{2,1,0:T(8,128)S(1)}, u32[]{:S(2)}, u32[]{:S(2)}) %collective-permute-start.5) | collective-permute-done | bytes 65568 | tf_op jit(solution)/shard_map/ppermute | solution.py:238
  36.5 4.0 %collective-permute-start.6 = (f32[8,16,128]{2,1,0:T(8,128)S(1)}, f32[8,16,128]{2,1,0:T(8,128)S(1)}, u32[]{:S(2)}, u32[]{:S(2)}) collective-permute-start(f32[8,16,128]{2,1,0:T(8,128)S(1)} %add.48), channel_id=1, source_target_pairs={{0,192},{32,224},{64,128},{96,160},{128,64},{160,96},{192,0},{224,... | collective-permute-start | bytes 196616 | tf_op jit(solution)/shard_map/ppermute | solution.py:238
  40.5 2.5 %collective-permute-done.6 = f32[8,16,128]{2,1,0:T(8,128)S(1)} collective-permute-done((f32[8,16,128]{2,1,0:T(8,128)S(1)}, f32[8,16,128]{2,1,0:T(8,128)S(1)}, u32[]{:S(2)}, u32[]{:S(2)}) %collective-permute-start.6) | collective-permute-done | bytes 65568 | tf_op jit(solution)/shard_map/ppermute | solution.py:238
  43.1 1.2 %collective-permute-done.7.other_ref = f32[8,16,128]{2,1,0:T(8,128)S(1)} collective-permute-done((f32[8,16,128]{2,1,0:T(8,128)S(1)}, f32[8,16,128]{2,1,0:T(8,128)S(1)}, u32[]{:S(2)}, u32[]{:S(2)}) %collective-permute-start.7) | collective-permute-done | bytes 65568 | tf_op jit(solution)/shard_map/ppermute | solution.py:238
  44.4 0.4 collective-permute-start.8
  44.8 1.7 %collective-permute-start.9 = (f32[4,4,16,128]{3,2,1,0:T(8,128)S(1)}, f32[4,4,16,128]{3,2,1,0:T(8,128)S(1)}, u32[]{:S(2)}, u32[]{:S(2)}) collective-permute-start(f32[4,4,16,128]{3,2,1,0:T(8,128)S(1)} %get-tuple-element.20), channel_id=1, source_target_pairs={{0,24},{8,0},{16,8},{24,16},{1,25},{9,1},{17,9},{25,17},{2,26},{10... | collective-permute-start | bytes 393224 | tf_op jit(solution)/shard_map/ppermute | solution.py:224
  46.5 3.5 %collective-permute-done.8.lo_ref = f32[4,4,16,128]{3,2,1,0:T(8,128)S(1)} collective-permute-done((f32[4,4,16,128]{3,2,1,0:T(8,128)S(1)}, f32[4,4,16,128]{3,2,1,0:T(8,128)S(1)}, u32[]{:S(2)}, u32[]{:S(2)}) %collective-permute-start.8) | collective-permute-done | bytes 131104 | tf_op jit(solution)/shard_map/ppermute | solution.py:224
  50.1 1.3 %collective-permute-done.9.hi_ref = f32[4,4,16,128]{3,2,1,0:T(8,128)S(1)} collective-permute-done((f32[4,4,16,128]{3,2,1,0:T(8,128)S(1)}, f32[4,4,16,128]{3,2,1,0:T(8,128)S(1)}, u32[]{:S(2)}, u32[]{:S(2)}) %collective-permute-start.9) | collective-permute-done | bytes 131104 | tf_op jit(solution)/shard_map/ppermute | solution.py:224
  51.4 1.4 %collective-permute-start.10 = (f32[4,12,8,128]{3,2,1,0:T(8,128)S(1)}, f32[4,12,8,128]{3,2,1,0:T(8,128)S(1)}, u32[]{:S(2)}, u32[]{:S(2)}) collective-permute-start(f32[4,12,8,128]{3,2,1,0:T(8,128)S(1)} %get-tuple-element.21), channel_id=1, source_target_pairs={{0,7},{1,0},{2,1},{3,2},{4,3},{5,4},{6,5},{7,6},{8,15},{9,8},{10,9... | collective-permute-start | bytes 589832 | tf_op jit(solution)/shard_map/ppermute | solution.py:231
  52.8 0.7 collective-permute-start.11
  53.5 3.9 %collective-permute-done.10.above_ref = f32[4,12,8,128]{3,2,1,0:T(8,128)S(1)} collective-permute-done((f32[4,12,8,128]{3,2,1,0:T(8,128)S(1)}, f32[4,12,8,128]{3,2,1,0:T(8,128)S(1)}, u32[]{:S(2)}, u32[]{:S(2)}) %collective-permute-start.10) | collective-permute-done | bytes 196640 | tf_op jit(solution)/shard_map/ppermute | solution.py:231
  57.4 3.2 %collective-permute-done.11.below_ref = f32[4,12,8,128]{3,2,1,0:T(8,128)S(1)} collective-permute-done((f32[4,12,8,128]{3,2,1,0:T(8,128)S(1)}, f32[4,12,8,128]{3,2,1,0:T(8,128)S(1)}, u32[]{:S(2)}, u32[]{:S(2)}) %collective-permute-start.11) | collective-permute-done | bytes 196640 | tf_op jit(solution)/shard_map/ppermute | solution.py:232
  60.6 10.1 %shard_map.81 = (f32[2,16,16,128]{3,2,1,0:T(8,128)}, f32[8,4,8,128]{3,2,1,0:T(8,128)S(1)}) custom-call(f32[4,16,16,128]{3,2,1,0:T(8,128)S(1)} %get-tuple-element.18.centre_ref, f32[4,4,16,128]{3,2,1,0:T(8,128)S(1)} %collective-permute-done.8.lo_ref, f32[4,4,16,128]{3,2,1,0:T(8,128)S(1)} %collective-permute-done.9.hi_ref, ...), custom_call_target="tpu_custom_call" | custom-call | tf_op jit(solution)/shard_map/pallas_call | solution.py:15
  70.7 1.2 %collective-permute-done.12 = f32[4,4,8,128]{3,2,1,0:T(8,128)S(1)} collective-permute-done((f32[4,4,8,128]{3,2,1,0:T(8,128)S(1)}, f32[4,4,8,128]{3,2,1,0:T(8,128)S(1)}, u32[]{:S(2)}, u32[]{:S(2)}) %collective-permute-start.12) | collective-permute-done | bytes 65568 | tf_op jit(solution)/shard_map/ppermute | solution.py:238
  72.0 3.9 %collective-permute-start.15 = (f32[4,8,128]{2,1,0:T(8,128)S(1)}, f32[4,8,128]{2,1,0:T(8,128)S(1)}, u32[]{:S(2)}, u32[]{:S(2)}) collective-permute-start(f32[4,8,128]{2,1,0:T(8,128)S(1)} %get-tuple-element.32), channel_id=1, source_target_pairs={{0,192},{32,224},{64,128},{96,160},{128,64},{160,96},{192,0},{224,... | collective-permute-start | bytes 49160 | tf_op jit(solution)/shard_map/ppermute | solution.py:238
  75.9 1.9 %collective-permute-start.14 = (f32[4,8,128]{2,1,0:T(8,128)S(1)}, f32[4,8,128]{2,1,0:T(8,128)S(1)}, u32[]{:S(2)}, u32[]{:S(2)}) collective-permute-start(f32[4,8,128]{2,1,0:T(8,128)S(1)} %get-tuple-element.33), channel_id=1, source_target_pairs={{0,128},{32,160},{64,192},{96,224},{128,0},{160,32},{192,64},{224,... | collective-permute-start | bytes 49160 | tf_op jit(solution)/shard_map/ppermute | solution.py:238
  77.8 0.7 collective-permute-start.13
  78.6 5.0 %collective-permute-done.14.two_ref = f32[4,8,128]{2,1,0:T(8,128)S(1)} collective-permute-done((f32[4,8,128]{2,1,0:T(8,128)S(1)}, f32[4,8,128]{2,1,0:T(8,128)S(1)}, u32[]{:S(2)}, u32[]{:S(2)}) %collective-permute-start.14) | collective-permute-done | bytes 16416 | tf_op jit(solution)/shard_map/ppermute | solution.py:238
  83.5 0.8 shard_map.82
  (32 shorter events, 0.5 us)
Async XLA Ops:
  0.6 1.6 %copy-start = (f32[2,16,16,128]{3,2,1,0:T(8,128)S(1)}, f32[2,16,16,128]{3,2,1,0:T(8,128)}, u32[]{:S(2)}) copy-start(f32[2,16,16,128]{3,2,1,0:T(8,128)} %orb_ref.5) | copy-start | bytes 786436
  2.3 2.4 %copy-start.1 = (f32[16,16,128]{2,1,0:T(8,128)S(1)}, f32[16,16,128]{2,1,0:T(8,128)}, u32[]{:S(2)}) copy-start(f32[16,16,128]{2,1,0:T(8,128)} %pert_ref.1) | copy-start | bytes 393220
  2.3 4.7 %collective-permute-start = (f32[3,4,16,128]{3,2,1,0:T(8,128)S(1)}, f32[3,4,16,128]{3,2,1,0:T(8,128)S(1)}, u32[]{:S(2)}, u32[]{:S(2)}) collective-permute-start(f32[3,4,16,128]{3,2,1,0:T(8,128)S(1)} %pad_maximum_fusion.1), channel_id=1, source_target_pairs={{0,8},{8,16},{16,24},{24,0},{1,9},{9,17},{17,25},{25,1},{2,10},{10... | collective-permute-start | bytes 294920 | tf_op jit(solution)/shard_map/ppermute | solution.py:224
  4.6 0.9 %copy-start.5 = (f32[16,16,128]{2,1,0:T(8,128)S(1)}, f32[16,16,128]{2,1,0:T(8,128)}, u32[]{:S(2)}) copy-start(f32[16,16,128]{2,1,0:T(8,128)} %param.9) | copy-start | bytes 393220
  4.6 5.9 %collective-permute-start.1 = (f32[3,4,16,128]{3,2,1,0:T(8,128)S(1)}, f32[3,4,16,128]{3,2,1,0:T(8,128)S(1)}, u32[]{:S(2)}, u32[]{:S(2)}) collective-permute-start(f32[3,4,16,128]{3,2,1,0:T(8,128)S(1)} %pad_maximum_fusion.2), channel_id=1, source_target_pairs={{0,24},{8,0},{16,8},{24,16},{1,25},{9,1},{17,9},{25,17},{2,26},{10... | collective-permute-start | bytes 294920 | tf_op jit(solution)/shard_map/ppermute | solution.py:224
  10.5 5.4 %collective-permute-start.2 = (f32[3,12,8,128]{3,2,1,0:T(8,128)S(1)}, f32[3,12,8,128]{3,2,1,0:T(8,128)S(1)}, u32[]{:S(2)}, u32[]{:S(2)}) collective-permute-start(f32[3,12,8,128]{3,2,1,0:T(8,128)S(1)} %get-tuple-element.14), channel_id=1, source_target_pairs={{0,7},{1,0},{2,1},{3,2},{4,3},{5,4},{6,5},{7,6},{8,15},{9,8},{10,9... | collective-permute-start | bytes 442376 | tf_op jit(solution)/shard_map/ppermute | solution.py:231
  13.2 7.3 %collective-permute-start.3 = (f32[3,12,8,128]{3,2,1,0:T(8,128)S(1)}, f32[3,12,8,128]{3,2,1,0:T(8,128)S(1)}, u32[]{:S(2)}, u32[]{:S(2)}) collective-permute-start(f32[3,12,8,128]{3,2,1,0:T(8,128)S(1)} %get-tuple-element.15), channel_id=1, source_target_pairs={{0,1},{1,2},{2,3},{3,4},{4,5},{5,6},{6,7},{7,0},{8,9},{9,10},{10,1... | collective-permute-start | bytes 442376 | tf_op jit(solution)/shard_map/ppermute | solution.py:232
  13.3 7.3 %copy-start.3 = (f32[2]{0:T(128)S(1)}, f32[2]{0:T(128)}, u32[]{:S(2)}) copy-start(f32[2]{0:T(128)} %occ_ref.3) | copy-start | bytes 28
  13.3 7.3 %copy-start.4 = (f32[2]{0:T(128)S(1)}, f32[2]{0:T(128)}, u32[]{:S(2)}) copy-start(f32[2]{0:T(128)} %shift_ref.1) | copy-start | bytes 28
  28.3 1.3 %collective-permute-start.4 = (f32[8,16,128]{2,1,0:T(8,128)S(1)}, f32[8,16,128]{2,1,0:T(8,128)S(1)}, u32[]{:S(2)}, u32[]{:S(2)}) collective-permute-start(f32[8,16,128]{2,1,0:T(8,128)S(1)} %constant_dynamic-slice_fusion), channel_id=1, source_target_pairs={{0,32},{32,0},{64,96},{96,64},{128,160},{160,128},{192,224},{224,1... | collective-permute-start | bytes 196616 | tf_op jit(solution)/shard_map/ppermute | solution.py:238
  29.7 6.7 %collective-permute-start.5 = (f32[8,16,128]{2,1,0:T(8,128)S(1)}, f32[8,16,128]{2,1,0:T(8,128)S(1)}, u32[]{:S(2)}, u32[]{:S(2)}) collective-permute-start(f32[8,16,128]{2,1,0:T(8,128)S(1)} %dynamic-slice_add_fusion), channel_id=1, source_target_pairs={{0,64},{32,96},{64,0},{96,32},{128,192},{160,224},{192,128},{224,1... | collective-permute-start | bytes 196616 | tf_op jit(solution)/shard_map/ppermute | solution.py:238
  36.4 7.9 %copy-start.2 = (f32[16,16,128]{2,1,0:T(8,128)S(1)}, f32[16,16,128]{2,1,0:T(8,128)}, u32[]{:S(2)}) copy-start(f32[16,16,128]{2,1,0:T(8,128)} %kern_ref.1) | copy-start | bytes 393220
  36.5 6.5 %collective-permute-start.6 = (f32[8,16,128]{2,1,0:T(8,128)S(1)}, f32[8,16,128]{2,1,0:T(8,128)S(1)}, u32[]{:S(2)}, u32[]{:S(2)}) collective-permute-start(f32[8,16,128]{2,1,0:T(8,128)S(1)} %add.48), channel_id=1, source_target_pairs={{0,192},{32,224},{64,128},{96,160},{128,64},{160,96},{192,0},{224,... | collective-permute-start | bytes 196616 | tf_op jit(solution)/shard_map/ppermute | solution.py:238
  43.0 1.3 %collective-permute-start.7 = (f32[8,16,128]{2,1,0:T(8,128)S(1)}, f32[8,16,128]{2,1,0:T(8,128)S(1)}, u32[]{:S(2)}, u32[]{:S(2)}) collective-permute-start(f32[8,16,128]{2,1,0:T(8,128)S(1)} %add.49.own_ref), channel_id=1, source_target_pairs={{0,32},{32,0},{64,96},{96,64},{128,160},{160,128},{192,224},{224,1... | collective-permute-start | bytes 196616 | tf_op jit(solution)/shard_map/ppermute | solution.py:238
  44.4 5.6 %collective-permute-start.8 = (f32[4,4,16,128]{3,2,1,0:T(8,128)S(1)}, f32[4,4,16,128]{3,2,1,0:T(8,128)S(1)}, u32[]{:S(2)}, u32[]{:S(2)}) collective-permute-start(f32[4,4,16,128]{3,2,1,0:T(8,128)S(1)} %get-tuple-element.19), channel_id=1, source_target_pairs={{0,8},{8,16},{16,24},{24,0},{1,9},{9,17},{17,25},{25,1},{2,10},{10... | collective-permute-start | bytes 393224 | tf_op jit(solution)/shard_map/ppermute | solution.py:224
  44.8 6.6 %collective-permute-start.9 = (f32[4,4,16,128]{3,2,1,0:T(8,128)S(1)}, f32[4,4,16,128]{3,2,1,0:T(8,128)S(1)}, u32[]{:S(2)}, u32[]{:S(2)}) collective-permute-start(f32[4,4,16,128]{3,2,1,0:T(8,128)S(1)} %get-tuple-element.20), channel_id=1, source_target_pairs={{0,24},{8,0},{16,8},{24,16},{1,25},{9,1},{17,9},{25,17},{2,26},{10... | collective-permute-start | bytes 393224 | tf_op jit(solution)/shard_map/ppermute | solution.py:224
  51.4 6.0 %collective-permute-start.10 = (f32[4,12,8,128]{3,2,1,0:T(8,128)S(1)}, f32[4,12,8,128]{3,2,1,0:T(8,128)S(1)}, u32[]{:S(2)}, u32[]{:S(2)}) collective-permute-start(f32[4,12,8,128]{3,2,1,0:T(8,128)S(1)} %get-tuple-element.21), channel_id=1, source_target_pairs={{0,7},{1,0},{2,1},{3,2},{4,3},{5,4},{6,5},{7,6},{8,15},{9,8},{10,9... | collective-permute-start | bytes 589832 | tf_op jit(solution)/shard_map/ppermute | solution.py:231
  52.8 7.8 %collective-permute-start.11 = (f32[4,12,8,128]{3,2,1,0:T(8,128)S(1)}, f32[4,12,8,128]{3,2,1,0:T(8,128)S(1)}, u32[]{:S(2)}, u32[]{:S(2)}) collective-permute-start(f32[4,12,8,128]{3,2,1,0:T(8,128)S(1)} %get-tuple-element.22), channel_id=1, source_target_pairs={{0,1},{1,2},{2,3},{3,4},{4,5},{5,6},{6,7},{7,0},{8,9},{9,10},{10,1... | collective-permute-start | bytes 589832 | tf_op jit(solution)/shard_map/ppermute | solution.py:232
  70.7 1.3 %collective-permute-start.12 = (f32[4,4,8,128]{3,2,1,0:T(8,128)S(1)}, f32[4,4,8,128]{3,2,1,0:T(8,128)S(1)}, u32[]{:S(2)}, u32[]{:S(2)}) collective-permute-start(f32[4,4,8,128]{3,2,1,0:T(8,128)S(1)} %dynamic-slice_bitcast_fusion), channel_id=1, source_target_pairs={{0,32},{32,0},{64,96},{96,64},{128,160},{160,128},{192,224},{224,1... | collective-permute-start | bytes 196616 | tf_op jit(solution)/shard_map/ppermute | solution.py:238
  72.0 6.6 %collective-permute-start.15 = (f32[4,8,128]{2,1,0:T(8,128)S(1)}, f32[4,8,128]{2,1,0:T(8,128)S(1)}, u32[]{:S(2)}, u32[]{:S(2)}) collective-permute-start(f32[4,8,128]{2,1,0:T(8,128)S(1)} %get-tuple-element.32), channel_id=1, source_target_pairs={{0,192},{32,224},{64,128},{96,160},{128,64},{160,96},{192,0},{224,... | collective-permute-start | bytes 49160 | tf_op jit(solution)/shard_map/ppermute | solution.py:238
  75.9 7.6 %collective-permute-start.14 = (f32[4,8,128]{2,1,0:T(8,128)S(1)}, f32[4,8,128]{2,1,0:T(8,128)S(1)}, u32[]{:S(2)}, u32[]{:S(2)}) collective-permute-start(f32[4,8,128]{2,1,0:T(8,128)S(1)} %get-tuple-element.33), channel_id=1, source_target_pairs={{0,128},{32,160},{64,192},{96,224},{128,0},{160,32},{192,64},{224,... | collective-permute-start | bytes 49160 | tf_op jit(solution)/shard_map/ppermute | solution.py:238
  77.8 5.7 %collective-permute-start.13 = (f32[4,8,128]{2,1,0:T(8,128)S(1)}, f32[4,8,128]{2,1,0:T(8,128)S(1)}, u32[]{:S(2)}, u32[]{:S(2)}) collective-permute-start(f32[4,8,128]{2,1,0:T(8,128)S(1)} %get-tuple-element.34), channel_id=1, source_target_pairs={{0,64},{32,96},{64,0},{96,32},{128,192},{160,224},{192,128},{224,1... | collective-permute-start | bytes 49160 | tf_op jit(solution)/shard_map/ppermute | solution.py:238

commit v2 on v1

--- a/solution.py
+++ b/solution.py
@@ -11,11 +11,11 @@
 SMEM = pl.BlockSpec(memory_space=pltpu.SMEM)
 
 
-def call(body, outs, *args, scratch=(), smem=0):
+def call(body, outs, *args, scratch=(), smem=0, where=VMEM):
     return pl.pallas_call(
         body,
         out_shape=outs,
-        in_specs=[VMEM] * (len(args) - smem) + [SMEM] * smem,
+        in_specs=[where] * (len(args) - smem) + [SMEM] * smem,
         out_specs=jax.tree.map(lambda _: VMEM, outs),
         scratch_shapes=list(scratch),
         compiler_params=pltpu.CompilerParams(vmem_limit_bytes=48 * 2**20),
@@ -30,12 +30,14 @@
     return lax.broadcasted_iota(jnp.int32, (8, 128), 0) < 4
 
 
-def pack_z(row, head_ref, tail_ref, field):
+def pack_z(row, even, near_ref, far_ref, field):
     low = low_half()
     for j in range(12):
         a, b = row(j), row(j + 12)
-        head_ref[field, j] = jnp.where(low, a[:8], pltpu.roll(b[:8], 4, 0))
-        tail_ref[field, j] = jnp.where(low, pltpu.roll(b[8:], 4, 0), a[8:])
+        head = jnp.where(low, a[:8], pltpu.roll(b[:8], 4, 0))
+        tail = jnp.where(low, pltpu.roll(b[8:], 4, 0), a[8:])
+        near_ref[field, j] = jnp.where(even, tail, head)
+        far_ref[field, j] = jnp.where(even, head, tail)
 
 
 def padded_row(centre_ref, lo_ref, hi_ref, field):
@@ -49,17 +51,19 @@
     return row
 
 
-def pack_kernel(centre_ref, lo_ref, hi_ref, head_ref, tail_ref):
+def pack_kernel(centre_ref, lo_ref, hi_ref, odd_ref, far_ref, near_ref):
+    even = odd_ref[0] == 0
     for field in range(centre_ref.shape[0]):
-        pack_z(padded_row(centre_ref, lo_ref, hi_ref, field), head_ref, tail_ref, field)
-
-
-def assemble(row, above_ref, below_ref, field, dest_ref, at):
-    low = low_half()
+        pack_z(padded_row(centre_ref, lo_ref, hi_ref, field), even, near_ref, far_ref, field)
+
+
+def assemble(row, near_ref, far_ref, field, odd_ref, dest_ref, at):
+    low, even = low_half(), odd_ref[0] == 0
     for r in range(24):
         dest_ref[at, r, 0:16] = row(r)
     for j in range(12):
-        above, below = above_ref[field, j], below_ref[field, j]
+        near, far = near_ref[field, j], far_ref[field, j]
+        above, below = jnp.where(even, near, far), jnp.where(even, far, near)
         dest_ref[at, j, 16:24] = jnp.where(low, above, below)
         dest_ref[at, j + 12, 16:24] = pltpu.roll(jnp.where(low, below, above), 4, 0)
 
@@ -72,17 +76,12 @@
     return pltpu.roll(u, 1, u.ndim - 1) + pltpu.roll(u, 127, u.ndim - 1)
 
 
-def by_rows(first, last, load, emit, step=2):
-    def body(i, carry):
-        before, at = carry
-        r = first + step * i
-        for k in range(step):
-            after = load(r + k + 1)
-            emit(r + k, before, at, after)
-            before, at = at, after
-        return before, at
-
-    lax.fori_loop(0, (last - first) // step, body, (load(first - 1), load(first)))
+def by_rows(first, last, load, emit):
+    before, at = load(first - 1), load(first)
+    for r in range(first, last):
+        after = load(r + 1)
+        emit(r, before, at, after)
+        before, at = at, after
 
 
 def sources(p_ref, scale_ref, sc_ref, o):
@@ -132,26 +131,40 @@
 
 
 def first_kernel(
-    centre_ref, lo_ref, hi_ref, above_ref, below_ref, orb_ref, shift_ref, occ_ref,
+    centre_ref, lo_ref, hi_ref, far_ref, near_ref, orb_ref, shift_ref, occ_ref, odd_ref,
     resp_ref, dens_ref, scale_ref, p_ref, sc_ref, a_ref, b_ref,
 ):
     for field in range(2):
-        assemble(padded_row(centre_ref, lo_ref, hi_ref, field), above_ref, below_ref, field, p_ref, field)
-    assemble(padded_row(centre_ref, lo_ref, hi_ref, 2), above_ref, below_ref, 2, a_ref, 0)
+        assemble(padded_row(centre_ref, lo_ref, hi_ref, field), near_ref, far_ref, field, odd_ref, p_ref, field)
+    assemble(padded_row(centre_ref, lo_ref, hi_ref, 2), near_ref, far_ref, 2, odd_ref, a_ref, 0)
     for o in range(2):
         base = 32.0 / 15.0 + shift_ref[o]
 
-        def scales(r, _):
+        for r in range(1, 23):
             scale_ref[o, r] = (RELAX / 60.0) / (base + a_ref[0, r])
-            return 0
-
-        lax.fori_loop(1, 23, scales, 0)
     for o in range(2):
         sources(p_ref, scale_ref, sc_ref, o)
     for o in range(2):
         sweep(sc_ref, scale_ref, sc_ref, o, 2, into(a_ref, o))
         sweep(a_ref, scale_ref, sc_ref, o, 3, into(b_ref, o))
         last_sweep(b_ref, scale_ref, sc_ref, o, orb_ref, occ_ref, resp_ref, dens_ref)
+
+
+def product_kernel(orb_hbm, pert_hbm, pot_hbm, centre_ref, up_ref, down_ref, orb_ref, pert_ref, pot_ref, sems):
+    pairs = ((orb_hbm, orb_ref), (pert_hbm, pert_ref), (pot_hbm, pot_ref))
+    copies = [pltpu.make_async_copy(src, dest, sems.at[i]) for i, (src, dest) in enumerate(pairs)]
+    for copy in copies:
+        copy.start()
+    for copy in copies:
+        copy.wait()
+    for y in range(16):
+        for field in range(3):
+            value = pot_ref[y] if field == 2 else pert_ref[y] * orb_ref[field, y]
+            centre_ref[field, y] = value
+            if y < 4:
+                down_ref[field, y] = value
+            if y >= 12:
+                up_ref[field, y - 12] = value
 
 
 def change_kernel(own_ref, other_ref, pert_ref, kern_ref, orb_ref, resp_ref, core_ref, centre_ref, up_ref, down_ref):
@@ -187,12 +200,12 @@
 
 
 def second_kernel(
-    centre_ref, lo_ref, hi_ref, above_ref, below_ref, scale_ref, orb_ref, occ_ref,
+    centre_ref, lo_ref, hi_ref, far_ref, near_ref, scale_ref, orb_ref, occ_ref, odd_ref,
     resp_ref, out_ref, p_ref, u_ref, sc_ref, a_ref, b_ref, dens_ref,
 ):
     for o in range(2):
-        assemble(padded_row(centre_ref, lo_ref, hi_ref, o), above_ref, below_ref, o, p_ref, o)
-        assemble(padded_row(centre_ref, lo_ref, hi_ref, 2 + o), above_ref, below_ref, 2 + o, u_ref, o)
+        assemble(padded_row(centre_ref, lo_ref, hi_ref, o), near_ref, far_ref, o, odd_ref, p_ref, o)
+        assemble(padded_row(centre_ref, lo_ref, hi_ref, 2 + o), near_ref, far_ref, 2 + o, odd_ref, u_ref, o)
     for o in range(2):
         sources(p_ref, scale_ref, sc_ref, o)
         sweep(u_ref, scale_ref, sc_ref, o, 1, into(a_ref, o))
@@ -224,13 +237,18 @@
     return lax.ppermute(up, "gy", ring("gy", 1)), lax.ppermute(down, "gy", ring("gy", -1))
 
 
-def exchange_z(centre, lo, hi):
+def exchange_z(centre, lo, hi, odd):
     fields = centre.shape[0]
     strip = f32(fields, 12, 8, 128)
-    head, tail = call(pack_kernel, (strip, strip), centre, lo, hi)
-    above = lax.ppermute(head, "gz", ring("gz", -1))
-    below = lax.ppermute(tail, "gz", ring("gz", 1))
-    return above, below
+    far, near = call(pack_kernel, (strip, strip), centre, lo, hi, odd, smem=1)
+    count = lax.axis_size("gz")
+    far = lax.ppermute(far, "gz", far_pairs(count))
+    near = lax.ppermute(near, "gz", [(i, i ^ 1) for i in range(count)])
+    return near, far
+
+
+def far_pairs(count):
+    return [(i, (i - 1) % count if i % 2 == 0 else (i + 1) % count) for i in range(count)]
 
 
 def partner(value, step):
@@ -240,20 +258,23 @@
 
 def on_device(orbitals, orbital_shift, occupation, potential, perturbation, kernel):
     group = lax.axis_index("bands")
-    core, far = group % 2, group // 2
+    core, chip = group % 2, group // 2
     padded = f32(2, 24, 24, 128)
     wide = pltpu.VMEM((2, 24, 24, 128), jnp.float32)
 
-    def fields(rows):
-        return jnp.concatenate([perturbation[None, rows] * orbitals[:, rows], potential[None, rows]], 0)
-
-    lo, hi = exchange_y(fields(slice(12, 16)), fields(slice(0, 4)))
-    centre = fields(slice(0, 16))
-    above, below = exchange_z(centre, lo, hi)
+    odd = (lax.axis_index("gz") % 2)[None].astype(jnp.int32)
+    centre, up, down = call(
+        product_kernel, (f32(3, 16, 16, 128), f32(3, 4, 16, 128), f32(3, 4, 16, 128)),
+        orbitals, perturbation, potential, where=pl.BlockSpec(memory_space=pltpu.HBM),
+        scratch=[pltpu.VMEM(shape, jnp.float32) for shape in ((2, 16, 16, 128), (16, 16, 128), (16, 16, 128))]
+        + [pltpu.SemaphoreType.DMA((3,))],
+    )
+    lo, hi = exchange_y(up, down)
+    near, far = exchange_z(centre, lo, hi, odd)
     response, partial, scale = call(
         first_kernel, (f32(2, 16, 16, 128), f32(16, 16, 128), padded),
-        centre, lo, hi, above, below, orbitals, orbital_shift, occupation,
-        scratch=[wide] * 4, smem=2,
+        centre, lo, hi, far, near, orbitals, orbital_shift, occupation, odd,
+        scratch=[wide] * 4, smem=3,
     )
 
     own = lax.dynamic_slice_in_dim(partial, 8 * core, 8, 0)
@@ -266,11 +287,11 @@
         own, other, perturbation, kernel, orbitals, response, core[None].astype(jnp.int32), smem=1,
     )
     lo, hi = exchange_y(up, down)
-    above, below = exchange_z(centre, lo, hi)
+    near, far = exchange_z(centre, lo, hi, odd)
     response, blocks = call(
         second_kernel, (f32(2, 16, 16, 128), f32(8, 4, 8, 128)),
-        centre, lo, hi, above, below, scale, orbitals, occupation,
-        scratch=[wide] * 5 + [pltpu.VMEM((16, 16, 128), jnp.float32)], smem=1,
+        centre, lo, hi, far, near, scale, orbitals, occupation, odd,
+        scratch=[wide] * 5 + [pltpu.VMEM((16, 16, 128), jnp.float32)], smem=2,
     )
 
     blocks = blocks.reshape(4, 2, 4, 8, 128)
@@ -278,7 +299,7 @@
     kept = kept + partner(lax.dynamic_index_in_dim(blocks, 1 - core, 1, keepdims=False), 1)
 
     def block_of(step):
-        return lax.dynamic_index_in_dim(kept, far ^ step, 0, keepdims=False)
+        return lax.dynamic_index_in_dim(kept, chip ^ step, 0, keepdims=False)
 
     two, one, three = (partner(block_of(step), 2 * step) for step in (2, 1, 3))
     density = call(final_kernel, f32(16, 16, 16), block_of(0), one, two, three)

time: 84.5 us -> 70.6 us (0.84)
  Pallas kernels: 18.8 us -> 5.97 us
  waiting for transfers between devices: 38.7 us -> 36 us
  starting transfers between devices: 23.4 us -> 24.8 us
    pallas_call x6 -> x7, Pallas kernels: 18.8 us -> 5.97 us  [call(): pl.pallas_call(body, out_shape=outs, in_specs=[where] * (len(args) - smem...]
    ppermute x4, waiting for transfers between devices: 14.3 us -> 10.8 us  [the longest x2 9.2 us: exchange_z(): far = lax.ppermute(far, 'gz', far_pairs(count))]
    unnamed x12 -> x16, local copies, waits for them, and re-layouts: 0.79 us -> 2.77 us
    ppermute x4, starting transfers between devices: 4.81 us -> 6.25 us  [the longest x2 6.25 us: exchange_z(): far = lax.ppermute(far, 'gz', far_pairs(count))]
    ppermute x2, waiting for transfers between devices: 4.99 us -> 5.93 us  [exchange_y(): lax.ppermute(up, 'gy', ring('gy', 1))]
where the time goes in v2:
time: 70.6 us; the launch traced here: 70.4 us
  waiting for transfers between devices  36 us (51%)
  starting transfers between devices  24.8 us (35%)
  Pallas kernels  5.97 us (8%)
  local copies, waits for them, and re-layouts  2.81 us (4%)
  between operations  0.8 us (1%)
    ppermute x8, waiting for transfers between devices, partner(): return lax.ppermute(value, 'bands', [(i, i ^ step) for i in range(count)])  14.5 us
    ppermute x8, starting transfers between devices, partner(): return lax.ppermute(value, 'bands', [(i, i ^ step) for i in range(count)])  14.2 us
    ppermute x2, waiting for transfers between devices, exchange_z(): far = lax.ppermute(far, 'gz', far_pairs(count))  9.2 us
    ppermute x2, starting transfers between devices, exchange_z(): far = lax.ppermute(far, 'gz', far_pairs(count))  6.25 us
    pallas_call x7, Pallas kernels, call(): pl.pallas_call(body, out_shape=outs, in_specs=[where] * (len(args) - smem...  5.97 us
    ppermute x2, waiting for transfers between devices, exchange_y(): lax.ppermute(up, 'gy', ring('gy', 1))  5.93 us
    ppermute x2, waiting for transfers between devices, exchange_y(): lax.ppermute(down, 'gy', ring('gy', -1))  4.73 us
    unnamed x16, local copies, waits for them, and re-layouts  2.77 us
  transfers between devices with their start and end apart: 16, of which 14 were waited for; matrix products, arithmetic and copies ran while one was open for 0% of the time, Pallas kernels for 0%

profile of v2, /device:TPU:6, one launch (start us, length us, event | category | flops | bytes accessed | tf_op | source)
XLA Modules:
  0.0 70.4 jit_solution(11152346418921896153)
XLA Ops:
  0.6 0.9 %copy-done = f32[2,16,16,128]{3,2,1,0:T(8,128)S(1)} copy-done((f32[2,16,16,128]{3,2,1,0:T(8,128)S(1)}, f32[2,16,16,128]{3,2,1,0:T(8,128)}, u32[]{:S(2)}) %copy-start) | copy-done | bytes 262168
  1.6 0.9 %copy-done.2 = f32[16,16,128]{2,1,0:T(8,128)S(1)} copy-done((f32[16,16,128]{2,1,0:T(8,128)S(1)}, f32[16,16,128]{2,1,0:T(8,128)}, u32[]{:S(2)}) %copy-start.2) | copy-done | bytes 131096
  2.5 0.9 %copy-done.5 = f32[16,16,128]{2,1,0:T(8,128)S(1)} copy-done((f32[16,16,128]{2,1,0:T(8,128)S(1)}, f32[16,16,128]{2,1,0:T(8,128)}, u32[]{:S(2)}) %copy-start.5) | copy-done | bytes 131096
  3.4 0.4 shard_map.77
  3.8 2.3 %collective-permute-start = (f32[3,4,16,128]{3,2,1,0:T(8,128)S(1)}, f32[3,4,16,128]{3,2,1,0:T(8,128)S(1)}, u32[]{:S(2)}, u32[]{:S(2)}) collective-permute-start(f32[3,4,16,128]{3,2,1,0:T(8,128)S(1)} %get-tuple-element.18), channel_id=1, source_target_pairs={{0,8},{8,16},{16,24},{24,0},{1,9},{9,17},{17,25},{25,1},{2,10},{10... | collective-permute-start | bytes 294920 | tf_op jit(solution)/shard_map/ppermute | solution.py:237
  6.1 2.4 %collective-permute-done.lo_ref = f32[3,4,16,128]{3,2,1,0:T(8,128)S(1)} collective-permute-done((f32[3,4,16,128]{3,2,1,0:T(8,128)S(1)}, f32[3,4,16,128]{3,2,1,0:T(8,128)S(1)}, u32[]{:S(2)}, u32[]{:S(2)}) %collective-permute-start) | collective-permute-done | bytes 98336 | tf_op jit(solution)/shard_map/ppermute | solution.py:237
  8.5 3.4 %collective-permute-done.1.hi_ref = f32[3,4,16,128]{3,2,1,0:T(8,128)S(1)} collective-permute-done((f32[3,4,16,128]{3,2,1,0:T(8,128)S(1)}, f32[3,4,16,128]{3,2,1,0:T(8,128)S(1)}, u32[]{:S(2)}, u32[]{:S(2)}) %collective-permute-start.1) | collective-permute-done | bytes 98336 | tf_op jit(solution)/shard_map/ppermute | solution.py:237
  12.0 2.7 %collective-permute-start.2 = (f32[3,12,8,128]{3,2,1,0:T(8,128)S(1)}, f32[3,12,8,128]{3,2,1,0:T(8,128)S(1)}, u32[]{:S(2)}, u32[]{:S(2)}) collective-permute-start(f32[3,12,8,128]{3,2,1,0:T(8,128)S(1)} %get-tuple-element.20), channel_id=1, source_target_pairs={{0,7},{1,2},{2,1},{3,4},{4,3},{5,6},{6,5},{7,0},{8,15},{9,10},{10,... | collective-permute-start | bytes 442376 | tf_op jit(solution)/shard_map/ppermute | solution.py:245
  14.7 4.6 %collective-permute-done.2.far_ref = f32[3,12,8,128]{3,2,1,0:T(8,128)S(1)} collective-permute-done((f32[3,12,8,128]{3,2,1,0:T(8,128)S(1)}, f32[3,12,8,128]{3,2,1,0:T(8,128)S(1)}, u32[]{:S(2)}, u32[]{:S(2)}) %collective-permute-start.2) | collective-permute-done | bytes 147488 | tf_op jit(solution)/shard_map/ppermute | solution.py:245
  19.3 0.5 collective-permute-done.3.near_ref
  19.9 1.8 %shard_map.79 = (f32[2,16,16,128]{3,2,1,0:T(8,128)S(1)}, f32[16,16,128]{2,1,0:T(8,128)S(1)}, f32[2,24,24,128]{3,2,1,0:T(8,128)S(1)}) custom-call(f32[3,16,16,128]{3,2,1,0:T(8,128)S(1)} %get-tuple-element.17.centre_ref, f32[3,4,16,128]{3,2,1,0:T(8,128)S(1)} %collective-permute-done.lo_ref, f32[3,4,16,128]{3,2,1,0:T(8,128)S(1)} %collective-permute-done.1.hi_ref, ...), custom_call_target="tpu_custom_call" | custom-call | tf_op jit(solution)/shard_map/pallas_call | solution.py:15
  21.7 0.1 collective-permute-start.4
  21.8 1.2 %collective-permute-done.4 = f32[8,16,128]{2,1,0:T(8,128)S(1)} collective-permute-done((f32[8,16,128]{2,1,0:T(8,128)S(1)}, f32[8,16,128]{2,1,0:T(8,128)S(1)}, u32[]{:S(2)}, u32[]{:S(2)}) %collective-permute-start.4) | collective-permute-done | bytes 65568 | tf_op jit(solution)/shard_map/ppermute | solution.py:256
  23.0 3.4 %collective-permute-start.5 = (f32[8,16,128]{2,1,0:T(8,128)S(1)}, f32[8,16,128]{2,1,0:T(8,128)S(1)}, u32[]{:S(2)}, u32[]{:S(2)}) collective-permute-start(f32[8,16,128]{2,1,0:T(8,128)S(1)} %dynamic-slice_add_fusion), channel_id=1, source_target_pairs={{0,64},{32,96},{64,0},{96,32},{128,192},{160,224},{192,128},{224,1... | collective-permute-start | bytes 196616 | tf_op jit(solution)/shard_map/ppermute | solution.py:256
  26.4 3.4 %collective-permute-done.5 = f32[8,16,128]{2,1,0:T(8,128)S(1)} collective-permute-done((f32[8,16,128]{2,1,0:T(8,128)S(1)}, f32[8,16,128]{2,1,0:T(8,128)S(1)}, u32[]{:S(2)}, u32[]{:S(2)}) %collective-permute-start.5) | collective-permute-done | bytes 65568 | tf_op jit(solution)/shard_map/ppermute | solution.py:256
  29.8 4.0 %collective-permute-start.6 = (f32[8,16,128]{2,1,0:T(8,128)S(1)}, f32[8,16,128]{2,1,0:T(8,128)S(1)}, u32[]{:S(2)}, u32[]{:S(2)}) collective-permute-start(f32[8,16,128]{2,1,0:T(8,128)S(1)} %add.52), channel_id=1, source_target_pairs={{0,192},{32,224},{64,128},{96,160},{128,64},{160,96},{192,0},{224,... | collective-permute-start | bytes 196616 | tf_op jit(solution)/shard_map/ppermute | solution.py:256
  33.8 2.5 %collective-permute-done.6 = f32[8,16,128]{2,1,0:T(8,128)S(1)} collective-permute-done((f32[8,16,128]{2,1,0:T(8,128)S(1)}, f32[8,16,128]{2,1,0:T(8,128)S(1)}, u32[]{:S(2)}, u32[]{:S(2)}) %collective-permute-start.6) | collective-permute-done | bytes 65568 | tf_op jit(solution)/shard_map/ppermute | solution.py:256
  36.4 1.2 %collective-permute-done.7.other_ref = f32[8,16,128]{2,1,0:T(8,128)S(1)} collective-permute-done((f32[8,16,128]{2,1,0:T(8,128)S(1)}, f32[8,16,128]{2,1,0:T(8,128)S(1)}, u32[]{:S(2)}, u32[]{:S(2)}) %collective-permute-start.7) | collective-permute-done | bytes 65568 | tf_op jit(solution)/shard_map/ppermute | solution.py:256
  37.8 0.4 collective-permute-start.8
  38.1 1.7 %collective-permute-start.9 = (f32[4,4,16,128]{3,2,1,0:T(8,128)S(1)}, f32[4,4,16,128]{3,2,1,0:T(8,128)S(1)}, u32[]{:S(2)}, u32[]{:S(2)}) collective-permute-start(f32[4,4,16,128]{3,2,1,0:T(8,128)S(1)} %get-tuple-element.26), channel_id=1, source_target_pairs={{0,24},{8,0},{16,8},{24,16},{1,25},{9,1},{17,9},{25,17},{2,26},{10... | collective-permute-start | bytes 393224 | tf_op jit(solution)/shard_map/ppermute | solution.py:237
  39.9 3.5 %collective-permute-done.8.lo_ref = f32[4,4,16,128]{3,2,1,0:T(8,128)S(1)} collective-permute-done((f32[4,4,16,128]{3,2,1,0:T(8,128)S(1)}, f32[4,4,16,128]{3,2,1,0:T(8,128)S(1)}, u32[]{:S(2)}, u32[]{:S(2)}) %collective-permute-start.8) | collective-permute-done | bytes 131104 | tf_op jit(solution)/shard_map/ppermute | solution.py:237
  43.4 1.3 %collective-permute-done.9.hi_ref = f32[4,4,16,128]{3,2,1,0:T(8,128)S(1)} collective-permute-done((f32[4,4,16,128]{3,2,1,0:T(8,128)S(1)}, f32[4,4,16,128]{3,2,1,0:T(8,128)S(1)}, u32[]{:S(2)}, u32[]{:S(2)}) %collective-permute-start.9) | collective-permute-done | bytes 131104 | tf_op jit(solution)/shard_map/ppermute | solution.py:237
  44.7 3.5 %collective-permute-start.10 = (f32[4,12,8,128]{3,2,1,0:T(8,128)S(1)}, f32[4,12,8,128]{3,2,1,0:T(8,128)S(1)}, u32[]{:S(2)}, u32[]{:S(2)}) collective-permute-start(f32[4,12,8,128]{3,2,1,0:T(8,128)S(1)} %get-tuple-element.27), channel_id=1, source_target_pairs={{0,7},{1,2},{2,1},{3,4},{4,3},{5,6},{6,5},{7,0},{8,15},{9,10},{10,... | collective-permute-start | bytes 589832 | tf_op jit(solution)/shard_map/ppermute | solution.py:245
  48.3 4.6 %collective-permute-done.10.far_ref = f32[4,12,8,128]{3,2,1,0:T(8,128)S(1)} collective-permute-done((f32[4,12,8,128]{3,2,1,0:T(8,128)S(1)}, f32[4,12,8,128]{3,2,1,0:T(8,128)S(1)}, u32[]{:S(2)}, u32[]{:S(2)}) %collective-permute-start.10) | collective-permute-done | bytes 196640 | tf_op jit(solution)/shard_map/ppermute | solution.py:245
  52.9 1.1 %collective-permute-done.11.near_ref = f32[4,12,8,128]{3,2,1,0:T(8,128)S(1)} collective-permute-done((f32[4,12,8,128]{3,2,1,0:T(8,128)S(1)}, f32[4,12,8,128]{3,2,1,0:T(8,128)S(1)}, u32[]{:S(2)}, u32[]{:S(2)}) %collective-permute-start.11) | collective-permute-done | bytes 196640 | tf_op jit(solution)/shard_map/ppermute | solution.py:246
  53.9 2.9 %shard_map.82 = (f32[2,16,16,128]{3,2,1,0:T(8,128)}, f32[8,4,8,128]{3,2,1,0:T(8,128)S(1)}) custom-call(f32[4,16,16,128]{3,2,1,0:T(8,128)S(1)} %get-tuple-element.24.centre_ref, f32[4,4,16,128]{3,2,1,0:T(8,128)S(1)} %collective-permute-done.8.lo_ref, f32[4,4,16,128]{3,2,1,0:T(8,128)S(1)} %collective-permute-done.9.hi_ref, ...), custom_call_target="tpu_custom_call" | custom-call | tf_op jit(solution)/shard_map/pallas_call | solution.py:15
  56.8 1.2 %collective-permute-done.12 = f32[4,4,8,128]{3,2,1,0:T(8,128)S(1)} collective-permute-done((f32[4,4,8,128]{3,2,1,0:T(8,128)S(1)}, f32[4,4,8,128]{3,2,1,0:T(8,128)S(1)}, u32[]{:S(2)}, u32[]{:S(2)}) %collective-permute-start.12) | collective-permute-done | bytes 65568 | tf_op jit(solution)/shard_map/ppermute | solution.py:256
  58.1 3.9 %collective-permute-start.15 = (f32[4,8,128]{2,1,0:T(8,128)S(1)}, f32[4,8,128]{2,1,0:T(8,128)S(1)}, u32[]{:S(2)}, u32[]{:S(2)}) collective-permute-start(f32[4,8,128]{2,1,0:T(8,128)S(1)} %get-tuple-element.32), channel_id=1, source_target_pairs={{0,192},{32,224},{64,128},{96,160},{128,64},{160,96},{192,0},{224,... | collective-permute-start | bytes 49160 | tf_op jit(solution)/shard_map/ppermute | solution.py:256
  62.0 1.9 %collective-permute-start.14 = (f32[4,8,128]{2,1,0:T(8,128)S(1)}, f32[4,8,128]{2,1,0:T(8,128)S(1)}, u32[]{:S(2)}, u32[]{:S(2)}) collective-permute-start(f32[4,8,128]{2,1,0:T(8,128)S(1)} %get-tuple-element.33), channel_id=1, source_target_pairs={{0,128},{32,160},{64,192},{96,224},{128,0},{160,32},{192,64},{224,... | collective-permute-start | bytes 49160 | tf_op jit(solution)/shard_map/ppermute | solution.py:256
  63.9 0.8 %collective-permute-start.13 = (f32[4,8,128]{2,1,0:T(8,128)S(1)}, f32[4,8,128]{2,1,0:T(8,128)S(1)}, u32[]{:S(2)}, u32[]{:S(2)}) collective-permute-start(f32[4,8,128]{2,1,0:T(8,128)S(1)} %get-tuple-element.34), channel_id=1, source_target_pairs={{0,64},{32,96},{64,0},{96,32},{128,192},{160,224},{192,128},{224,1... | collective-permute-start | bytes 49160 | tf_op jit(solution)/shard_map/ppermute | solution.py:256
  64.7 5.0 %collective-permute-done.14.two_ref = f32[4,8,128]{2,1,0:T(8,128)S(1)} collective-permute-done((f32[4,8,128]{2,1,0:T(8,128)S(1)}, f32[4,8,128]{2,1,0:T(8,128)S(1)}, u32[]{:S(2)}, u32[]{:S(2)}) %collective-permute-start.14) | collective-permute-done | bytes 16416 | tf_op jit(solution)/shard_map/ppermute | solution.py:256
  69.7 0.8 %shard_map.83 = f32[16,16,16]{2,1,0:T(8,128)} custom-call(f32[4,8,128]{2,1,0:T(8,128)S(1)} %get-tuple-element.35.own_ref, f32[4,8,128]{2,1,0:T(8,128)S(1)} %collective-permute-done.13.one_ref, f32[4,8,128]{2,1,0:T(8,128)S(1)} %collective-permute-done.14.two_ref, f32[4,8,128]{2,1,0:T(8,128)S(1)} %collective-permute-done.15.three_ref), custom_call_target="tpu_custom_call" | custom-call | tf_op jit(solution)/shard_map/pallas_call | solution.py:15
  (30 shorter events, 0.3 us)
Async XLA Ops:
  0.6 1.0 %copy-start = (f32[2,16,16,128]{3,2,1,0:T(8,128)S(1)}, f32[2,16,16,128]{3,2,1,0:T(8,128)}, u32[]{:S(2)}) copy-start(f32[2,16,16,128]{3,2,1,0:T(8,128)} %orb_ref.5) | copy-start | bytes 786436
  1.6 0.9 %copy-start.2 = (f32[16,16,128]{2,1,0:T(8,128)S(1)}, f32[16,16,128]{2,1,0:T(8,128)}, u32[]{:S(2)}) copy-start(f32[16,16,128]{2,1,0:T(8,128)} %pert_ref.1) | copy-start | bytes 393220
  2.5 0.9 %copy-start.5 = (f32[16,16,128]{2,1,0:T(8,128)S(1)}, f32[16,16,128]{2,1,0:T(8,128)}, u32[]{:S(2)}) copy-start(f32[16,16,128]{2,1,0:T(8,128)} %pot_hbm.1) | copy-start | bytes 393220
  3.8 4.7 %collective-permute-start = (f32[3,4,16,128]{3,2,1,0:T(8,128)S(1)}, f32[3,4,16,128]{3,2,1,0:T(8,128)S(1)}, u32[]{:S(2)}, u32[]{:S(2)}) collective-permute-start(f32[3,4,16,128]{3,2,1,0:T(8,128)S(1)} %get-tuple-element.18), channel_id=1, source_target_pairs={{0,8},{8,16},{16,24},{24,0},{1,9},{9,17},{17,25},{25,1},{2,10},{10... | collective-permute-start | bytes 294920 | tf_op jit(solution)/shard_map/ppermute | solution.py:237
  6.1 5.8 %collective-permute-start.1 = (f32[3,4,16,128]{3,2,1,0:T(8,128)S(1)}, f32[3,4,16,128]{3,2,1,0:T(8,128)S(1)}, u32[]{:S(2)}, u32[]{:S(2)}) collective-permute-start(f32[3,4,16,128]{3,2,1,0:T(8,128)S(1)} %get-tuple-element.19), channel_id=1, source_target_pairs={{0,24},{8,0},{16,8},{24,16},{1,25},{9,1},{17,9},{25,17},{2,26},{10... | collective-permute-start | bytes 294920 | tf_op jit(solution)/shard_map/ppermute | solution.py:237
  11.9 7.9 %copy-start.1 = (f32[2,16,16,128]{3,2,1,0:T(8,128)S(1)}, f32[2,16,16,128]{3,2,1,0:T(8,128)}, u32[]{:S(2)}) copy-start(f32[2,16,16,128]{3,2,1,0:T(8,128)} %orb_ref.5) | copy-start | bytes 786436
  12.0 7.3 %collective-permute-start.2 = (f32[3,12,8,128]{3,2,1,0:T(8,128)S(1)}, f32[3,12,8,128]{3,2,1,0:T(8,128)S(1)}, u32[]{:S(2)}, u32[]{:S(2)}) collective-permute-start(f32[3,12,8,128]{3,2,1,0:T(8,128)S(1)} %get-tuple-element.20), channel_id=1, source_target_pairs={{0,7},{1,2},{2,1},{3,4},{4,3},{5,6},{6,5},{7,0},{8,15},{9,10},{10,... | collective-permute-start | bytes 442376 | tf_op jit(solution)/shard_map/ppermute | solution.py:245
  14.7 5.1 %collective-permute-start.3 = (f32[3,12,8,128]{3,2,1,0:T(8,128)S(1)}, f32[3,12,8,128]{3,2,1,0:T(8,128)S(1)}, u32[]{:S(2)}, u32[]{:S(2)}) collective-permute-start(f32[3,12,8,128]{3,2,1,0:T(8,128)S(1)} %get-tuple-element.21), channel_id=1, source_target_pairs={{0,1},{1,0},{2,3},{3,2},{4,5},{5,4},{6,7},{7,6},{8,9},{9,8},{10,11... | collective-permute-start | bytes 442376 | tf_op jit(solution)/shard_map/ppermute | solution.py:246
  14.7 5.1 %copy-start.6 = (f32[2]{0:T(128)S(1)}, f32[2]{0:T(128)}, u32[]{:S(2)}) copy-start(f32[2]{0:T(128)} %occ_ref.3) | copy-start | bytes 28
  14.7 5.1 %copy-start.7 = (f32[2]{0:T(128)S(1)}, f32[2]{0:T(128)}, u32[]{:S(2)}) copy-start(f32[2]{0:T(128)} %shift_ref.1) | copy-start | bytes 28
  21.7 1.3 %collective-permute-start.4 = (f32[8,16,128]{2,1,0:T(8,128)S(1)}, f32[8,16,128]{2,1,0:T(8,128)S(1)}, u32[]{:S(2)}, u32[]{:S(2)}) collective-permute-start(f32[8,16,128]{2,1,0:T(8,128)S(1)} %constant_dynamic-slice_fusion), channel_id=1, source_target_pairs={{0,32},{32,0},{64,96},{96,64},{128,160},{160,128},{192,224},{224,1... | collective-permute-start | bytes 196616 | tf_op jit(solution)/shard_map/ppermute | solution.py:256
  23.0 6.7 %collective-permute-start.5 = (f32[8,16,128]{2,1,0:T(8,128)S(1)}, f32[8,16,128]{2,1,0:T(8,128)S(1)}, u32[]{:S(2)}, u32[]{:S(2)}) collective-permute-start(f32[8,16,128]{2,1,0:T(8,128)S(1)} %dynamic-slice_add_fusion), channel_id=1, source_target_pairs={{0,64},{32,96},{64,0},{96,32},{128,192},{160,224},{192,128},{224,1... | collective-permute-start | bytes 196616 | tf_op jit(solution)/shard_map/ppermute | solution.py:256
  29.8 7.9 %copy-start.4 = (f32[16,16,128]{2,1,0:T(8,128)S(1)}, f32[16,16,128]{2,1,0:T(8,128)}, u32[]{:S(2)}) copy-start(f32[16,16,128]{2,1,0:T(8,128)} %kern_ref.1) | copy-start | bytes 393220
  29.8 7.9 %copy-start.3 = (f32[16,16,128]{2,1,0:T(8,128)S(1)}, f32[16,16,128]{2,1,0:T(8,128)}, u32[]{:S(2)}) copy-start(f32[16,16,128]{2,1,0:T(8,128)} %pert_ref.1) | copy-start | bytes 393220
  29.8 6.5 %collective-permute-start.6 = (f32[8,16,128]{2,1,0:T(8,128)S(1)}, f32[8,16,128]{2,1,0:T(8,128)S(1)}, u32[]{:S(2)}, u32[]{:S(2)}) collective-permute-start(f32[8,16,128]{2,1,0:T(8,128)S(1)} %add.52), channel_id=1, source_target_pairs={{0,192},{32,224},{64,128},{96,160},{128,64},{160,96},{192,0},{224,... | collective-permute-start | bytes 196616 | tf_op jit(solution)/shard_map/ppermute | solution.py:256
  36.3 1.3 %collective-permute-start.7 = (f32[8,16,128]{2,1,0:T(8,128)S(1)}, f32[8,16,128]{2,1,0:T(8,128)S(1)}, u32[]{:S(2)}, u32[]{:S(2)}) collective-permute-start(f32[8,16,128]{2,1,0:T(8,128)S(1)} %add.53.own_ref), channel_id=1, source_target_pairs={{0,32},{32,0},{64,96},{96,64},{128,160},{160,128},{192,224},{224,1... | collective-permute-start | bytes 196616 | tf_op jit(solution)/shard_map/ppermute | solution.py:256
  37.8 5.6 %collective-permute-start.8 = (f32[4,4,16,128]{3,2,1,0:T(8,128)S(1)}, f32[4,4,16,128]{3,2,1,0:T(8,128)S(1)}, u32[]{:S(2)}, u32[]{:S(2)}) collective-permute-start(f32[4,4,16,128]{3,2,1,0:T(8,128)S(1)} %get-tuple-element.25), channel_id=1, source_target_pairs={{0,8},{8,16},{16,24},{24,0},{1,9},{9,17},{17,25},{25,1},{2,10},{10... | collective-permute-start | bytes 393224 | tf_op jit(solution)/shard_map/ppermute | solution.py:237
  38.1 6.6 %collective-permute-start.9 = (f32[4,4,16,128]{3,2,1,0:T(8,128)S(1)}, f32[4,4,16,128]{3,2,1,0:T(8,128)S(1)}, u32[]{:S(2)}, u32[]{:S(2)}) collective-permute-start(f32[4,4,16,128]{3,2,1,0:T(8,128)S(1)} %get-tuple-element.26), channel_id=1, source_target_pairs={{0,24},{8,0},{16,8},{24,16},{1,25},{9,1},{17,9},{25,17},{2,26},{10... | collective-permute-start | bytes 393224 | tf_op jit(solution)/shard_map/ppermute | solution.py:237
  44.7 8.1 %collective-permute-start.10 = (f32[4,12,8,128]{3,2,1,0:T(8,128)S(1)}, f32[4,12,8,128]{3,2,1,0:T(8,128)S(1)}, u32[]{:S(2)}, u32[]{:S(2)}) collective-permute-start(f32[4,12,8,128]{3,2,1,0:T(8,128)S(1)} %get-tuple-element.27), channel_id=1, source_target_pairs={{0,7},{1,2},{2,1},{3,4},{4,3},{5,6},{6,5},{7,0},{8,15},{9,10},{10,... | collective-permute-start | bytes 589832 | tf_op jit(solution)/shard_map/ppermute | solution.py:245
  48.3 5.7 %collective-permute-start.11 = (f32[4,12,8,128]{3,2,1,0:T(8,128)S(1)}, f32[4,12,8,128]{3,2,1,0:T(8,128)S(1)}, u32[]{:S(2)}, u32[]{:S(2)}) collective-permute-start(f32[4,12,8,128]{3,2,1,0:T(8,128)S(1)} %get-tuple-element.28), channel_id=1, source_target_pairs={{0,1},{1,0},{2,3},{3,2},{4,5},{5,4},{6,7},{7,6},{8,9},{9,8},{10,11... | collective-permute-start | bytes 589832 | tf_op jit(solution)/shard_map/ppermute | solution.py:246
  56.8 1.3 %collective-permute-start.12 = (f32[4,4,8,128]{3,2,1,0:T(8,128)S(1)}, f32[4,4,8,128]{3,2,1,0:T(8,128)S(1)}, u32[]{:S(2)}, u32[]{:S(2)}) collective-permute-start(f32[4,4,8,128]{3,2,1,0:T(8,128)S(1)} %dynamic-slice_bitcast_fusion), channel_id=1, source_target_pairs={{0,32},{32,0},{64,96},{96,64},{128,160},{160,128},{192,224},{224,1... | collective-permute-start | bytes 196616 | tf_op jit(solution)/shard_map/ppermute | solution.py:256
  58.1 6.6 %collective-permute-start.15 = (f32[4,8,128]{2,1,0:T(8,128)S(1)}, f32[4,8,128]{2,1,0:T(8,128)S(1)}, u32[]{:S(2)}, u32[]{:S(2)}) collective-permute-start(f32[4,8,128]{2,1,0:T(8,128)S(1)} %get-tuple-element.32), channel_id=1, source_target_pairs={{0,192},{32,224},{64,128},{96,160},{128,64},{160,96},{192,0},{224,... | collective-permute-start | bytes 49160 | tf_op jit(solution)/shard_map/ppermute | solution.py:256
  62.0 7.6 %collective-permute-start.14 = (f32[4,8,128]{2,1,0:T(8,128)S(1)}, f32[4,8,128]{2,1,0:T(8,128)S(1)}, u32[]{:S(2)}, u32[]{:S(2)}) collective-permute-start(f32[4,8,128]{2,1,0:T(8,128)S(1)} %get-tuple-element.33), channel_id=1, source_target_pairs={{0,128},{32,160},{64,192},{96,224},{128,0},{160,32},{192,64},{224,... | collective-permute-start | bytes 49160 | tf_op jit(solution)/shard_map/ppermute | solution.py:256
  63.9 5.8 %collective-permute-start.13 = (f32[4,8,128]{2,1,0:T(8,128)S(1)}, f32[4,8,128]{2,1,0:T(8,128)S(1)}, u32[]{:S(2)}, u32[]{:S(2)}) collective-permute-start(f32[4,8,128]{2,1,0:T(8,128)S(1)} %get-tuple-element.34), channel_id=1, source_target_pairs={{0,64},{32,96},{64,0},{96,32},{128,192},{160,224},{192,128},{224,1... | collective-permute-start | bytes 49160 | tf_op jit(solution)/shard_map/ppermute | solution.py:256

commit v3 on v2

v3 whole, which is shorter than its diff:
```python
import jax
import jax.numpy as jnp
from jax import lax
from jax.experimental import pallas as pl
from jax.experimental.pallas import tpu as pltpu
from jax.sharding import PartitionSpec as P

RELAX = 0.8
VMEM = pl.BlockSpec(memory_space=pltpu.VMEM)
SMEM = pl.BlockSpec(memory_space=pltpu.SMEM)
HBM = pl.BlockSpec(memory_space=pltpu.HBM)

Y_ROWS = 35
Z_TILES = 130


def call(body, outs, *args, scratch=(), smem=0, where=VMEM, limit=16 * 2**20):
    return pl.pallas_call(
        body,
        out_shape=outs,
        in_specs=[where] * (len(args) - smem) + [SMEM] * smem,
        out_specs=jax.tree.map(lambda _: VMEM, outs),
        scratch_shapes=list(scratch),
        compiler_params=pltpu.CompilerParams(vmem_limit_bytes=limit),
    )(*args)


def f32(*shape):
    return jax.ShapeDtypeStruct(shape, jnp.float32)


def scratch32(*shape):
    return pltpu.VMEM(shape, jnp.float32)


def low_half():
    return lax.broadcasted_iota(jnp.int32, (8, 128), 0) < 4


def strip_row(kind, o, tail_of, y):
    base, width = {"product": (8 * o, 8), "potential": (16, 7), "orbital": (23 + 4 * o, 4), "kernel": (31, 4)}[kind]
    return base + (y + width if tail_of else y - 16)


def border_rows():
    for o in range(2):
        for i in range(8):
            yield "product", o, i, 8 + i
    for i in range(7):
        yield "potential", 0, i, 9 + i
    for o in range(2):
        for i in range(4):
            yield "orbital", o, i, 12 + i
    for i in range(4):
        yield "kernel", 0, i, 12 + i


def own_row(refs, kind, o, y):
    orb_ref, pert_ref, pot_ref, kern_ref = refs
    if kind == "product":
        return pert_ref[y] * orb_ref[o, y]
    if kind == "potential":
        return pot_ref[y]
    return orb_ref[o, y] if kind == "orbital" else kern_ref[y]


def strips_kernel(orb_hbm, pert_hbm, pot_hbm, kern_hbm, place_ref, near_ref, far_ref, orb_ref, pert_ref, pot_ref, kern_ref, sems):
    refs = (orb_ref, pert_ref, pot_ref, kern_ref)
    copies = [
        pltpu.make_async_copy(src, dest, sems.at[i])
        for i, (src, dest) in enumerate(zip((orb_hbm, pert_hbm, pot_hbm, kern_hbm), refs))
    ]
    for copy in copies:
        copy.start()
    for copy in copies:
        copy.wait()
    even = place_ref[0] == 0
    for at, (kind, o, head_y, tail_y) in enumerate(border_rows()):
        head, tail = own_row(refs, kind, o, head_y), own_row(refs, kind, o, tail_y)
        near_ref[at] = jnp.where(even, tail, head)
        far_ref[at] = jnp.where(even, head, tail)


def row_reader(refs, near_ref, far_ref, place_ref):
    even = place_ref[0] == 0

    def row(kind, o, y):
        if y < 0:
            at = strip_row(kind, o, True, y)
            return jnp.where(even, far_ref[at], near_ref[at])
        if y >= 16:
            at = strip_row(kind, o, False, y)
            return jnp.where(even, near_ref[at], far_ref[at])
        return own_row(refs, kind, o, y)

    return row


def wide_fields():
    return ("product", 0, 0, -8), ("product", 1, 32, -8), ("potential", 0, 64, -7)


def narrow_fields():
    return ("orbital", 0, 94), ("orbital", 1, 106), ("kernel", 0, 118)


def pack_kernel(orb_ref, pert_ref, pot_ref, kern_ref, ynear_ref, yfar_ref, place_ref, far_ref, near_ref):
    row = row_reader((orb_ref, pert_ref, pot_ref, kern_ref), ynear_ref, yfar_ref, place_ref)
    even, low = place_ref[1] == 0, low_half()

    def put(at, head, tail):
        near_ref[at] = jnp.where(even, tail, head)
        far_ref[at] = jnp.where(even, head, tail)

    for kind, o, at, first in wide_fields():
        for y in range(first, 16 - first):
            cells = row(kind, o, y)
            put(at + y - first, cells[:8], cells[8:])
    for kind, o, at in narrow_fields():
        for j in range(12):
            a, b = row(kind, o, j - 4), row(kind, o, j + 8)
            head = jnp.where(low, a[:8], pltpu.roll(b[:8], 4, 0))
            tail = jnp.where(low, pltpu.roll(b[8:], 4, 0), a[8:])
            put(at + j, head, tail)


def shifts_z(u):
    return pltpu.roll(u, 1, u.ndim - 2) + pltpu.roll(u, u.shape[-2] - 1, u.ndim - 2)


def shifts_x(u):
    return pltpu.roll(u, 1, u.ndim - 1) + pltpu.roll(u, 127, u.ndim - 1)


def by_rows(first, last, load, emit):
    before, at = load(first - 1), load(first)
    for r in range(first, last):
        after = load(r + 1)
        emit(r, before, at, after)
        before, at = at, after


def sources(p_ref, scale_ref, sc_ref, o):
    def load(r):
        return p_ref[o, r]

    def emit(r, before, at, after):
        faces = shifts_x(at) + shifts_z(at) + (before + after)
        sc_ref[o, r] = scale_ref[o, r] * (-30.0 * at - 5.0 * faces)

    by_rows(1, p_ref.shape[1] - 1, load, emit)


def sweep(src_ref, scale_ref, sc_ref, o, margin, store):
    def load(r):
        u = src_ref[o, r]
        return u, shifts_z(u)

    def emit(r, before, at, after):
        u, along_z = at
        across = before[1] + after[1]
        m = before[0] + after[0] + along_z
        n = 3.0 * m + across
        total = shifts_x(14.0 * u + n) + (3.0 * n + 5.0 * m)
        store(r, 0.2 * u + sc_ref[o, r] + scale_ref[o, r] * total)

    by_rows(margin, src_ref.shape[1] - margin, load, emit)


def into(dest_ref, o):
    def store(r, new):
        dest_ref[o, r] = new

    return store


def first_kernel(
    orb_ref, pert_ref, pot_ref, kern_ref, ynear_ref, yfar_ref, zfar_ref, znear_ref, shift_ref, occ_ref, place_ref,
    resp_ref, dens_ref, scale_ref, prod_ref, orbs_ref, kerns_ref, p_ref, s_ref, sc_ref, a_ref, b_ref, pot_scr,
):
    row = row_reader((orb_ref, pert_ref, pot_ref, kern_ref), ynear_ref, yfar_ref, place_ref)
    even, low = place_ref[1] == 0, low_half()

    def sides(at):
        near, far = znear_ref[at], zfar_ref[at]
        return jnp.where(even, near, far), jnp.where(even, far, near)

    for kind, o, at, first in wide_fields():
        dest = pot_scr if kind == "potential" else p_ref.at[o]
        for y in range(first, 16 - first):
            above, below = sides(at + y - first)
            dest[y + 8, 0:16] = row(kind, o, y)
            dest[y + 8, 16:24] = above
            dest[y + 8, 24:32] = below
    for kind, o, at in narrow_fields():
        dest = kerns_ref if kind == "kernel" else orbs_ref.at[o]
        for r in range(24):
            dest[r, 0:16] = row(kind, o, r - 4)
        for j in range(12):
            above, below = sides(at + j)
            dest[j, 16:24] = jnp.where(low, above, below)
            dest[j + 12, 16:24] = pltpu.roll(jnp.where(low, below, above), 4, 0)

    def narrow(dest, r, cells):
        dest[r, 0:16] = cells[:16]
        dest[r, 16:24] = jnp.where(low, cells[16:24], cells[24:32])

    for o in range(2):
        base = 32.0 / 15.0 + shift_ref[o]
        for r in range(1, 31):
            scale = (RELAX / 60.0) / (base + pot_scr[r])
            s_ref[o, r] = scale
            if 4 <= r < 28:
                narrow(scale_ref.at[o], r - 4, scale)
                narrow(prod_ref.at[o], r - 4, p_ref[o, r])
        sources(p_ref, s_ref, sc_ref, o)
        sweep(sc_ref, s_ref, sc_ref, o, 2, into(a_ref, o))
        sweep(a_ref, s_ref, sc_ref, o, 3, into(b_ref, o))
        occupation = occ_ref[o]

        def store(r, new):
            narrow(resp_ref.at[o], r - 4, new)
            term = occupation * orbs_ref[o, r - 4] * resp_ref[o, r - 4]
            dens_ref[r - 4] = term if o == 0 else dens_ref[r - 4] + term

        sweep(b_ref, s_ref, sc_ref, o, 4, store)


def swap_blocks(rows):
    block = lax.broadcasted_iota(jnp.int32, rows[0].shape, rows[0].ndim - 1) // 16
    for d in (1, 2, 4):
        keep = (block // d) % 2 == 0
        out = list(rows)
        for k in range(8):
            if k & d == 0:
                a, b = rows[k], rows[k + d]
                out[k] = jnp.where(keep, a, pltpu.roll(b, 16 * d, 1))
                out[k + d] = jnp.where(keep, pltpu.roll(a, 128 - 16 * d, 1), b)
        rows = out
    return rows


def second_kernel(
    own_ref, other_ref, resp_in_ref, scale_ref, prod_ref, orbs_ref, kerns_ref, occ_ref, place_ref,
    resp_ref, out_ref, p_ref, sc_ref, a_ref, b_ref, dens_ref,
):
    first_core = place_ref[2] == 0
    for r in range(24):
        mine, theirs = own_ref[r % 12], other_ref[r % 12]
        total = jnp.where(first_core, mine, theirs) if r < 12 else jnp.where(first_core, theirs, mine)
        raised = kerns_ref[r] * total
        for o in range(2):
            p_ref[o, r] = prod_ref[o, r] + raised * orbs_ref[o, r]
    for o in range(2):
        sources(p_ref, scale_ref, sc_ref, o)
        sweep(resp_in_ref, scale_ref, sc_ref, o, 1, into(a_ref, o))
        sweep(a_ref, scale_ref, sc_ref, o, 2, into(b_ref, o))
        sweep(b_ref, scale_ref, sc_ref, o, 3, into(a_ref, o))
        occupation = occ_ref[o]

        def store(r, new):
            own = new[:16]
            resp_ref[o, r - 4] = own
            term = occupation * orbs_ref[o, r, 0:16] * own
            dens_ref[r - 4] = term if o == 0 else dens_ref[r - 4] + term

        sweep(a_ref, scale_ref, sc_ref, o, 4, store)
    for part in range(4):
        y, z = part // 2, 8 * (part % 2)
        blocks = swap_blocks([dens_ref[2 * k + y, z : z + 8] for k in range(8)])
        for b in range(8):
            out_ref[b, part] = blocks[b]


def final_kernel(own_ref, one_ref, two_ref, three_ref, dens_ref):
    for part in range(4):
        y, z = part // 2, 8 * (part % 2)
        total = (own_ref[part] + one_ref[part]) + (two_ref[part] + three_ref[part])
        for k in range(8):
            moved = total if k == 0 else pltpu.roll(total, 128 - 16 * k, 1)
            dens_ref[2 * k + y, z : z + 8, :] = moved[:, :16]


def exchange(near, far, axis):
    count = lax.axis_size(axis)
    far = lax.ppermute(far, axis, [(i, (i - 1) % count if i % 2 == 0 else (i + 1) % count) for i in range(count)])
    near = lax.ppermute(near, axis, [(i, i ^ 1) for i in range(count)])
    return near, far


def partner(value, *steps):
    count = lax.axis_size("bands")
    return lax.ppermute(value, "bands", [(i, i ^ steps[i % len(steps)]) for i in range(count)])


def on_device(orbitals, orbital_shift, occupation, potential, perturbation, kernel):
    group = lax.axis_index("bands")
    core, chip = group % 2, group // 2
    place = jnp.stack([lax.axis_index("gy") % 2, lax.axis_index("gz") % 2, core]).astype(jnp.int32)
    arrays = (orbitals, perturbation, potential, kernel)

    strip = f32(Y_ROWS, 16, 128)
    near, far = call(
        strips_kernel, (strip, strip), *arrays, place, smem=1, where=HBM, limit=None,
        scratch=[scratch32(2, 16, 16, 128)] + [scratch32(16, 16, 128)] * 3 + [pltpu.SemaphoreType.DMA((4,))],
    )
    ynear, yfar = exchange(near, far, "gy")
    strip = f32(Z_TILES, 8, 128)
    far, near = call(pack_kernel, (strip, strip), *arrays, ynear, yfar, place, smem=1)
    znear, zfar = exchange(near, far, "gz")
    pair, single = f32(2, 24, 24, 128), f32(24, 24, 128)
    response, partial, scale, products, orbs, kernels = call(
        first_kernel, (pair, single, pair, pair, pair, single),
        *arrays, ynear, yfar, zfar, znear, orbital_shift, occupation, place,
        scratch=[scratch32(2, 32, 32, 128)] * 5 + [scratch32(32, 32, 128)], smem=3,
    )

    own = lax.dynamic_slice_in_dim(partial, 12 * core, 12, 0)
    own = own + partner(lax.dynamic_slice_in_dim(partial, 12 * (1 - core), 12, 0), 1)
    own = own + partner(own, 2, 6)
    own = own + partner(own, 6, 2)
    other = partner(own, 1)
    response, blocks = call(
        second_kernel, (f32(2, 16, 16, 128), f32(8, 4, 8, 128)),
        own, other, response, scale, products, orbs, kernels, occupation, place,
        scratch=[scratch32(2, 24, 24, 128)] * 4 + [scratch32(16, 16, 128)], smem=2,
    )

    blocks = blocks.reshape(4, 2, 4, 8, 128)
    kept = lax.dynamic_index_in_dim(blocks, core, 1, keepdims=False)
    kept = kept + partner(lax.dynamic_index_in_dim(blocks, 1 - core, 1, keepdims=False), 1)

    def block_of(step):
        return lax.dynamic_index_in_dim(kept, chip ^ step, 0, keepdims=False)

    two, one, three = (partner(block_of(step), 2 * step) for step in (2, 1, 3))
    density = call(final_kernel, f32(16, 16, 16), block_of(0), one, two, three)
    return response, density


def solution(mesh):
    placed = (
        P("bands", "gy", "gz", None),
        P("bands"),
        P("bands"),
        P("gy", "gz", None),
        P("gy", "gz", None),
        P("gy", "gz", None),
    )
    return jax.shard_map(
        on_device,
        mesh=mesh,
        in_specs=placed,
        out_specs=(P("bands", "gy", "gz", None), P("gy", "gz", "bands")),
        check_vma=False,
    )
```

time: 70.6 us -> 76.1 us (1.078)
  Pallas kernels: 5.97 us -> 10.3 us
  starting transfers between devices: 24.8 us -> 21.7 us
  other arithmetic: 0.04 us -> 1.62 us
  waiting for transfers between devices: 36 us -> 37.2 us
    pallas_call x7 -> x5, Pallas kernels: 5.97 us -> 10.3 us  [call(): pl.pallas_call(body, out_shape=outs, in_specs=[where] * (len(args) - smem...]
    ppermute x16 -> x12, starting transfers between devices: 24.8 us -> 21.7 us  [the longest x8 14.8 us: partner(): lax.ppermute(value, 'bands', [(i, i ^ steps[i % len(steps)]) for i in ran...]
    ppermute x16 -> x12, waiting for transfers between devices: 36 us -> 37.2 us  [the longest x8 16.6 us: partner(): lax.ppermute(value, 'bands', [(i, i ^ steps[i % len(steps)]) for i in ran...]
    add x3, other arithmetic: 0.03 us -> 0.96 us  [the longest x1 0.93 us: on_device(): own + partner(lax.dynamic_slice_in_dim(partial, 12 * (1 - core), 12, 0), 1)]
    unnamed x16 -> x28, local copies, waits for them, and re-layouts: 2.77 us -> 3.53 us
  transfers between devices with their start and end apart: 16 -> 12, of which waited for: 14 -> 11; matrix products, arithmetic and copies ran while one was open for 0% -> 0% of each run, Pallas kernels for 0% -> 0%
where the time goes in v3:
time: 76.1 us; the launch traced here: 75.2 us
  waiting for transfers between devices  37.2 us (49%)
  starting transfers between devices  21.7 us (29%)
  Pallas kernels  10.3 us (14%)
  local copies, waits for them, and re-layouts  3.56 us (5%)
  other arithmetic  1.62 us (2%)
  between operations  0.81 us (1%)
    ppermute x8, waiting for transfers between devices, partner(): lax.ppermute(value, 'bands', [(i, i ^ steps[i % len(steps)]) for i in ran...  16.6 us
    ppermute x8, starting transfers between devices, partner(): lax.ppermute(value, 'bands', [(i, i ^ steps[i % len(steps)]) for i in ran...  14.8 us
    ppermute x2, waiting for transfers between devices, exchange(): lax.ppermute(far, axis, [(i, (i - 1) % count if i % 2 == 0 else (i + 1) %...  12.7 us
    pallas_call x5, Pallas kernels, call(): pl.pallas_call(body, out_shape=outs, in_specs=[where] * (len(args) - smem...  10.3 us
    ppermute x2, waiting for transfers between devices, exchange(): near = lax.ppermute(near, axis, [(i, i ^ 1) for i in range(count)])  7.93 us
    ppermute x2, starting transfers between devices, exchange(): lax.ppermute(far, axis, [(i, (i - 1) % count if i % 2 == 0 else (i + 1) %...  5.94 us
    unnamed x28, local copies, waits for them, and re-layouts  3.53 us
  transfers between devices with their start and end apart: 12, of which 11 were waited for; matrix products, arithmetic and copies ran while one was open for 0% of the time, Pallas kernels for 0%

profile of v3, /device:TPU:6, one launch (start us, length us, event | category | flops | bytes accessed | tf_op | source)
XLA Modules:
  0.0 75.2 jit_solution(12125959107520857096)
XLA Ops:
  0.7 0.7 pad_add_fusion.place_ref
  1.3 2.8 %shard_map.77 = (f32[35,16,128]{2,1,0:T(8,128)}, f32[35,16,128]{2,1,0:T(8,128)}) custom-call(f32[2,16,16,128]{3,2,1,0:T(8,128)} %orb_ref.3, f32[16,16,128]{2,1,0:T(8,128)} %pert_ref.3, f32[16,16,128]{2,1,0:T(8,128)} %pot_ref.3, f32[16,16,128]{2,1,0:T(8,128)} %kern_ref.3, s32[3]{0:T(128)} %pad_add_fusion.place_ref), custom_call_target="tpu_custom_call" | custom-call | tf_op jit(solution)/shard_map/pallas_call | solution.py:18
  4.1 0.9 %collective-permute-start = (f32[35,16,128]{2,1,0:T(8,128)}, f32[35,16,128]{2,1,0:T(8,128)S(1)}, u32[]{:S(2)}, u32[]{:S(2)}) collective-permute-start(f32[35,16,128]{2,1,0:T(8,128)} %get-tuple-element.14), channel_id=1, source_target_pairs={{0,8},{8,0},{16,24},{24,16},{1,9},{9,1},{17,25},{25,17},{2,10},{10... | collective-permute-start | bytes 860168 | tf_op jit(solution)/shard_map/ppermute | solution.py:287
  5.1 1.5 %collective-permute-start.1 = (f32[35,16,128]{2,1,0:T(8,128)}, f32[35,16,128]{2,1,0:T(8,128)S(1)}, u32[]{:S(2)}, u32[]{:S(2)}) collective-permute-start(f32[35,16,128]{2,1,0:T(8,128)} %get-tuple-element.15), channel_id=1, source_target_pairs={{0,24},{8,16},{16,8},{24,0},{1,25},{9,17},{17,9},{25,1},{2,26},{10... | collective-permute-start | bytes 860168 | tf_op jit(solution)/shard_map/ppermute | solution.py:286
  6.5 6.5 %collective-permute-done.ynear_ref = f32[35,16,128]{2,1,0:T(8,128)S(1)} collective-permute-done((f32[35,16,128]{2,1,0:T(8,128)}, f32[35,16,128]{2,1,0:T(8,128)S(1)}, u32[]{:S(2)}, u32[]{:S(2)}) %collective-permute-start) | collective-permute-done | bytes 286752 | tf_op jit(solution)/shard_map/ppermute | solution.py:287
  13.0 1.8 %collective-permute-done.1.yfar_ref = f32[35,16,128]{2,1,0:T(8,128)S(1)} collective-permute-done((f32[35,16,128]{2,1,0:T(8,128)}, f32[35,16,128]{2,1,0:T(8,128)S(1)}, u32[]{:S(2)}, u32[]{:S(2)}) %collective-permute-start.1) | collective-permute-done | bytes 286752 | tf_op jit(solution)/shard_map/ppermute | solution.py:286
  14.8 0.7 shard_map.78
  15.5 4.5 %collective-permute-start.2 = (f32[130,8,128]{2,1,0:T(8,128)S(1)}, f32[130,8,128]{2,1,0:T(8,128)S(1)}, u32[]{:S(2)}, u32[]{:S(2)}) collective-permute-start(f32[130,8,128]{2,1,0:T(8,128)S(1)} %get-tuple-element.16), channel_id=1, source_target_pairs={{0,7},{1,2},{2,1},{3,4},{4,3},{5,6},{6,5},{7,0},{8,15},{9,10},{10,... | collective-permute-start | bytes 1597448 | tf_op jit(solution)/shard_map/ppermute | solution.py:286
  19.9 10.9 %collective-permute-done.2.zfar_ref = f32[130,8,128]{2,1,0:T(8,128)S(1)} collective-permute-done((f32[130,8,128]{2,1,0:T(8,128)S(1)}, f32[130,8,128]{2,1,0:T(8,128)S(1)}, u32[]{:S(2)}, u32[]{:S(2)}) %collective-permute-start.2) | collective-permute-done | bytes 532512 | tf_op jit(solution)/shard_map/ppermute | solution.py:286
  30.8 1.5 %collective-permute-done.3.znear_ref = f32[130,8,128]{2,1,0:T(8,128)S(1)} collective-permute-done((f32[130,8,128]{2,1,0:T(8,128)S(1)}, f32[130,8,128]{2,1,0:T(8,128)S(1)}, u32[]{:S(2)}, u32[]{:S(2)}) %collective-permute-start.3) | collective-permute-done | bytes 532512 | tf_op jit(solution)/shard_map/ppermute | solution.py:287
  32.3 0.8 %copy-done.6 = f32[130,8,128]{2,1,0:T(8,128)} copy-done((f32[130,8,128]{2,1,0:T(8,128)}, f32[130,8,128]{2,1,0:T(8,128)S(1)}, u32[]{:S(2)}) %copy-start.6) | copy-done | bytes 532504
  33.1 1.0 %copy-done.7 = f32[130,8,128]{2,1,0:T(8,128)S(1)} copy-done((f32[130,8,128]{2,1,0:T(8,128)S(1)}, f32[130,8,128]{2,1,0:T(8,128)}, u32[]{:S(2)}) %copy-start.7) | copy-done | bytes 532504
  34.2 3.2 %shard_map.79 = (f32[2,24,24,128]{3,2,1,0:T(8,128)S(1)}, f32[24,24,128]{2,1,0:T(8,128)S(1)}, f32[2,24,24,128]{3,2,1,0:T(8,128)S(1)}, f32[2,24,24,128]{3,2,1,0:T(...) custom-call(f32[2,16,16,128]{3,2,1,0:T(8,128)S(1)} %copy-done, f32[16,16,128]{2,1,0:T(8,128)S(1)} %copy-done.1, ...), custom_call_target="tpu_custom_call" | custom-call | tf_op jit(solution)/shard_map/pallas_call | solution.py:18
  37.3 0.8 %copy-done.4 = f32[2,24,24,128]{3,2,1,0:T(8,128)} copy-done((f32[2,24,24,128]{3,2,1,0:T(8,128)}, f32[2,24,24,128]{3,2,1,0:T(8,128)S(1)}, u32[]{:S(2)}) %copy-start.4) | copy-done | bytes 589848
  38.1 0.7 copy-done.8
  39.0 1.3 %collective-permute-done.4 = f32[12,24,128]{2,1,0:T(8,128)S(1)} collective-permute-done((f32[12,24,128]{2,1,0:T(8,128)S(1)}, f32[12,24,128]{2,1,0:T(8,128)S(1)}, u32[]{:S(2)}, u32[]{:S(2)}) %collective-permute-start.4) | collective-permute-done | bytes 147488 | tf_op jit(solution)/shard_map/ppermute | solution.py:293
  40.3 0.9 %dynamic-slice_add_fusion = f32[12,24,128]{2,1,0:T(8,128)S(1)} fusion(f32[12,24,128]{2,1,0:T(8,128)S(1)} %collective-permute-done.4, f32[24,24,128]{2,1,0:T(8,128)} %copy-done.8, s32[]{:T(128)S(6)} %select_n.48), kind=kLoop, calls=%fused_computation | loop fusion | flops 36864 | bytes 442372 | tf_op jit(solution)/shard_map/add | solution.py:319
  41.3 3.4 %collective-permute-start.5 = (f32[12,24,128]{2,1,0:T(8,128)S(1)}, f32[12,24,128]{2,1,0:T(8,128)S(1)}, u32[]{:S(2)}, u32[]{:S(2)}) collective-permute-start(f32[12,24,128]{2,1,0:T(8,128)S(1)} %dynamic-slice_add_fusion), channel_id=1, source_target_pairs={{0,64},{32,224},{64,0},{96,160},{128,192},{160,96},{192,128},{224,... | collective-permute-start | bytes 442376 | tf_op jit(solution)/shard_map/ppermute | solution.py:293
  44.6 4.3 %collective-permute-done.5 = f32[12,24,128]{2,1,0:T(8,128)S(1)} collective-permute-done((f32[12,24,128]{2,1,0:T(8,128)S(1)}, f32[12,24,128]{2,1,0:T(8,128)S(1)}, u32[]{:S(2)}, u32[]{:S(2)}) %collective-permute-start.5) | collective-permute-done | bytes 147488 | tf_op jit(solution)/shard_map/ppermute | solution.py:293
  49.0 4.6 %collective-permute-start.6 = (f32[12,24,128]{2,1,0:T(8,128)S(1)}, f32[12,24,128]{2,1,0:T(8,128)S(1)}, u32[]{:S(2)}, u32[]{:S(2)}) collective-permute-start(f32[12,24,128]{2,1,0:T(8,128)S(1)} %add.56), channel_id=1, source_target_pairs={{0,192},{32,96},{64,128},{96,32},{128,64},{160,224},{192,0},{224,1... | collective-permute-start | bytes 442376 | tf_op jit(solution)/shard_map/ppermute | solution.py:293
  53.6 4.7 %collective-permute-done.6 = f32[12,24,128]{2,1,0:T(8,128)S(1)} collective-permute-done((f32[12,24,128]{2,1,0:T(8,128)S(1)}, f32[12,24,128]{2,1,0:T(8,128)S(1)}, u32[]{:S(2)}, u32[]{:S(2)}) %collective-permute-start.6) | collective-permute-done | bytes 147488 | tf_op jit(solution)/shard_map/ppermute | solution.py:293
  58.3 0.1 collective-permute-start.7
  58.4 1.3 %collective-permute-done.7.other_ref = f32[12,24,128]{2,1,0:T(8,128)S(1)} collective-permute-done((f32[12,24,128]{2,1,0:T(8,128)S(1)}, f32[12,24,128]{2,1,0:T(8,128)S(1)}, u32[]{:S(2)}, u32[]{:S(2)}) %collective-permute-start.7) | collective-permute-done | bytes 147488 | tf_op jit(solution)/shard_map/ppermute | solution.py:293
  59.8 2.9 %shard_map.80 = (f32[2,16,16,128]{3,2,1,0:T(8,128)}, f32[8,4,8,128]{3,2,1,0:T(8,128)S(1)}) custom-call(f32[12,24,128]{2,1,0:T(8,128)S(1)} %add.57.own_ref, f32[12,24,128]{2,1,0:T(8,128)S(1)} %collective-permute-done.7.other_ref, f32[2,24,24,128]{3,2,1,0:T(8,128)S(1)} %get-tuple-element.19.resp_in_ref, f32[2,24,24,128]{3,2,1,0:T(8,128)S(1)} %get-tuple-element.20.scale_ref, ...), custom_call_target="tpu_custom_call" | custom-call | tf_op jit(solution)/shard_map/pallas_call | solution.py:18
  62.7 0.1 collective-permute-start.8
  62.9 1.1 %collective-permute-done.8 = f32[4,4,8,128]{3,2,1,0:T(8,128)S(1)} collective-permute-done((f32[4,4,8,128]{3,2,1,0:T(8,128)S(1)}, f32[4,4,8,128]{3,2,1,0:T(8,128)S(1)}, u32[]{:S(2)}, u32[]{:S(2)}) %collective-permute-start.8) | collective-permute-done | bytes 65568 | tf_op jit(solution)/shard_map/ppermute | solution.py:293
  64.0 4.6 %collective-permute-start.10 = (f32[4,8,128]{2,1,0:T(8,128)S(1)}, f32[4,8,128]{2,1,0:T(8,128)S(1)}, u32[]{:S(2)}, u32[]{:S(2)}) collective-permute-start(f32[4,8,128]{2,1,0:T(8,128)S(1)} %get-tuple-element.27), channel_id=1, source_target_pairs={{0,128},{32,160},{64,192},{96,224},{128,0},{160,32},{192,64},{224,... | collective-permute-start | bytes 49160 | tf_op jit(solution)/shard_map/ppermute | solution.py:293
  68.6 0.4 collective-permute-start.11
  69.0 1.6 %collective-permute-start.9 = (f32[4,8,128]{2,1,0:T(8,128)S(1)}, f32[4,8,128]{2,1,0:T(8,128)S(1)}, u32[]{:S(2)}, u32[]{:S(2)}) collective-permute-start(f32[4,8,128]{2,1,0:T(8,128)S(1)} %get-tuple-element.28), channel_id=1, source_target_pairs={{0,64},{32,96},{64,0},{96,32},{128,192},{160,224},{192,128},{224,1... | collective-permute-start | bytes 49160 | tf_op jit(solution)/shard_map/ppermute | solution.py:293
  70.6 1.1 %collective-permute-done.10.two_ref = f32[4,8,128]{2,1,0:T(8,128)S(1)} collective-permute-done((f32[4,8,128]{2,1,0:T(8,128)S(1)}, f32[4,8,128]{2,1,0:T(8,128)S(1)}, u32[]{:S(2)}, u32[]{:S(2)}) %collective-permute-start.10) | collective-permute-done | bytes 16416 | tf_op jit(solution)/shard_map/ppermute | solution.py:293
  71.7 2.7 %collective-permute-done.11.three_ref = f32[4,8,128]{2,1,0:T(8,128)S(1)} collective-permute-done((f32[4,8,128]{2,1,0:T(8,128)S(1)}, f32[4,8,128]{2,1,0:T(8,128)S(1)}, u32[]{:S(2)}, u32[]{:S(2)}) %collective-permute-start.11) | collective-permute-done | bytes 16416 | tf_op jit(solution)/shard_map/ppermute | solution.py:293
  74.4 0.8 %shard_map.81 = f32[16,16,16]{2,1,0:T(8,128)} custom-call(f32[4,8,128]{2,1,0:T(8,128)S(1)} %get-tuple-element.29.own_ref, f32[4,8,128]{2,1,0:T(8,128)S(1)} %collective-permute-done.9.one_ref, f32[4,8,128]{2,1,0:T(8,128)S(1)} %collective-permute-done.10.two_ref, f32[4,8,128]{2,1,0:T(8,128)S(1)} %collective-permute-done.11.three_ref), custom_call_target="tpu_custom_call" | custom-call | tf_op jit(solution)/shard_map/pallas_call | solution.py:18
  (33 shorter events, 0.2 us)
Async XLA Ops:
  1.3 13.5 %copy-start = (f32[2,16,16,128]{3,2,1,0:T(8,128)S(1)}, f32[2,16,16,128]{3,2,1,0:T(8,128)}, u32[]{:S(2)}) copy-start(f32[2,16,16,128]{3,2,1,0:T(8,128)} %orb_ref.3) | copy-start | bytes 786436
  1.3 13.5 %copy-start.1 = (f32[16,16,128]{2,1,0:T(8,128)S(1)}, f32[16,16,128]{2,1,0:T(8,128)}, u32[]{:S(2)}) copy-start(f32[16,16,128]{2,1,0:T(8,128)} %pert_ref.3) | copy-start | bytes 393220
  1.3 13.5 %copy-start.2 = (f32[16,16,128]{2,1,0:T(8,128)S(1)}, f32[16,16,128]{2,1,0:T(8,128)}, u32[]{:S(2)}) copy-start(f32[16,16,128]{2,1,0:T(8,128)} %pot_ref.3) | copy-start | bytes 393220
  1.3 13.5 %copy-start.3 = (f32[16,16,128]{2,1,0:T(8,128)S(1)}, f32[16,16,128]{2,1,0:T(8,128)}, u32[]{:S(2)}) copy-start(f32[16,16,128]{2,1,0:T(8,128)} %kern_ref.3) | copy-start | bytes 393220
  4.1 10.7 %copy-start.11 = (s32[3]{0:T(128)S(1)}, s32[3]{0:T(128)}, u32[]{:S(2)}) copy-start(s32[3]{0:T(128)} %pad_add_fusion.place_ref) | copy-start | bytes 40
  4.1 8.9 %collective-permute-start = (f32[35,16,128]{2,1,0:T(8,128)}, f32[35,16,128]{2,1,0:T(8,128)S(1)}, u32[]{:S(2)}, u32[]{:S(2)}) collective-permute-start(f32[35,16,128]{2,1,0:T(8,128)} %get-tuple-element.14), channel_id=1, source_target_pairs={{0,8},{8,0},{16,24},{24,16},{1,9},{9,1},{17,25},{25,17},{2,10},{10... | collective-permute-start | bytes 860168 | tf_op jit(solution)/shard_map/ppermute | solution.py:287
  5.1 9.7 %collective-permute-start.1 = (f32[35,16,128]{2,1,0:T(8,128)}, f32[35,16,128]{2,1,0:T(8,128)S(1)}, u32[]{:S(2)}, u32[]{:S(2)}) collective-permute-start(f32[35,16,128]{2,1,0:T(8,128)} %get-tuple-element.15), channel_id=1, source_target_pairs={{0,24},{8,16},{16,8},{24,0},{1,25},{9,17},{17,9},{25,1},{2,26},{10... | collective-permute-start | bytes 860168 | tf_op jit(solution)/shard_map/ppermute | solution.py:286
  15.5 15.4 %collective-permute-start.2 = (f32[130,8,128]{2,1,0:T(8,128)S(1)}, f32[130,8,128]{2,1,0:T(8,128)S(1)}, u32[]{:S(2)}, u32[]{:S(2)}) collective-permute-start(f32[130,8,128]{2,1,0:T(8,128)S(1)} %get-tuple-element.16), channel_id=1, source_target_pairs={{0,7},{1,2},{2,1},{3,4},{4,3},{5,6},{6,5},{7,0},{8,15},{9,10},{10,... | collective-permute-start | bytes 1597448 | tf_op jit(solution)/shard_map/ppermute | solution.py:286
  19.9 12.4 %collective-permute-start.3 = (f32[130,8,128]{2,1,0:T(8,128)S(1)}, f32[130,8,128]{2,1,0:T(8,128)S(1)}, u32[]{:S(2)}, u32[]{:S(2)}) collective-permute-start(f32[130,8,128]{2,1,0:T(8,128)S(1)} %get-tuple-element.17), channel_id=1, source_target_pairs={{0,1},{1,0},{2,3},{3,2},{4,5},{5,4},{6,7},{7,6},{8,9},{9,8},{10,11... | collective-permute-start | bytes 1597448 | tf_op jit(solution)/shard_map/ppermute | solution.py:287
  19.9 13.2 %copy-start.12 = (f32[2]{0:T(128)S(1)}, f32[2]{0:T(128)}, u32[]{:S(2)}) copy-start(f32[2]{0:T(128)} %occ_ref.3) | copy-start | bytes 28
  19.9 13.2 %copy-start.13 = (f32[2]{0:T(128)S(1)}, f32[2]{0:T(128)}, u32[]{:S(2)}) copy-start(f32[2]{0:T(128)} %shift_ref.1) | copy-start | bytes 28
  32.3 0.8 %copy-start.6 = (f32[130,8,128]{2,1,0:T(8,128)}, f32[130,8,128]{2,1,0:T(8,128)S(1)}, u32[]{:S(2)}) copy-start(f32[130,8,128]{2,1,0:T(8,128)S(1)} %collective-permute-done.3.znear_ref) | copy-start | bytes 1597444
  33.1 1.0 %copy-start.7 = (f32[130,8,128]{2,1,0:T(8,128)S(1)}, f32[130,8,128]{2,1,0:T(8,128)}, u32[]{:S(2)}) copy-start(f32[130,8,128]{2,1,0:T(8,128)} %copy-done.6) | copy-start | bytes 1597444
  37.3 0.8 %copy-start.4 = (f32[2,24,24,128]{3,2,1,0:T(8,128)}, f32[2,24,24,128]{3,2,1,0:T(8,128)S(1)}, u32[]{:S(2)}) copy-start(f32[2,24,24,128]{3,2,1,0:T(8,128)S(1)} %get-tuple-element.22.orbs_ref) | copy-start | bytes 1769476
  38.1 0.7 copy-start.8
  38.1 0.8 %copy-start.9 = (f32[24,24,128]{2,1,0:T(8,128)}, f32[24,24,128]{2,1,0:T(8,128)S(1)}, u32[]{:S(2)}) copy-start(f32[24,24,128]{2,1,0:T(8,128)S(1)} %get-tuple-element.23.kerns_ref) | copy-start | bytes 884740
  39.0 1.4 %collective-permute-start.4 = (f32[12,24,128]{2,1,0:T(8,128)S(1)}, f32[12,24,128]{2,1,0:T(8,128)S(1)}, u32[]{:S(2)}, u32[]{:S(2)}) collective-permute-start(f32[12,24,128]{2,1,0:T(8,128)S(1)} %constant_dynamic-slice_fusion), channel_id=1, source_target_pairs={{0,32},{32,0},{64,96},{96,64},{128,160},{160,128},{192,224},{224,1... | collective-permute-start | bytes 442376 | tf_op jit(solution)/shard_map/ppermute | solution.py:293
  39.0 20.8 %copy-start.5 = (f32[2,24,24,128]{3,2,1,0:T(8,128)S(1)}, f32[2,24,24,128]{3,2,1,0:T(8,128)}, u32[]{:S(2)}) copy-start(f32[2,24,24,128]{3,2,1,0:T(8,128)} %copy-done.4) | copy-start | bytes 1769476
  41.3 7.6 %collective-permute-start.5 = (f32[12,24,128]{2,1,0:T(8,128)S(1)}, f32[12,24,128]{2,1,0:T(8,128)S(1)}, u32[]{:S(2)}, u32[]{:S(2)}) collective-permute-start(f32[12,24,128]{2,1,0:T(8,128)S(1)} %dynamic-slice_add_fusion), channel_id=1, source_target_pairs={{0,64},{32,224},{64,0},{96,160},{128,192},{160,96},{192,128},{224,... | collective-permute-start | bytes 442376 | tf_op jit(solution)/shard_map/ppermute | solution.py:293
  48.9 10.8 %copy-start.10 = (f32[24,24,128]{2,1,0:T(8,128)S(1)}, f32[24,24,128]{2,1,0:T(8,128)}, u32[]{:S(2)}) copy-start(f32[24,24,128]{2,1,0:T(8,128)} %copy-done.9) | copy-start | bytes 884740
  49.0 9.3 %collective-permute-start.6 = (f32[12,24,128]{2,1,0:T(8,128)S(1)}, f32[12,24,128]{2,1,0:T(8,128)S(1)}, u32[]{:S(2)}, u32[]{:S(2)}) collective-permute-start(f32[12,24,128]{2,1,0:T(8,128)S(1)} %add.56), channel_id=1, source_target_pairs={{0,192},{32,96},{64,128},{96,32},{128,64},{160,224},{192,0},{224,1... | collective-permute-start | bytes 442376 | tf_op jit(solution)/shard_map/ppermute | solution.py:293
  58.3 1.5 %collective-permute-start.7 = (f32[12,24,128]{2,1,0:T(8,128)S(1)}, f32[12,24,128]{2,1,0:T(8,128)S(1)}, u32[]{:S(2)}, u32[]{:S(2)}) collective-permute-start(f32[12,24,128]{2,1,0:T(8,128)S(1)} %add.57.own_ref), channel_id=1, source_target_pairs={{0,32},{32,0},{64,96},{96,64},{128,160},{160,128},{192,224},{224,1... | collective-permute-start | bytes 442376 | tf_op jit(solution)/shard_map/ppermute | solution.py:293
  62.7 1.3 %collective-permute-start.8 = (f32[4,4,8,128]{3,2,1,0:T(8,128)S(1)}, f32[4,4,8,128]{3,2,1,0:T(8,128)S(1)}, u32[]{:S(2)}, u32[]{:S(2)}) collective-permute-start(f32[4,4,8,128]{3,2,1,0:T(8,128)S(1)} %dynamic-slice_bitcast_fusion), channel_id=1, source_target_pairs={{0,32},{32,0},{64,96},{96,64},{128,160},{160,128},{192,224},{224,1... | collective-permute-start | bytes 196616 | tf_op jit(solution)/shard_map/ppermute | solution.py:293
  64.0 7.7 %collective-permute-start.10 = (f32[4,8,128]{2,1,0:T(8,128)S(1)}, f32[4,8,128]{2,1,0:T(8,128)S(1)}, u32[]{:S(2)}, u32[]{:S(2)}) collective-permute-start(f32[4,8,128]{2,1,0:T(8,128)S(1)} %get-tuple-element.27), channel_id=1, source_target_pairs={{0,128},{32,160},{64,192},{96,224},{128,0},{160,32},{192,64},{224,... | collective-permute-start | bytes 49160 | tf_op jit(solution)/shard_map/ppermute | solution.py:293
  68.6 5.8 %collective-permute-start.11 = (f32[4,8,128]{2,1,0:T(8,128)S(1)}, f32[4,8,128]{2,1,0:T(8,128)S(1)}, u32[]{:S(2)}, u32[]{:S(2)}) collective-permute-start(f32[4,8,128]{2,1,0:T(8,128)S(1)} %get-tuple-element.26), channel_id=1, source_target_pairs={{0,192},{32,224},{64,128},{96,160},{128,64},{160,96},{192,0},{224,... | collective-permute-start | bytes 49160 | tf_op jit(solution)/shard_map/ppermute | solution.py:293
  69.0 5.4 %collective-permute-start.9 = (f32[4,8,128]{2,1,0:T(8,128)S(1)}, f32[4,8,128]{2,1,0:T(8,128)S(1)}, u32[]{:S(2)}, u32[]{:S(2)}) collective-permute-start(f32[4,8,128]{2,1,0:T(8,128)S(1)} %get-tuple-element.28), channel_id=1, source_target_pairs={{0,64},{32,96},{64,0},{96,32},{128,192},{160,224},{192,128},{224,1... | collective-permute-start | bytes 49160 | tf_op jit(solution)/shard_map/ppermute | solution.py:293

commit v4 on v2

--- a/solution.py
+++ b/solution.py
@@ -11,11 +11,11 @@
 SMEM = pl.BlockSpec(memory_space=pltpu.SMEM)
 
 
-def call(body, outs, *args, scratch=(), smem=0, where=VMEM):
+def call(body, outs, *args, scratch=(), smem=0):
     return pl.pallas_call(
         body,
         out_shape=outs,
-        in_specs=[where] * (len(args) - smem) + [SMEM] * smem,
+        in_specs=[VMEM] * (len(args) - smem) + [SMEM] * smem,
         out_specs=jax.tree.map(lambda _: VMEM, outs),
         scratch_shapes=list(scratch),
         compiler_params=pltpu.CompilerParams(vmem_limit_bytes=48 * 2**20),
@@ -148,23 +148,6 @@
         sweep(sc_ref, scale_ref, sc_ref, o, 2, into(a_ref, o))
         sweep(a_ref, scale_ref, sc_ref, o, 3, into(b_ref, o))
         last_sweep(b_ref, scale_ref, sc_ref, o, orb_ref, occ_ref, resp_ref, dens_ref)
-
-
-def product_kernel(orb_hbm, pert_hbm, pot_hbm, centre_ref, up_ref, down_ref, orb_ref, pert_ref, pot_ref, sems):
-    pairs = ((orb_hbm, orb_ref), (pert_hbm, pert_ref), (pot_hbm, pot_ref))
-    copies = [pltpu.make_async_copy(src, dest, sems.at[i]) for i, (src, dest) in enumerate(pairs)]
-    for copy in copies:
-        copy.start()
-    for copy in copies:
-        copy.wait()
-    for y in range(16):
-        for field in range(3):
-            value = pot_ref[y] if field == 2 else pert_ref[y] * orb_ref[field, y]
-            centre_ref[field, y] = value
-            if y < 4:
-                down_ref[field, y] = value
-            if y >= 12:
-                up_ref[field, y - 12] = value
 
 
 def change_kernel(own_ref, other_ref, pert_ref, kern_ref, orb_ref, resp_ref, core_ref, centre_ref, up_ref, down_ref):
@@ -251,9 +234,9 @@
     return [(i, (i - 1) % count if i % 2 == 0 else (i + 1) % count) for i in range(count)]
 
 
-def partner(value, step):
+def partner(value, *steps):
     count = lax.axis_size("bands")
-    return lax.ppermute(value, "bands", [(i, i ^ step) for i in range(count)])
+    return lax.ppermute(value, "bands", [(i, i ^ steps[i % len(steps)]) for i in range(count)])
 
 
 def on_device(orbitals, orbital_shift, occupation, potential, perturbation, kernel):
@@ -263,12 +246,14 @@
     wide = pltpu.VMEM((2, 24, 24, 128), jnp.float32)
 
     odd = (lax.axis_index("gz") % 2)[None].astype(jnp.int32)
-    centre, up, down = call(
-        product_kernel, (f32(3, 16, 16, 128), f32(3, 4, 16, 128), f32(3, 4, 16, 128)),
-        orbitals, perturbation, potential, where=pl.BlockSpec(memory_space=pltpu.HBM),
-        scratch=[pltpu.VMEM(shape, jnp.float32) for shape in ((2, 16, 16, 128), (16, 16, 128), (16, 16, 128))]
-        + [pltpu.SemaphoreType.DMA((3,))],
-    )
+    def ends(field):
+        return field[12:16], field[0:4]
+
+    edges = lax.optimization_barrier([ends(field) for field in (perturbation, potential, orbitals[0], orbitals[1])])
+    up, down = (
+        jnp.stack([edges[0][i] * edges[2][i], edges[0][i] * edges[3][i], edges[1][i]]) for i in range(2)
+    )
+    centre = jnp.concatenate([perturbation[None] * orbitals, potential[None]], 0)
     lo, hi = exchange_y(up, down)
     near, far = exchange_z(centre, lo, hi, odd)
     response, partial, scale = call(
@@ -279,8 +264,8 @@
 
     own = lax.dynamic_slice_in_dim(partial, 8 * core, 8, 0)
     own = own + partner(lax.dynamic_slice_in_dim(partial, 8 * (1 - core), 8, 0), 1)
-    own = own + partner(own, 2)
-    own = own + partner(own, 6)
+    own = own + partner(own, 2, 6)
+    own = own + partner(own, 6, 2)
     other = partner(own, 1)
     centre, up, down = call(
         change_kernel, (f32(4, 16, 16, 128), f32(4, 4, 16, 128), f32(4, 4, 16, 128)),

time: 70.6 us -> 70.5 us (level)
  starting transfers between devices: 24.8 us -> 29.7 us
  waiting for transfers between devices: 36 us -> 33.2 us
  local copies, waits for them, and re-layouts: 2.81 us -> 1.08 us
    ppermute x2, starting transfers between devices: 2.65 us -> 5.9 us  [exchange_y(): lax.ppermute(up, 'gy', ring('gy', 1))]
    ppermute x2, waiting for transfers between devices: 5.93 us -> 3.08 us  [exchange_y(): lax.ppermute(up, 'gy', ring('gy', 1))]
    unnamed x16 -> x12, local copies, waits for them, and re-layouts: 2.77 us -> 0.17 us
    ppermute x2, starting transfers between devices: 6.25 us -> 7.75 us  [exchange_z(): far = lax.ppermute(far, 'gz', far_pairs(count))]
    ppermute x2, waiting for transfers between devices: 9.2 us -> 7.82 us  [exchange_z(): far = lax.ppermute(far, 'gz', far_pairs(count))]
    ppermute x2, waiting for transfers between devices: 1.6 us -> 2.98 us  [exchange_z(): near = lax.ppermute(near, 'gz', [(i, i ^ 1) for i in range(count)])]
    ppermute x2, waiting for transfers between devices: 4.73 us -> 5.82 us  [exchange_y(): lax.ppermute(down, 'gy', ring('gy', -1))]
    ppermute x8, waiting for transfers between devices: 14.5 us -> 13.5 us  [partner(): lax.ppermute(value, 'bands', [(i, i ^ steps[i % len(steps)]) for i in ran...]
  transfers between devices with their start and end apart: 16 -> 16, of which waited for: 14 -> 13; matrix products, arithmetic and copies ran while one was open for 0% -> 0% of each run, Pallas kernels for 0% -> 0%
where the time goes in v4:
time: 70.5 us; the launch traced here: 70.4 us
  waiting for transfers between devices  33.2 us (47%)
  starting transfers between devices  29.7 us (42%)
  Pallas kernels  5.55 us (8%)
  local copies, waits for them, and re-layouts  1.08 us (2%)
  between operations  0.86 us (1%)
    ppermute x8, starting transfers between devices, partner(): lax.ppermute(value, 'bands', [(i, i ^ steps[i % len(steps)]) for i in ran...  15.1 us
    ppermute x8, waiting for transfers between devices, partner(): lax.ppermute(value, 'bands', [(i, i ^ steps[i % len(steps)]) for i in ran...  13.5 us
    ppermute x2, waiting for transfers between devices, exchange_z(): far = lax.ppermute(far, 'gz', far_pairs(count))  7.82 us
    ppermute x2, starting transfers between devices, exchange_z(): far = lax.ppermute(far, 'gz', far_pairs(count))  7.75 us
    ppermute x2, starting transfers between devices, exchange_y(): lax.ppermute(up, 'gy', ring('gy', 1))  5.9 us
    ppermute x2, waiting for transfers between devices, exchange_y(): lax.ppermute(down, 'gy', ring('gy', -1))  5.82 us
    pallas_call x6, Pallas kernels, call(): pl.pallas_call(body, out_shape=outs, in_specs=[VMEM] * (len(args) - smem)...  5.55 us
    ppermute x2, waiting for transfers between devices, exchange_y(): lax.ppermute(up, 'gy', ring('gy', 1))  3.08 us
  transfers between devices with their start and end apart: 16, of which 13 were waited for; matrix products, arithmetic and copies ran while one was open for 0% of the time, Pallas kernels for 0%

profile of v4, /device:TPU:6, one launch (start us, length us, event | category | flops | bytes accessed | tf_op | source)
XLA Modules:
  0.0 70.4 jit_solution(10209033170244095487)
XLA Ops:
  0.6 0.9 %slice_bitcast_fusion = (f32[4,16,128]{2,1,0:T(8,128)S(1)}, f32[4,16,128]{2,1,0:T(8,128)S(1)}, f32[4,16,128]{2,1,0:T(8,128)S(1)}, f32[4,16,128]{2,1,0:T(8,128)S(1)}) fusion(f32[2,16,16,128]{3,2,1,0:T(8,128)} %orb_ref.5), kind=kLoop, calls=%fused_computation.11 | loop fusion | bytes 262144 | tf_op jit(solution)/shard_map/slice | solution.py:250
  1.5 0.0 copy-done.1
  1.5 0.1 copy-done.5
  1.7 0.9 %collective-permute-start.1 = (f32[3,4,16,128]{3,2,1,0:T(8,128)S(1)}, f32[3,4,16,128]{3,2,1,0:T(8,128)S(1)}, u32[]{:S(2)}, u32[]{:S(2)}) collective-permute-start(f32[3,4,16,128]{3,2,1,0:T(8,128)S(1)} %pad_maximum_fusion.2), channel_id=1, source_target_pairs={{0,24},{8,0},{16,8},{24,16},{1,25},{9,1},{17,9},{25,17},{2,26},{10... | collective-permute-start | bytes 294920 | tf_op jit(solution)/shard_map/ppermute | solution.py:220
  2.7 2.5 %collective-permute-start = (f32[3,4,16,128]{3,2,1,0:T(8,128)S(1)}, f32[3,4,16,128]{3,2,1,0:T(8,128)S(1)}, u32[]{:S(2)}, u32[]{:S(2)}) collective-permute-start(f32[3,4,16,128]{3,2,1,0:T(8,128)S(1)} %pad_maximum_fusion.1), channel_id=1, source_target_pairs={{0,8},{8,16},{16,24},{24,0},{1,9},{9,17},{17,25},{25,1},{2,10},{10... | collective-permute-start | bytes 294920 | tf_op jit(solution)/shard_map/ppermute | solution.py:220
  5.2 2.4 %collective-permute-done.1.hi_ref = f32[3,4,16,128]{3,2,1,0:T(8,128)S(1)} collective-permute-done((f32[3,4,16,128]{3,2,1,0:T(8,128)S(1)}, f32[3,4,16,128]{3,2,1,0:T(8,128)S(1)}, u32[]{:S(2)}, u32[]{:S(2)}) %collective-permute-start.1) | collective-permute-done | bytes 98336 | tf_op jit(solution)/shard_map/ppermute | solution.py:220
  7.7 4.5 %collective-permute-start.2 = (f32[3,12,8,128]{3,2,1,0:T(8,128)S(1)}, f32[3,12,8,128]{3,2,1,0:T(8,128)S(1)}, u32[]{:S(2)}, u32[]{:S(2)}) collective-permute-start(f32[3,12,8,128]{3,2,1,0:T(8,128)S(1)} %get-tuple-element.30), channel_id=1, source_target_pairs={{0,7},{1,2},{2,1},{3,4},{4,3},{5,6},{6,5},{7,0},{8,15},{9,10},{10,... | collective-permute-start | bytes 442376 | tf_op jit(solution)/shard_map/ppermute | solution.py:228
  12.1 3.1 %collective-permute-done.2.far_ref = f32[3,12,8,128]{3,2,1,0:T(8,128)S(1)} collective-permute-done((f32[3,12,8,128]{3,2,1,0:T(8,128)S(1)}, f32[3,12,8,128]{3,2,1,0:T(8,128)S(1)}, u32[]{:S(2)}, u32[]{:S(2)}) %collective-permute-start.2) | collective-permute-done | bytes 147488 | tf_op jit(solution)/shard_map/ppermute | solution.py:228
  15.2 2.0 %collective-permute-done.3.near_ref = f32[3,12,8,128]{3,2,1,0:T(8,128)S(1)} collective-permute-done((f32[3,12,8,128]{3,2,1,0:T(8,128)S(1)}, f32[3,12,8,128]{3,2,1,0:T(8,128)S(1)}, u32[]{:S(2)}, u32[]{:S(2)}) %collective-permute-start.3) | collective-permute-done | bytes 147488 | tf_op jit(solution)/shard_map/ppermute | solution.py:229
  17.3 1.8 %shard_map.78 = (f32[2,16,16,128]{3,2,1,0:T(8,128)S(1)}, f32[16,16,128]{2,1,0:T(8,128)S(1)}, f32[2,24,24,128]{3,2,1,0:T(8,128)S(1)}) custom-call(f32[3,16,16,128]{3,2,1,0:T(8,128)S(1)} %pad_maximum_fusion.centre_ref, f32[3,4,16,128]{3,2,1,0:T(8,128)S(1)} %collective-permute-done.lo_ref, f32[3,4,16,128]{3,2,1,0:T(8,128)S(1)} %collective-permute-done.1.hi_ref, ...), custom_call_target="tpu_custom_call" | custom-call | tf_op jit(solution)/shard_map/pallas_call | solution.py:15
  19.1 0.1 collective-permute-start.4
  19.2 1.2 %collective-permute-done.4 = f32[8,16,128]{2,1,0:T(8,128)S(1)} collective-permute-done((f32[8,16,128]{2,1,0:T(8,128)S(1)}, f32[8,16,128]{2,1,0:T(8,128)S(1)}, u32[]{:S(2)}, u32[]{:S(2)}) %collective-permute-start.4) | collective-permute-done | bytes 65568 | tf_op jit(solution)/shard_map/ppermute | solution.py:239
  20.5 3.4 %collective-permute-start.5 = (f32[8,16,128]{2,1,0:T(8,128)S(1)}, f32[8,16,128]{2,1,0:T(8,128)S(1)}, u32[]{:S(2)}, u32[]{:S(2)}) collective-permute-start(f32[8,16,128]{2,1,0:T(8,128)S(1)} %dynamic-slice_add_fusion), channel_id=1, source_target_pairs={{0,64},{32,224},{64,0},{96,160},{128,192},{160,96},{192,128},{224,... | collective-permute-start | bytes 196616 | tf_op jit(solution)/shard_map/ppermute | solution.py:239
  23.8 2.5 %collective-permute-done.5 = f32[8,16,128]{2,1,0:T(8,128)S(1)} collective-permute-done((f32[8,16,128]{2,1,0:T(8,128)S(1)}, f32[8,16,128]{2,1,0:T(8,128)S(1)}, u32[]{:S(2)}, u32[]{:S(2)}) %collective-permute-start.5) | collective-permute-done | bytes 65568 | tf_op jit(solution)/shard_map/ppermute | solution.py:239
  26.3 5.0 %collective-permute-start.6 = (f32[8,16,128]{2,1,0:T(8,128)S(1)}, f32[8,16,128]{2,1,0:T(8,128)S(1)}, u32[]{:S(2)}, u32[]{:S(2)}) collective-permute-start(f32[8,16,128]{2,1,0:T(8,128)S(1)} %add.52), channel_id=1, source_target_pairs={{0,192},{32,96},{64,128},{96,32},{128,64},{160,224},{192,0},{224,1... | collective-permute-start | bytes 196616 | tf_op jit(solution)/shard_map/ppermute | solution.py:239
  31.3 2.3 %collective-permute-done.6 = f32[8,16,128]{2,1,0:T(8,128)S(1)} collective-permute-done((f32[8,16,128]{2,1,0:T(8,128)S(1)}, f32[8,16,128]{2,1,0:T(8,128)S(1)}, u32[]{:S(2)}, u32[]{:S(2)}) %collective-permute-start.6) | collective-permute-done | bytes 65568 | tf_op jit(solution)/shard_map/ppermute | solution.py:239
  33.6 0.1 collective-permute-start.7
  33.7 1.2 %collective-permute-done.7.other_ref = f32[8,16,128]{2,1,0:T(8,128)S(1)} collective-permute-done((f32[8,16,128]{2,1,0:T(8,128)S(1)}, f32[8,16,128]{2,1,0:T(8,128)S(1)}, u32[]{:S(2)}, u32[]{:S(2)}) %collective-permute-start.7) | collective-permute-done | bytes 65568 | tf_op jit(solution)/shard_map/ppermute | solution.py:239
  35.0 0.1 shard_map.79
  35.0 3.4 %collective-permute-start.8 = (f32[4,4,16,128]{3,2,1,0:T(8,128)S(1)}, f32[4,4,16,128]{3,2,1,0:T(8,128)S(1)}, u32[]{:S(2)}, u32[]{:S(2)}) collective-permute-start(f32[4,4,16,128]{3,2,1,0:T(8,128)S(1)} %get-tuple-element.35), channel_id=1, source_target_pairs={{0,8},{8,16},{16,24},{24,0},{1,9},{9,17},{17,25},{25,1},{2,10},{10... | collective-permute-start | bytes 393224 | tf_op jit(solution)/shard_map/ppermute | solution.py:220
  38.5 3.1 %collective-permute-done.8.lo_ref = f32[4,4,16,128]{3,2,1,0:T(8,128)S(1)} collective-permute-done((f32[4,4,16,128]{3,2,1,0:T(8,128)S(1)}, f32[4,4,16,128]{3,2,1,0:T(8,128)S(1)}, u32[]{:S(2)}, u32[]{:S(2)}) %collective-permute-start.8) | collective-permute-done | bytes 131104 | tf_op jit(solution)/shard_map/ppermute | solution.py:220
  41.5 3.4 %collective-permute-done.9.hi_ref = f32[4,4,16,128]{3,2,1,0:T(8,128)S(1)} collective-permute-done((f32[4,4,16,128]{3,2,1,0:T(8,128)S(1)}, f32[4,4,16,128]{3,2,1,0:T(8,128)S(1)}, u32[]{:S(2)}, u32[]{:S(2)}) %collective-permute-start.9) | collective-permute-done | bytes 131104 | tf_op jit(solution)/shard_map/ppermute | solution.py:220
  45.0 3.3 %collective-permute-start.10 = (f32[4,12,8,128]{3,2,1,0:T(8,128)S(1)}, f32[4,12,8,128]{3,2,1,0:T(8,128)S(1)}, u32[]{:S(2)}, u32[]{:S(2)}) collective-permute-start(f32[4,12,8,128]{3,2,1,0:T(8,128)S(1)} %get-tuple-element.37), channel_id=1, source_target_pairs={{0,7},{1,2},{2,1},{3,4},{4,3},{5,6},{6,5},{7,0},{8,15},{9,10},{10,... | collective-permute-start | bytes 589832 | tf_op jit(solution)/shard_map/ppermute | solution.py:228
  48.3 4.7 %collective-permute-done.10.far_ref = f32[4,12,8,128]{3,2,1,0:T(8,128)S(1)} collective-permute-done((f32[4,12,8,128]{3,2,1,0:T(8,128)S(1)}, f32[4,12,8,128]{3,2,1,0:T(8,128)S(1)}, u32[]{:S(2)}, u32[]{:S(2)}) %collective-permute-start.10) | collective-permute-done | bytes 196640 | tf_op jit(solution)/shard_map/ppermute | solution.py:228
  53.0 1.0 %collective-permute-done.11.near_ref = f32[4,12,8,128]{3,2,1,0:T(8,128)S(1)} collective-permute-done((f32[4,12,8,128]{3,2,1,0:T(8,128)S(1)}, f32[4,12,8,128]{3,2,1,0:T(8,128)S(1)}, u32[]{:S(2)}, u32[]{:S(2)}) %collective-permute-start.11) | collective-permute-done | bytes 196640 | tf_op jit(solution)/shard_map/ppermute | solution.py:229
  54.0 2.9 %shard_map.81 = (f32[2,16,16,128]{3,2,1,0:T(8,128)}, f32[8,4,8,128]{3,2,1,0:T(8,128)S(1)}) custom-call(f32[4,16,16,128]{3,2,1,0:T(8,128)S(1)} %get-tuple-element.34.centre_ref, f32[4,4,16,128]{3,2,1,0:T(8,128)S(1)} %collective-permute-done.8.lo_ref, f32[4,4,16,128]{3,2,1,0:T(8,128)S(1)} %collective-permute-done.9.hi_ref, ...), custom_call_target="tpu_custom_call" | custom-call | tf_op jit(solution)/shard_map/pallas_call | solution.py:15
  56.9 1.2 %collective-permute-done.12 = f32[4,4,8,128]{3,2,1,0:T(8,128)S(1)} collective-permute-done((f32[4,4,8,128]{3,2,1,0:T(8,128)S(1)}, f32[4,4,8,128]{3,2,1,0:T(8,128)S(1)}, u32[]{:S(2)}, u32[]{:S(2)}) %collective-permute-start.12) | collective-permute-done | bytes 65568 | tf_op jit(solution)/shard_map/ppermute | solution.py:239
  58.1 3.7 %collective-permute-start.15 = (f32[4,8,128]{2,1,0:T(8,128)S(1)}, f32[4,8,128]{2,1,0:T(8,128)S(1)}, u32[]{:S(2)}, u32[]{:S(2)}) collective-permute-start(f32[4,8,128]{2,1,0:T(8,128)S(1)} %get-tuple-element.50), channel_id=1, source_target_pairs={{0,192},{32,224},{64,128},{96,160},{128,64},{160,96},{192,0},{224,... | collective-permute-start | bytes 49160 | tf_op jit(solution)/shard_map/ppermute | solution.py:239
  61.8 1.7 %collective-permute-start.14 = (f32[4,8,128]{2,1,0:T(8,128)S(1)}, f32[4,8,128]{2,1,0:T(8,128)S(1)}, u32[]{:S(2)}, u32[]{:S(2)}) collective-permute-start(f32[4,8,128]{2,1,0:T(8,128)S(1)} %get-tuple-element.51), channel_id=1, source_target_pairs={{0,128},{32,160},{64,192},{96,224},{128,0},{160,32},{192,64},{224,... | collective-permute-start | bytes 49160 | tf_op jit(solution)/shard_map/ppermute | solution.py:239
  63.5 1.2 %collective-permute-start.13 = (f32[4,8,128]{2,1,0:T(8,128)S(1)}, f32[4,8,128]{2,1,0:T(8,128)S(1)}, u32[]{:S(2)}, u32[]{:S(2)}) collective-permute-start(f32[4,8,128]{2,1,0:T(8,128)S(1)} %get-tuple-element.52), channel_id=1, source_target_pairs={{0,64},{32,96},{64,0},{96,32},{128,192},{160,224},{192,128},{224,1... | collective-permute-start | bytes 49160 | tf_op jit(solution)/shard_map/ppermute | solution.py:239
  64.7 5.0 %collective-permute-done.14.two_ref = f32[4,8,128]{2,1,0:T(8,128)S(1)} collective-permute-done((f32[4,8,128]{2,1,0:T(8,128)S(1)}, f32[4,8,128]{2,1,0:T(8,128)S(1)}, u32[]{:S(2)}, u32[]{:S(2)}) %collective-permute-start.14) | collective-permute-done | bytes 16416 | tf_op jit(solution)/shard_map/ppermute | solution.py:239
  69.7 0.8 %shard_map.82 = f32[16,16,16]{2,1,0:T(8,128)} custom-call(f32[4,8,128]{2,1,0:T(8,128)S(1)} %get-tuple-element.53.own_ref, f32[4,8,128]{2,1,0:T(8,128)S(1)} %collective-permute-done.13.one_ref, f32[4,8,128]{2,1,0:T(8,128)S(1)} %collective-permute-done.14.two_ref, f32[4,8,128]{2,1,0:T(8,128)S(1)} %collective-permute-done.15.three_ref), custom_call_target="tpu_custom_call" | custom-call | tf_op jit(solution)/shard_map/pallas_call | solution.py:15
  (33 shorter events, 0.3 us)
Async XLA Ops:
  0.6 0.9 %copy-start.1 = (f32[16,16,128]{2,1,0:T(8,128)S(1)}, f32[16,16,128]{2,1,0:T(8,128)}, u32[]{:S(2)}) copy-start(f32[16,16,128]{2,1,0:T(8,128)} %pert_ref.1) | copy-start | bytes 393220
  0.6 1.0 %copy-start.5 = (f32[16,16,128]{2,1,0:T(8,128)S(1)}, f32[16,16,128]{2,1,0:T(8,128)}, u32[]{:S(2)}) copy-start(f32[16,16,128]{2,1,0:T(8,128)} %param.9) | copy-start | bytes 393220
  1.7 3.5 %copy-start = (f32[2,16,16,128]{3,2,1,0:T(8,128)S(1)}, f32[2,16,16,128]{3,2,1,0:T(8,128)}, u32[]{:S(2)}) copy-start(f32[2,16,16,128]{3,2,1,0:T(8,128)} %orb_ref.5) | copy-start | bytes 786436
  1.7 5.9 %collective-permute-start.1 = (f32[3,4,16,128]{3,2,1,0:T(8,128)S(1)}, f32[3,4,16,128]{3,2,1,0:T(8,128)S(1)}, u32[]{:S(2)}, u32[]{:S(2)}) collective-permute-start(f32[3,4,16,128]{3,2,1,0:T(8,128)S(1)} %pad_maximum_fusion.2), channel_id=1, source_target_pairs={{0,24},{8,0},{16,8},{24,16},{1,25},{9,1},{17,9},{25,17},{2,26},{10... | collective-permute-start | bytes 294920 | tf_op jit(solution)/shard_map/ppermute | solution.py:220
  2.7 5.0 %collective-permute-start = (f32[3,4,16,128]{3,2,1,0:T(8,128)S(1)}, f32[3,4,16,128]{3,2,1,0:T(8,128)S(1)}, u32[]{:S(2)}, u32[]{:S(2)}) collective-permute-start(f32[3,4,16,128]{3,2,1,0:T(8,128)S(1)} %pad_maximum_fusion.1), channel_id=1, source_target_pairs={{0,8},{8,16},{16,24},{24,0},{1,9},{9,17},{17,25},{25,1},{2,10},{10... | collective-permute-start | bytes 294920 | tf_op jit(solution)/shard_map/ppermute | solution.py:220
  7.7 7.6 %collective-permute-start.2 = (f32[3,12,8,128]{3,2,1,0:T(8,128)S(1)}, f32[3,12,8,128]{3,2,1,0:T(8,128)S(1)}, u32[]{:S(2)}, u32[]{:S(2)}) collective-permute-start(f32[3,12,8,128]{3,2,1,0:T(8,128)S(1)} %get-tuple-element.30), channel_id=1, source_target_pairs={{0,7},{1,2},{2,1},{3,4},{4,3},{5,6},{6,5},{7,0},{8,15},{9,10},{10,... | collective-permute-start | bytes 442376 | tf_op jit(solution)/shard_map/ppermute | solution.py:228
  12.1 5.1 %collective-permute-start.3 = (f32[3,12,8,128]{3,2,1,0:T(8,128)S(1)}, f32[3,12,8,128]{3,2,1,0:T(8,128)S(1)}, u32[]{:S(2)}, u32[]{:S(2)}) collective-permute-start(f32[3,12,8,128]{3,2,1,0:T(8,128)S(1)} %get-tuple-element.31), channel_id=1, source_target_pairs={{0,1},{1,0},{2,3},{3,2},{4,5},{5,4},{6,7},{7,6},{8,9},{9,8},{10,11... | collective-permute-start | bytes 442376 | tf_op jit(solution)/shard_map/ppermute | solution.py:229
  12.1 5.1 %copy-start.3 = (f32[2]{0:T(128)S(1)}, f32[2]{0:T(128)}, u32[]{:S(2)}) copy-start(f32[2]{0:T(128)} %occ_ref.3) | copy-start | bytes 28
  12.1 5.1 %copy-start.4 = (f32[2]{0:T(128)S(1)}, f32[2]{0:T(128)}, u32[]{:S(2)}) copy-start(f32[2]{0:T(128)} %shift_ref.1) | copy-start | bytes 28
  19.1 1.3 %collective-permute-start.4 = (f32[8,16,128]{2,1,0:T(8,128)S(1)}, f32[8,16,128]{2,1,0:T(8,128)S(1)}, u32[]{:S(2)}, u32[]{:S(2)}) collective-permute-start(f32[8,16,128]{2,1,0:T(8,128)S(1)} %constant_dynamic-slice_fusion), channel_id=1, source_target_pairs={{0,32},{32,0},{64,96},{96,64},{128,160},{160,128},{192,224},{224,1... | collective-permute-start | bytes 196616 | tf_op jit(solution)/shard_map/ppermute | solution.py:239
  20.5 5.8 %collective-permute-start.5 = (f32[8,16,128]{2,1,0:T(8,128)S(1)}, f32[8,16,128]{2,1,0:T(8,128)S(1)}, u32[]{:S(2)}, u32[]{:S(2)}) collective-permute-start(f32[8,16,128]{2,1,0:T(8,128)S(1)} %dynamic-slice_add_fusion), channel_id=1, source_target_pairs={{0,64},{32,224},{64,0},{96,160},{128,192},{160,96},{192,128},{224,... | collective-permute-start | bytes 196616 | tf_op jit(solution)/shard_map/ppermute | solution.py:239
  26.3 8.7 %copy-start.2 = (f32[16,16,128]{2,1,0:T(8,128)S(1)}, f32[16,16,128]{2,1,0:T(8,128)}, u32[]{:S(2)}) copy-start(f32[16,16,128]{2,1,0:T(8,128)} %kern_ref.1) | copy-start | bytes 393220
  26.3 7.3 %collective-permute-start.6 = (f32[8,16,128]{2,1,0:T(8,128)S(1)}, f32[8,16,128]{2,1,0:T(8,128)S(1)}, u32[]{:S(2)}, u32[]{:S(2)}) collective-permute-start(f32[8,16,128]{2,1,0:T(8,128)S(1)} %add.52), channel_id=1, source_target_pairs={{0,192},{32,96},{64,128},{96,32},{128,64},{160,224},{192,0},{224,1... | collective-permute-start | bytes 196616 | tf_op jit(solution)/shard_map/ppermute | solution.py:239
  33.6 1.3 %collective-permute-start.7 = (f32[8,16,128]{2,1,0:T(8,128)S(1)}, f32[8,16,128]{2,1,0:T(8,128)S(1)}, u32[]{:S(2)}, u32[]{:S(2)}) collective-permute-start(f32[8,16,128]{2,1,0:T(8,128)S(1)} %add.53.own_ref), channel_id=1, source_target_pairs={{0,32},{32,0},{64,96},{96,64},{128,160},{160,128},{192,224},{224,1... | collective-permute-start | bytes 196616 | tf_op jit(solution)/shard_map/ppermute | solution.py:239
  35.0 6.5 %collective-permute-start.8 = (f32[4,4,16,128]{3,2,1,0:T(8,128)S(1)}, f32[4,4,16,128]{3,2,1,0:T(8,128)S(1)}, u32[]{:S(2)}, u32[]{:S(2)}) collective-permute-start(f32[4,4,16,128]{3,2,1,0:T(8,128)S(1)} %get-tuple-element.35), channel_id=1, source_target_pairs={{0,8},{8,16},{16,24},{24,0},{1,9},{9,17},{17,25},{25,1},{2,10},{10... | collective-permute-start | bytes 393224 | tf_op jit(solution)/shard_map/ppermute | solution.py:220
  38.5 6.5 %collective-permute-start.9 = (f32[4,4,16,128]{3,2,1,0:T(8,128)S(1)}, f32[4,4,16,128]{3,2,1,0:T(8,128)S(1)}, u32[]{:S(2)}, u32[]{:S(2)}) collective-permute-start(f32[4,4,16,128]{3,2,1,0:T(8,128)S(1)} %get-tuple-element.36), channel_id=1, source_target_pairs={{0,24},{8,0},{16,8},{24,16},{1,25},{9,1},{17,9},{25,17},{2,26},{10... | collective-permute-start | bytes 393224 | tf_op jit(solution)/shard_map/ppermute | solution.py:220
  45.0 8.0 %collective-permute-start.10 = (f32[4,12,8,128]{3,2,1,0:T(8,128)S(1)}, f32[4,12,8,128]{3,2,1,0:T(8,128)S(1)}, u32[]{:S(2)}, u32[]{:S(2)}) collective-permute-start(f32[4,12,8,128]{3,2,1,0:T(8,128)S(1)} %get-tuple-element.37), channel_id=1, source_target_pairs={{0,7},{1,2},{2,1},{3,4},{4,3},{5,6},{6,5},{7,0},{8,15},{9,10},{10,... | collective-permute-start | bytes 589832 | tf_op jit(solution)/shard_map/ppermute | solution.py:228
  48.3 5.7 %collective-permute-start.11 = (f32[4,12,8,128]{3,2,1,0:T(8,128)S(1)}, f32[4,12,8,128]{3,2,1,0:T(8,128)S(1)}, u32[]{:S(2)}, u32[]{:S(2)}) collective-permute-start(f32[4,12,8,128]{3,2,1,0:T(8,128)S(1)} %get-tuple-element.38), channel_id=1, source_target_pairs={{0,1},{1,0},{2,3},{3,2},{4,5},{5,4},{6,7},{7,6},{8,9},{9,8},{10,11... | collective-permute-start | bytes 589832 | tf_op jit(solution)/shard_map/ppermute | solution.py:229
  56.8 1.3 %collective-permute-start.12 = (f32[4,4,8,128]{3,2,1,0:T(8,128)S(1)}, f32[4,4,8,128]{3,2,1,0:T(8,128)S(1)}, u32[]{:S(2)}, u32[]{:S(2)}) collective-permute-start(f32[4,4,8,128]{3,2,1,0:T(8,128)S(1)} %dynamic-slice_bitcast_fusion), channel_id=1, source_target_pairs={{0,32},{32,0},{64,96},{96,64},{128,160},{160,128},{192,224},{224,1... | collective-permute-start | bytes 196616 | tf_op jit(solution)/shard_map/ppermute | solution.py:239
  58.1 6.6 %collective-permute-start.15 = (f32[4,8,128]{2,1,0:T(8,128)S(1)}, f32[4,8,128]{2,1,0:T(8,128)S(1)}, u32[]{:S(2)}, u32[]{:S(2)}) collective-permute-start(f32[4,8,128]{2,1,0:T(8,128)S(1)} %get-tuple-element.50), channel_id=1, source_target_pairs={{0,192},{32,224},{64,128},{96,160},{128,64},{160,96},{192,0},{224,... | collective-permute-start | bytes 49160 | tf_op jit(solution)/shard_map/ppermute | solution.py:239
  61.8 7.9 %collective-permute-start.14 = (f32[4,8,128]{2,1,0:T(8,128)S(1)}, f32[4,8,128]{2,1,0:T(8,128)S(1)}, u32[]{:S(2)}, u32[]{:S(2)}) collective-permute-start(f32[4,8,128]{2,1,0:T(8,128)S(1)} %get-tuple-element.51), channel_id=1, source_target_pairs={{0,128},{32,160},{64,192},{96,224},{128,0},{160,32},{192,64},{224,... | collective-permute-start | bytes 49160 | tf_op jit(solution)/shard_map/ppermute | solution.py:239
  63.5 6.2 %collective-permute-start.13 = (f32[4,8,128]{2,1,0:T(8,128)S(1)}, f32[4,8,128]{2,1,0:T(8,128)S(1)}, u32[]{:S(2)}, u32[]{:S(2)}) collective-permute-start(f32[4,8,128]{2,1,0:T(8,128)S(1)} %get-tuple-element.52), channel_id=1, source_target_pairs={{0,64},{32,96},{64,0},{96,32},{128,192},{160,224},{192,128},{224,1... | collective-permute-start | bytes 49160 | tf_op jit(solution)/shard_map/ppermute | solution.py:239

commit v5 on v4

--- a/solution.py
+++ b/solution.py
@@ -148,6 +148,15 @@
         sweep(sc_ref, scale_ref, sc_ref, o, 2, into(a_ref, o))
         sweep(a_ref, scale_ref, sc_ref, o, 3, into(b_ref, o))
         last_sweep(b_ref, scale_ref, sc_ref, o, orb_ref, occ_ref, resp_ref, dens_ref)
+
+
+def strips_kernel(*refs):
+    perturbation, potential, orbitals, dests = refs[0:2], refs[2:4], (refs[4:6], refs[6:8]), refs[8:10]
+    for end, dest_ref in enumerate(dests):
+        for y in range(4):
+            for o in range(2):
+                dest_ref[o, y] = perturbation[end][y] * orbitals[o][end][y]
+            dest_ref[2, y] = potential[end][y]
 
 
 def change_kernel(own_ref, other_ref, pert_ref, kern_ref, orb_ref, resp_ref, core_ref, centre_ref, up_ref, down_ref):
@@ -202,7 +211,8 @@
             out_ref[b, part] = blocks[b]
 
 
-def final_kernel(own_ref, one_ref, two_ref, three_ref, dens_ref):
+def final_kernel(own_ref, one_ref, two_ref, three_ref, resp_ref, dens_ref, response_ref):
+    response_ref[...] = resp_ref[...]
     for part in range(4):
         y, z = part // 2, 8 * (part % 2)
         total = (own_ref[part] + one_ref[part]) + (two_ref[part] + three_ref[part])
@@ -250,9 +260,7 @@
         return field[12:16], field[0:4]
 
     edges = lax.optimization_barrier([ends(field) for field in (perturbation, potential, orbitals[0], orbitals[1])])
-    up, down = (
-        jnp.stack([edges[0][i] * edges[2][i], edges[0][i] * edges[3][i], edges[1][i]]) for i in range(2)
-    )
+    up, down = call(strips_kernel, (f32(3, 4, 16, 128), f32(3, 4, 16, 128)), *(end for pair in edges for end in pair))
     centre = jnp.concatenate([perturbation[None] * orbitals, potential[None]], 0)
     lo, hi = exchange_y(up, down)
     near, far = exchange_z(centre, lo, hi, odd)
@@ -287,7 +295,9 @@
         return lax.dynamic_index_in_dim(kept, chip ^ step, 0, keepdims=False)
 
     two, one, three = (partner(block_of(step), 2 * step) for step in (2, 1, 3))
-    density = call(final_kernel, f32(16, 16, 16), block_of(0), one, two, three)
+    density, response = call(
+        final_kernel, (f32(16, 16, 16), f32(2, 16, 16, 128)), block_of(0), one, two, three, response
+    )
     return response, density
 
 

time: 70.5 us -> 67.6 us (0.959)
  starting transfers between devices: 29.7 us -> 25.6 us
  waiting for transfers between devices: 33.2 us -> 34.7 us
    ppermute x2, starting transfers between devices: 5.9 us -> 2.65 us  [exchange_y(): lax.ppermute(up, 'gy', ring('gy', 1))]
    ppermute x2, waiting for transfers between devices: 3.08 us -> 5.85 us  [exchange_y(): lax.ppermute(up, 'gy', ring('gy', 1))]
    ppermute x2, starting transfers between devices: 7.75 us -> 6.02 us  [exchange_z(): far = lax.ppermute(far, 'gz', far_pairs(count))]
    ppermute x2, waiting for transfers between devices: 2.98 us -> 1.38 us  [exchange_z(): near = lax.ppermute(near, 'gz', [(i, i ^ 1) for i in range(count)])]
    ppermute x2, waiting for transfers between devices: 7.82 us -> 9.43 us  [exchange_z(): far = lax.ppermute(far, 'gz', far_pairs(count))]
    ppermute x2, waiting for transfers between devices: 5.82 us -> 4.73 us  [exchange_y(): lax.ppermute(down, 'gy', ring('gy', -1))]
    ppermute x2, starting transfers between devices: 0.91 us -> 1.75 us  [exchange_y(): lax.ppermute(down, 'gy', ring('gy', -1))]
    pallas_call x6 -> x7, Pallas kernels: 5.55 us -> 5.1 us  [call(): pl.pallas_call(body, out_shape=outs, in_specs=[VMEM] * (len(args) - smem)...]
  transfers between devices with their start and end apart: 16 -> 16, of which waited for: 13 -> 14; matrix products, arithmetic and copies ran while one was open for 0% -> 0% of each run, Pallas kernels for 0% -> 0%
where the time goes in v5:
time: 67.6 us; the launch traced here: 67.5 us
  waiting for transfers between devices  34.7 us (51%)
  starting transfers between devices  25.6 us (38%)
  Pallas kernels  5.1 us (8%)
  local copies, waits for them, and re-layouts  1.09 us (2%)
  between operations  0.85 us (1%)
    ppermute x8, starting transfers between devices, partner(): lax.ppermute(value, 'bands', [(i, i ^ steps[i % len(steps)]) for i in ran...  15.2 us
    ppermute x8, waiting for transfers between devices, partner(): lax.ppermute(value, 'bands', [(i, i ^ steps[i % len(steps)]) for i in ran...  13.3 us
    ppermute x2, waiting for transfers between devices, exchange_z(): far = lax.ppermute(far, 'gz', far_pairs(count))  9.43 us
    ppermute x2, starting transfers between devices, exchange_z(): far = lax.ppermute(far, 'gz', far_pairs(count))  6.02 us
    ppermute x2, waiting for transfers between devices, exchange_y(): lax.ppermute(up, 'gy', ring('gy', 1))  5.85 us
    pallas_call x7, Pallas kernels, call(): pl.pallas_call(body, out_shape=outs, in_specs=[VMEM] * (len(args) - smem)...  5.1 us
    ppermute x2, waiting for transfers between devices, exchange_y(): lax.ppermute(down, 'gy', ring('gy', -1))  4.73 us
    ppermute x2, starting transfers between devices, exchange_y(): lax.ppermute(up, 'gy', ring('gy', 1))  2.65 us
  transfers between devices with their start and end apart: 16, of which 14 were waited for; matrix products, arithmetic and copies ran while one was open for 0% of the time, Pallas kernels for 0%

profile of v5, /device:TPU:6, one launch (start us, length us, event | category | flops | bytes accessed | tf_op | source)
XLA Modules:
  0.0 67.5 jit_solution(12712404273696181828)
XLA Ops:
  0.6 0.9 %slice_bitcast_fusion = (f32[4,16,128]{2,1,0:T(8,128)S(1)}, f32[4,16,128]{2,1,0:T(8,128)S(1)}, f32[4,16,128]{2,1,0:T(8,128)S(1)}, f32[4,16,128]{2,1,0:T(8,128)S(1)}) fusion(f32[2,16,16,128]{3,2,1,0:T(8,128)} %orb_ref.5), kind=kLoop, calls=%fused_computation.5 | loop fusion | bytes 262144 | tf_op jit(solution)/shard_map/slice | solution.py:260
  1.5 0.1 copy-done.5
  1.7 2.3 %collective-permute-start = (f32[3,4,16,128]{3,2,1,0:T(8,128)S(1)}, f32[3,4,16,128]{3,2,1,0:T(8,128)S(1)}, u32[]{:S(2)}, u32[]{:S(2)}) collective-permute-start(f32[3,4,16,128]{3,2,1,0:T(8,128)S(1)} %get-tuple-element.34), channel_id=1, source_target_pairs={{0,8},{8,16},{16,24},{24,0},{1,9},{9,17},{17,25},{25,1},{2,10},{10... | collective-permute-start | bytes 294920 | tf_op jit(solution)/shard_map/ppermute | solution.py:230
  4.1 2.3 %collective-permute-done.lo_ref = f32[3,4,16,128]{3,2,1,0:T(8,128)S(1)} collective-permute-done((f32[3,4,16,128]{3,2,1,0:T(8,128)S(1)}, f32[3,4,16,128]{3,2,1,0:T(8,128)S(1)}, u32[]{:S(2)}, u32[]{:S(2)}) %collective-permute-start) | collective-permute-done | bytes 98336 | tf_op jit(solution)/shard_map/ppermute | solution.py:230
  6.4 3.4 %collective-permute-done.1.hi_ref = f32[3,4,16,128]{3,2,1,0:T(8,128)S(1)} collective-permute-done((f32[3,4,16,128]{3,2,1,0:T(8,128)S(1)}, f32[3,4,16,128]{3,2,1,0:T(8,128)S(1)}, u32[]{:S(2)}, u32[]{:S(2)}) %collective-permute-start.1) | collective-permute-done | bytes 98336 | tf_op jit(solution)/shard_map/ppermute | solution.py:230
  9.9 2.7 %collective-permute-start.2 = (f32[3,12,8,128]{3,2,1,0:T(8,128)S(1)}, f32[3,12,8,128]{3,2,1,0:T(8,128)S(1)}, u32[]{:S(2)}, u32[]{:S(2)}) collective-permute-start(f32[3,12,8,128]{3,2,1,0:T(8,128)S(1)} %get-tuple-element.36), channel_id=1, source_target_pairs={{0,7},{1,2},{2,1},{3,4},{4,3},{5,6},{6,5},{7,0},{8,15},{9,10},{10,... | collective-permute-start | bytes 442376 | tf_op jit(solution)/shard_map/ppermute | solution.py:238
  12.6 4.6 %collective-permute-done.2.far_ref = f32[3,12,8,128]{3,2,1,0:T(8,128)S(1)} collective-permute-done((f32[3,12,8,128]{3,2,1,0:T(8,128)S(1)}, f32[3,12,8,128]{3,2,1,0:T(8,128)S(1)}, u32[]{:S(2)}, u32[]{:S(2)}) %collective-permute-start.2) | collective-permute-done | bytes 147488 | tf_op jit(solution)/shard_map/ppermute | solution.py:238
  17.2 0.5 collective-permute-done.3.near_ref
  17.7 1.8 %shard_map.79 = (f32[2,16,16,128]{3,2,1,0:T(8,128)S(1)}, f32[16,16,128]{2,1,0:T(8,128)S(1)}, f32[2,24,24,128]{3,2,1,0:T(8,128)S(1)}) custom-call(f32[3,16,16,128]{3,2,1,0:T(8,128)S(1)} %pad_maximum_fusion.centre_ref, f32[3,4,16,128]{3,2,1,0:T(8,128)S(1)} %collective-permute-done.lo_ref, f32[3,4,16,128]{3,2,1,0:T(8,128)S(1)} %collective-permute-done.1.hi_ref, ...), custom_call_target="tpu_custom_call" | custom-call | tf_op jit(solution)/shard_map/pallas_call | solution.py:15
  19.6 0.1 collective-permute-start.4
  19.7 1.2 %collective-permute-done.4 = f32[8,16,128]{2,1,0:T(8,128)S(1)} collective-permute-done((f32[8,16,128]{2,1,0:T(8,128)S(1)}, f32[8,16,128]{2,1,0:T(8,128)S(1)}, u32[]{:S(2)}, u32[]{:S(2)}) %collective-permute-start.4) | collective-permute-done | bytes 65568 | tf_op jit(solution)/shard_map/ppermute | solution.py:249
  20.9 3.4 %collective-permute-start.5 = (f32[8,16,128]{2,1,0:T(8,128)S(1)}, f32[8,16,128]{2,1,0:T(8,128)S(1)}, u32[]{:S(2)}, u32[]{:S(2)}) collective-permute-start(f32[8,16,128]{2,1,0:T(8,128)S(1)} %dynamic-slice_add_fusion), channel_id=1, source_target_pairs={{0,64},{32,224},{64,0},{96,160},{128,192},{160,96},{192,128},{224,... | collective-permute-start | bytes 196616 | tf_op jit(solution)/shard_map/ppermute | solution.py:249
  24.3 2.5 %collective-permute-done.5 = f32[8,16,128]{2,1,0:T(8,128)S(1)} collective-permute-done((f32[8,16,128]{2,1,0:T(8,128)S(1)}, f32[8,16,128]{2,1,0:T(8,128)S(1)}, u32[]{:S(2)}, u32[]{:S(2)}) %collective-permute-start.5) | collective-permute-done | bytes 65568 | tf_op jit(solution)/shard_map/ppermute | solution.py:249
  26.8 5.0 %collective-permute-start.6 = (f32[8,16,128]{2,1,0:T(8,128)S(1)}, f32[8,16,128]{2,1,0:T(8,128)S(1)}, u32[]{:S(2)}, u32[]{:S(2)}) collective-permute-start(f32[8,16,128]{2,1,0:T(8,128)S(1)} %add.52), channel_id=1, source_target_pairs={{0,192},{32,96},{64,128},{96,32},{128,64},{160,224},{192,0},{224,1... | collective-permute-start | bytes 196616 | tf_op jit(solution)/shard_map/ppermute | solution.py:249
  31.8 2.3 %collective-permute-done.6 = f32[8,16,128]{2,1,0:T(8,128)S(1)} collective-permute-done((f32[8,16,128]{2,1,0:T(8,128)S(1)}, f32[8,16,128]{2,1,0:T(8,128)S(1)}, u32[]{:S(2)}, u32[]{:S(2)}) %collective-permute-start.6) | collective-permute-done | bytes 65568 | tf_op jit(solution)/shard_map/ppermute | solution.py:249
  34.1 0.1 collective-permute-start.7
  34.2 1.2 %collective-permute-done.7.other_ref = f32[8,16,128]{2,1,0:T(8,128)S(1)} collective-permute-done((f32[8,16,128]{2,1,0:T(8,128)S(1)}, f32[8,16,128]{2,1,0:T(8,128)S(1)}, u32[]{:S(2)}, u32[]{:S(2)}) %collective-permute-start.7) | collective-permute-done | bytes 65568 | tf_op jit(solution)/shard_map/ppermute | solution.py:249
  35.5 0.4 collective-permute-start.8
  35.9 1.7 %collective-permute-start.9 = (f32[4,4,16,128]{3,2,1,0:T(8,128)S(1)}, f32[4,4,16,128]{3,2,1,0:T(8,128)S(1)}, u32[]{:S(2)}, u32[]{:S(2)}) collective-permute-start(f32[4,4,16,128]{3,2,1,0:T(8,128)S(1)} %get-tuple-element.42), channel_id=1, source_target_pairs={{0,24},{8,0},{16,8},{24,16},{1,25},{9,1},{17,9},{25,17},{2,26},{10... | collective-permute-start | bytes 393224 | tf_op jit(solution)/shard_map/ppermute | solution.py:230
  37.6 3.5 %collective-permute-done.8.lo_ref = f32[4,4,16,128]{3,2,1,0:T(8,128)S(1)} collective-permute-done((f32[4,4,16,128]{3,2,1,0:T(8,128)S(1)}, f32[4,4,16,128]{3,2,1,0:T(8,128)S(1)}, u32[]{:S(2)}, u32[]{:S(2)}) %collective-permute-start.8) | collective-permute-done | bytes 131104 | tf_op jit(solution)/shard_map/ppermute | solution.py:230
  41.1 1.3 %collective-permute-done.9.hi_ref = f32[4,4,16,128]{3,2,1,0:T(8,128)S(1)} collective-permute-done((f32[4,4,16,128]{3,2,1,0:T(8,128)S(1)}, f32[4,4,16,128]{3,2,1,0:T(8,128)S(1)}, u32[]{:S(2)}, u32[]{:S(2)}) %collective-permute-start.9) | collective-permute-done | bytes 131104 | tf_op jit(solution)/shard_map/ppermute | solution.py:230
  42.5 3.3 %collective-permute-start.10 = (f32[4,12,8,128]{3,2,1,0:T(8,128)S(1)}, f32[4,12,8,128]{3,2,1,0:T(8,128)S(1)}, u32[]{:S(2)}, u32[]{:S(2)}) collective-permute-start(f32[4,12,8,128]{3,2,1,0:T(8,128)S(1)} %get-tuple-element.43), channel_id=1, source_target_pairs={{0,7},{1,2},{2,1},{3,4},{4,3},{5,6},{6,5},{7,0},{8,15},{9,10},{10,... | collective-permute-start | bytes 589832 | tf_op jit(solution)/shard_map/ppermute | solution.py:238
  45.8 4.8 %collective-permute-done.10.far_ref = f32[4,12,8,128]{3,2,1,0:T(8,128)S(1)} collective-permute-done((f32[4,12,8,128]{3,2,1,0:T(8,128)S(1)}, f32[4,12,8,128]{3,2,1,0:T(8,128)S(1)}, u32[]{:S(2)}, u32[]{:S(2)}) %collective-permute-start.10) | collective-permute-done | bytes 196640 | tf_op jit(solution)/shard_map/ppermute | solution.py:238
  50.6 0.9 %collective-permute-done.11.near_ref = f32[4,12,8,128]{3,2,1,0:T(8,128)S(1)} collective-permute-done((f32[4,12,8,128]{3,2,1,0:T(8,128)S(1)}, f32[4,12,8,128]{3,2,1,0:T(8,128)S(1)}, u32[]{:S(2)}, u32[]{:S(2)}) %collective-permute-start.11) | collective-permute-done | bytes 196640 | tf_op jit(solution)/shard_map/ppermute | solution.py:239
  51.5 2.4 %shard_map.82 = (f32[2,16,16,128]{3,2,1,0:T(8,128)S(1)}, f32[8,4,8,128]{3,2,1,0:T(8,128)S(1)}) custom-call(f32[4,16,16,128]{3,2,1,0:T(8,128)S(1)} %get-tuple-element.40.centre_ref, f32[4,4,16,128]{3,2,1,0:T(8,128)S(1)} %collective-permute-done.8.lo_ref, f32[4,4,16,128]{3,2,1,0:T(8,128)S(1)} %collective-permute-done.9.hi_ref, ...), custom_call_target="tpu_custom_call" | custom-call | tf_op jit(solution)/shard_map/pallas_call | solution.py:15
  53.9 0.1 collective-permute-start.12
  54.0 1.2 %collective-permute-done.12 = f32[4,4,8,128]{3,2,1,0:T(8,128)S(1)} collective-permute-done((f32[4,4,8,128]{3,2,1,0:T(8,128)S(1)}, f32[4,4,8,128]{3,2,1,0:T(8,128)S(1)}, u32[]{:S(2)}, u32[]{:S(2)}) %collective-permute-start.12) | collective-permute-done | bytes 65568 | tf_op jit(solution)/shard_map/ppermute | solution.py:249
  55.2 3.7 %collective-permute-start.15 = (f32[4,8,128]{2,1,0:T(8,128)S(1)}, f32[4,8,128]{2,1,0:T(8,128)S(1)}, u32[]{:S(2)}, u32[]{:S(2)}) collective-permute-start(f32[4,8,128]{2,1,0:T(8,128)S(1)} %get-tuple-element.58), channel_id=1, source_target_pairs={{0,192},{32,224},{64,128},{96,160},{128,64},{160,96},{192,0},{224,... | collective-permute-start | bytes 49160 | tf_op jit(solution)/shard_map/ppermute | solution.py:249
  58.9 1.7 %collective-permute-start.14 = (f32[4,8,128]{2,1,0:T(8,128)S(1)}, f32[4,8,128]{2,1,0:T(8,128)S(1)}, u32[]{:S(2)}, u32[]{:S(2)}) collective-permute-start(f32[4,8,128]{2,1,0:T(8,128)S(1)} %get-tuple-element.59), channel_id=1, source_target_pairs={{0,128},{32,160},{64,192},{96,224},{128,0},{160,32},{192,64},{224,... | collective-permute-start | bytes 49160 | tf_op jit(solution)/shard_map/ppermute | solution.py:249
  60.6 1.2 %collective-permute-start.13 = (f32[4,8,128]{2,1,0:T(8,128)S(1)}, f32[4,8,128]{2,1,0:T(8,128)S(1)}, u32[]{:S(2)}, u32[]{:S(2)}) collective-permute-start(f32[4,8,128]{2,1,0:T(8,128)S(1)} %get-tuple-element.60), channel_id=1, source_target_pairs={{0,64},{32,96},{64,0},{96,32},{128,192},{160,224},{192,128},{224,1... | collective-permute-start | bytes 49160 | tf_op jit(solution)/shard_map/ppermute | solution.py:249
  61.8 4.9 %collective-permute-done.14.two_ref = f32[4,8,128]{2,1,0:T(8,128)S(1)} collective-permute-done((f32[4,8,128]{2,1,0:T(8,128)S(1)}, f32[4,8,128]{2,1,0:T(8,128)S(1)}, u32[]{:S(2)}, u32[]{:S(2)}) %collective-permute-start.14) | collective-permute-done | bytes 16416 | tf_op jit(solution)/shard_map/ppermute | solution.py:249
  66.7 0.8 %shard_map.83 = (f32[16,16,16]{2,1,0:T(8,128)}, f32[2,16,16,128]{3,2,1,0:T(8,128)}) custom-call(f32[4,8,128]{2,1,0:T(8,128)S(1)} %get-tuple-element.61.own_ref, f32[4,8,128]{2,1,0:T(8,128)S(1)} %collective-permute-done.13.one_ref, f32[4,8,128]{2,1,0:T(8,128)S(1)} %collective-permute-done.14.two_ref, f32[4,8,128]{2,1,0:T(8,128)S(1)} %collective-permute-done.15.three_ref, ...), custom_call_target="tpu_custom_call" | custom-call | tf_op jit(solution)/shard_map/pallas_call | solution.py:15
  (30 shorter events, 0.4 us)
Async XLA Ops:
  0.6 0.9 %copy-start.1 = (f32[16,16,128]{2,1,0:T(8,128)S(1)}, f32[16,16,128]{2,1,0:T(8,128)}, u32[]{:S(2)}) copy-start(f32[16,16,128]{2,1,0:T(8,128)} %pert_ref.1) | copy-start | bytes 393220
  0.6 1.0 %copy-start.5 = (f32[16,16,128]{2,1,0:T(8,128)S(1)}, f32[16,16,128]{2,1,0:T(8,128)}, u32[]{:S(2)}) copy-start(f32[16,16,128]{2,1,0:T(8,128)} %param.9) | copy-start | bytes 393220
  1.7 2.3 %copy-start = (f32[2,16,16,128]{3,2,1,0:T(8,128)S(1)}, f32[2,16,16,128]{3,2,1,0:T(8,128)}, u32[]{:S(2)}) copy-start(f32[2,16,16,128]{3,2,1,0:T(8,128)} %orb_ref.5) | copy-start | bytes 786436
  1.7 4.7 %collective-permute-start = (f32[3,4,16,128]{3,2,1,0:T(8,128)S(1)}, f32[3,4,16,128]{3,2,1,0:T(8,128)S(1)}, u32[]{:S(2)}, u32[]{:S(2)}) collective-permute-start(f32[3,4,16,128]{3,2,1,0:T(8,128)S(1)} %get-tuple-element.34), channel_id=1, source_target_pairs={{0,8},{8,16},{16,24},{24,0},{1,9},{9,17},{17,25},{25,1},{2,10},{10... | collective-permute-start | bytes 294920 | tf_op jit(solution)/shard_map/ppermute | solution.py:230
  4.0 5.8 %collective-permute-start.1 = (f32[3,4,16,128]{3,2,1,0:T(8,128)S(1)}, f32[3,4,16,128]{3,2,1,0:T(8,128)S(1)}, u32[]{:S(2)}, u32[]{:S(2)}) collective-permute-start(f32[3,4,16,128]{3,2,1,0:T(8,128)S(1)} %get-tuple-element.35), channel_id=1, source_target_pairs={{0,24},{8,0},{16,8},{24,16},{1,25},{9,1},{17,9},{25,17},{2,26},{10... | collective-permute-start | bytes 294920 | tf_op jit(solution)/shard_map/ppermute | solution.py:230
  9.9 7.3 %collective-permute-start.2 = (f32[3,12,8,128]{3,2,1,0:T(8,128)S(1)}, f32[3,12,8,128]{3,2,1,0:T(8,128)S(1)}, u32[]{:S(2)}, u32[]{:S(2)}) collective-permute-start(f32[3,12,8,128]{3,2,1,0:T(8,128)S(1)} %get-tuple-element.36), channel_id=1, source_target_pairs={{0,7},{1,2},{2,1},{3,4},{4,3},{5,6},{6,5},{7,0},{8,15},{9,10},{10,... | collective-permute-start | bytes 442376 | tf_op jit(solution)/shard_map/ppermute | solution.py:238
  12.6 5.1 %collective-permute-start.3 = (f32[3,12,8,128]{3,2,1,0:T(8,128)S(1)}, f32[3,12,8,128]{3,2,1,0:T(8,128)S(1)}, u32[]{:S(2)}, u32[]{:S(2)}) collective-permute-start(f32[3,12,8,128]{3,2,1,0:T(8,128)S(1)} %get-tuple-element.37), channel_id=1, source_target_pairs={{0,1},{1,0},{2,3},{3,2},{4,5},{5,4},{6,7},{7,6},{8,9},{9,8},{10,11... | collective-permute-start | bytes 442376 | tf_op jit(solution)/shard_map/ppermute | solution.py:239
  12.6 5.1 %copy-start.3 = (f32[2]{0:T(128)S(1)}, f32[2]{0:T(128)}, u32[]{:S(2)}) copy-start(f32[2]{0:T(128)} %occ_ref.3) | copy-start | bytes 28
  12.6 5.1 %copy-start.4 = (f32[2]{0:T(128)S(1)}, f32[2]{0:T(128)}, u32[]{:S(2)}) copy-start(f32[2]{0:T(128)} %shift_ref.1) | copy-start | bytes 28
  19.6 1.3 %collective-permute-start.4 = (f32[8,16,128]{2,1,0:T(8,128)S(1)}, f32[8,16,128]{2,1,0:T(8,128)S(1)}, u32[]{:S(2)}, u32[]{:S(2)}) collective-permute-start(f32[8,16,128]{2,1,0:T(8,128)S(1)} %constant_dynamic-slice_fusion), channel_id=1, source_target_pairs={{0,32},{32,0},{64,96},{96,64},{128,160},{160,128},{192,224},{224,1... | collective-permute-start | bytes 196616 | tf_op jit(solution)/shard_map/ppermute | solution.py:249
  20.9 5.8 %collective-permute-start.5 = (f32[8,16,128]{2,1,0:T(8,128)S(1)}, f32[8,16,128]{2,1,0:T(8,128)S(1)}, u32[]{:S(2)}, u32[]{:S(2)}) collective-permute-start(f32[8,16,128]{2,1,0:T(8,128)S(1)} %dynamic-slice_add_fusion), channel_id=1, source_target_pairs={{0,64},{32,224},{64,0},{96,160},{128,192},{160,96},{192,128},{224,... | collective-permute-start | bytes 196616 | tf_op jit(solution)/shard_map/ppermute | solution.py:249
  26.8 8.7 %copy-start.2 = (f32[16,16,128]{2,1,0:T(8,128)S(1)}, f32[16,16,128]{2,1,0:T(8,128)}, u32[]{:S(2)}) copy-start(f32[16,16,128]{2,1,0:T(8,128)} %kern_ref.1) | copy-start | bytes 393220
  26.8 7.3 %collective-permute-start.6 = (f32[8,16,128]{2,1,0:T(8,128)S(1)}, f32[8,16,128]{2,1,0:T(8,128)S(1)}, u32[]{:S(2)}, u32[]{:S(2)}) collective-permute-start(f32[8,16,128]{2,1,0:T(8,128)S(1)} %add.52), channel_id=1, source_target_pairs={{0,192},{32,96},{64,128},{96,32},{128,64},{160,224},{192,0},{224,1... | collective-permute-start | bytes 196616 | tf_op jit(solution)/shard_map/ppermute | solution.py:249
  34.1 1.3 %collective-permute-start.7 = (f32[8,16,128]{2,1,0:T(8,128)S(1)}, f32[8,16,128]{2,1,0:T(8,128)S(1)}, u32[]{:S(2)}, u32[]{:S(2)}) collective-permute-start(f32[8,16,128]{2,1,0:T(8,128)S(1)} %add.53.own_ref), channel_id=1, source_target_pairs={{0,32},{32,0},{64,96},{96,64},{128,160},{160,128},{192,224},{224,1... | collective-permute-start | bytes 196616 | tf_op jit(solution)/shard_map/ppermute | solution.py:249
  35.5 5.6 %collective-permute-start.8 = (f32[4,4,16,128]{3,2,1,0:T(8,128)S(1)}, f32[4,4,16,128]{3,2,1,0:T(8,128)S(1)}, u32[]{:S(2)}, u32[]{:S(2)}) collective-permute-start(f32[4,4,16,128]{3,2,1,0:T(8,128)S(1)} %get-tuple-element.41), channel_id=1, source_target_pairs={{0,8},{8,16},{16,24},{24,0},{1,9},{9,17},{17,25},{25,1},{2,10},{10... | collective-permute-start | bytes 393224 | tf_op jit(solution)/shard_map/ppermute | solution.py:230
  35.9 6.6 %collective-permute-start.9 = (f32[4,4,16,128]{3,2,1,0:T(8,128)S(1)}, f32[4,4,16,128]{3,2,1,0:T(8,128)S(1)}, u32[]{:S(2)}, u32[]{:S(2)}) collective-permute-start(f32[4,4,16,128]{3,2,1,0:T(8,128)S(1)} %get-tuple-element.42), channel_id=1, source_target_pairs={{0,24},{8,0},{16,8},{24,16},{1,25},{9,1},{17,9},{25,17},{2,26},{10... | collective-permute-start | bytes 393224 | tf_op jit(solution)/shard_map/ppermute | solution.py:230
  42.5 8.1 %collective-permute-start.10 = (f32[4,12,8,128]{3,2,1,0:T(8,128)S(1)}, f32[4,12,8,128]{3,2,1,0:T(8,128)S(1)}, u32[]{:S(2)}, u32[]{:S(2)}) collective-permute-start(f32[4,12,8,128]{3,2,1,0:T(8,128)S(1)} %get-tuple-element.43), channel_id=1, source_target_pairs={{0,7},{1,2},{2,1},{3,4},{4,3},{5,6},{6,5},{7,0},{8,15},{9,10},{10,... | collective-permute-start | bytes 589832 | tf_op jit(solution)/shard_map/ppermute | solution.py:238
  45.8 5.7 %collective-permute-start.11 = (f32[4,12,8,128]{3,2,1,0:T(8,128)S(1)}, f32[4,12,8,128]{3,2,1,0:T(8,128)S(1)}, u32[]{:S(2)}, u32[]{:S(2)}) collective-permute-start(f32[4,12,8,128]{3,2,1,0:T(8,128)S(1)} %get-tuple-element.44), channel_id=1, source_target_pairs={{0,1},{1,0},{2,3},{3,2},{4,5},{5,4},{6,7},{7,6},{8,9},{9,8},{10,11... | collective-permute-start | bytes 589832 | tf_op jit(solution)/shard_map/ppermute | solution.py:239
  53.9 1.3 %collective-permute-start.12 = (f32[4,4,8,128]{3,2,1,0:T(8,128)S(1)}, f32[4,4,8,128]{3,2,1,0:T(8,128)S(1)}, u32[]{:S(2)}, u32[]{:S(2)}) collective-permute-start(f32[4,4,8,128]{3,2,1,0:T(8,128)S(1)} %dynamic-slice_bitcast_fusion), channel_id=1, source_target_pairs={{0,32},{32,0},{64,96},{96,64},{128,160},{160,128},{192,224},{224,1... | collective-permute-start | bytes 196616 | tf_op jit(solution)/shard_map/ppermute | solution.py:249
  55.2 6.6 %collective-permute-start.15 = (f32[4,8,128]{2,1,0:T(8,128)S(1)}, f32[4,8,128]{2,1,0:T(8,128)S(1)}, u32[]{:S(2)}, u32[]{:S(2)}) collective-permute-start(f32[4,8,128]{2,1,0:T(8,128)S(1)} %get-tuple-element.58), channel_id=1, source_target_pairs={{0,192},{32,224},{64,128},{96,160},{128,64},{160,96},{192,0},{224,... | collective-permute-start | bytes 49160 | tf_op jit(solution)/shard_map/ppermute | solution.py:249
  58.9 7.8 %collective-permute-start.14 = (f32[4,8,128]{2,1,0:T(8,128)S(1)}, f32[4,8,128]{2,1,0:T(8,128)S(1)}, u32[]{:S(2)}, u32[]{:S(2)}) collective-permute-start(f32[4,8,128]{2,1,0:T(8,128)S(1)} %get-tuple-element.59), channel_id=1, source_target_pairs={{0,128},{32,160},{64,192},{96,224},{128,0},{160,32},{192,64},{224,... | collective-permute-start | bytes 49160 | tf_op jit(solution)/shard_map/ppermute | solution.py:249
  60.6 6.1 %collective-permute-start.13 = (f32[4,8,128]{2,1,0:T(8,128)S(1)}, f32[4,8,128]{2,1,0:T(8,128)S(1)}, u32[]{:S(2)}, u32[]{:S(2)}) collective-permute-start(f32[4,8,128]{2,1,0:T(8,128)S(1)} %get-tuple-element.60), channel_id=1, source_target_pairs={{0,64},{32,96},{64,0},{96,32},{128,192},{160,224},{192,128},{224,1... | collective-permute-start | bytes 49160 | tf_op jit(solution)/shard_map/ppermute | solution.py:249

commit v6 on v5

--- a/solution.py
+++ b/solution.py
@@ -30,14 +30,12 @@
     return lax.broadcasted_iota(jnp.int32, (8, 128), 0) < 4
 
 
-def pack_z(row, even, near_ref, far_ref, field):
+def pack_z(row, head_ref, tail_ref, field):
     low = low_half()
     for j in range(12):
         a, b = row(j), row(j + 12)
-        head = jnp.where(low, a[:8], pltpu.roll(b[:8], 4, 0))
-        tail = jnp.where(low, pltpu.roll(b[8:], 4, 0), a[8:])
-        near_ref[field, j] = jnp.where(even, tail, head)
-        far_ref[field, j] = jnp.where(even, head, tail)
+        head_ref[field, j] = jnp.where(low, a[:8], pltpu.roll(b[:8], 4, 0))
+        tail_ref[field, j] = jnp.where(low, pltpu.roll(b[8:], 4, 0), a[8:])
 
 
 def padded_row(centre_ref, lo_ref, hi_ref, field):
@@ -51,19 +49,17 @@
     return row
 
 
-def pack_kernel(centre_ref, lo_ref, hi_ref, odd_ref, far_ref, near_ref):
-    even = odd_ref[0] == 0
+def pack_kernel(centre_ref, lo_ref, hi_ref, tail_ref, head_ref):
     for field in range(centre_ref.shape[0]):
-        pack_z(padded_row(centre_ref, lo_ref, hi_ref, field), even, near_ref, far_ref, field)
-
-
-def assemble(row, near_ref, far_ref, field, odd_ref, dest_ref, at):
-    low, even = low_half(), odd_ref[0] == 0
+        pack_z(padded_row(centre_ref, lo_ref, hi_ref, field), head_ref, tail_ref, field)
+
+
+def assemble(row, above_ref, below_ref, field, dest_ref, at):
+    low = low_half()
     for r in range(24):
         dest_ref[at, r, 0:16] = row(r)
     for j in range(12):
-        near, far = near_ref[field, j], far_ref[field, j]
-        above, below = jnp.where(even, near, far), jnp.where(even, far, near)
+        above, below = above_ref[field, j], below_ref[field, j]
         dest_ref[at, j, 16:24] = jnp.where(low, above, below)
         dest_ref[at, j + 12, 16:24] = pltpu.roll(jnp.where(low, below, above), 4, 0)
 
@@ -131,12 +127,12 @@
 
 
 def first_kernel(
-    centre_ref, lo_ref, hi_ref, far_ref, near_ref, orb_ref, shift_ref, occ_ref, odd_ref,
+    centre_ref, lo_ref, hi_ref, below_ref, above_ref, orb_ref, shift_ref, occ_ref,
     resp_ref, dens_ref, scale_ref, p_ref, sc_ref, a_ref, b_ref,
 ):
     for field in range(2):
-        assemble(padded_row(centre_ref, lo_ref, hi_ref, field), near_ref, far_ref, field, odd_ref, p_ref, field)
-    assemble(padded_row(centre_ref, lo_ref, hi_ref, 2), near_ref, far_ref, 2, odd_ref, a_ref, 0)
+        assemble(padded_row(centre_ref, lo_ref, hi_ref, field), above_ref, below_ref, field, p_ref, field)
+    assemble(padded_row(centre_ref, lo_ref, hi_ref, 2), above_ref, below_ref, 2, a_ref, 0)
     for o in range(2):
         base = 32.0 / 15.0 + shift_ref[o]
 
@@ -192,12 +188,12 @@
 
 
 def second_kernel(
-    centre_ref, lo_ref, hi_ref, far_ref, near_ref, scale_ref, orb_ref, occ_ref, odd_ref,
+    centre_ref, lo_ref, hi_ref, below_ref, above_ref, scale_ref, orb_ref, occ_ref,
     resp_ref, out_ref, p_ref, u_ref, sc_ref, a_ref, b_ref, dens_ref,
 ):
     for o in range(2):
-        assemble(padded_row(centre_ref, lo_ref, hi_ref, o), near_ref, far_ref, o, odd_ref, p_ref, o)
-        assemble(padded_row(centre_ref, lo_ref, hi_ref, 2 + o), near_ref, far_ref, 2 + o, odd_ref, u_ref, o)
+        assemble(padded_row(centre_ref, lo_ref, hi_ref, o), above_ref, below_ref, o, p_ref, o)
+        assemble(padded_row(centre_ref, lo_ref, hi_ref, 2 + o), above_ref, below_ref, 2 + o, u_ref, o)
     for o in range(2):
         sources(p_ref, scale_ref, sc_ref, o)
         sweep(u_ref, scale_ref, sc_ref, o, 1, into(a_ref, o))
@@ -211,11 +207,11 @@
             out_ref[b, part] = blocks[b]
 
 
-def final_kernel(own_ref, one_ref, two_ref, three_ref, resp_ref, dens_ref, response_ref):
+def final_kernel(own_ref, last_ref, resp_ref, dens_ref, response_ref):
     response_ref[...] = resp_ref[...]
     for part in range(4):
         y, z = part // 2, 8 * (part % 2)
-        total = (own_ref[part] + one_ref[part]) + (two_ref[part] + three_ref[part])
+        total = own_ref[part] + last_ref[part]
         for k in range(8):
             moved = total if k == 0 else pltpu.roll(total, 128 - 16 * k, 1)
             dens_ref[2 * k + y, z : z + 8, :] = moved[:, :16]
@@ -230,18 +226,11 @@
     return lax.ppermute(up, "gy", ring("gy", 1)), lax.ppermute(down, "gy", ring("gy", -1))
 
 
-def exchange_z(centre, lo, hi, odd):
+def exchange_z(centre, lo, hi):
     fields = centre.shape[0]
     strip = f32(fields, 12, 8, 128)
-    far, near = call(pack_kernel, (strip, strip), centre, lo, hi, odd, smem=1)
-    count = lax.axis_size("gz")
-    far = lax.ppermute(far, "gz", far_pairs(count))
-    near = lax.ppermute(near, "gz", [(i, i ^ 1) for i in range(count)])
-    return near, far
-
-
-def far_pairs(count):
-    return [(i, (i - 1) % count if i % 2 == 0 else (i + 1) % count) for i in range(count)]
+    tail, head = call(pack_kernel, (strip, strip), centre, lo, hi)
+    return lax.ppermute(head, "gz", ring("gz", -1)), lax.ppermute(tail, "gz", ring("gz", 1))
 
 
 def partner(value, *steps):
@@ -255,7 +244,6 @@
     padded = f32(2, 24, 24, 128)
     wide = pltpu.VMEM((2, 24, 24, 128), jnp.float32)
 
-    odd = (lax.axis_index("gz") % 2)[None].astype(jnp.int32)
     def ends(field):
         return field[12:16], field[0:4]
 
@@ -263,11 +251,11 @@
     up, down = call(strips_kernel, (f32(3, 4, 16, 128), f32(3, 4, 16, 128)), *(end for pair in edges for end in pair))
     centre = jnp.concatenate([perturbation[None] * orbitals, potential[None]], 0)
     lo, hi = exchange_y(up, down)
-    near, far = exchange_z(centre, lo, hi, odd)
+    above, below = exchange_z(centre, lo, hi)
     response, partial, scale = call(
         first_kernel, (f32(2, 16, 16, 128), f32(16, 16, 128), padded),
-        centre, lo, hi, far, near, orbitals, orbital_shift, occupation, odd,
-        scratch=[wide] * 4, smem=3,
+        centre, lo, hi, below, above, orbitals, orbital_shift, occupation,
+        scratch=[wide] * 4, smem=2,
     )
 
     own = lax.dynamic_slice_in_dim(partial, 8 * core, 8, 0)
@@ -280,11 +268,11 @@
         own, other, perturbation, kernel, orbitals, response, core[None].astype(jnp.int32), smem=1,
     )
     lo, hi = exchange_y(up, down)
-    near, far = exchange_z(centre, lo, hi, odd)
+    above, below = exchange_z(centre, lo, hi)
     response, blocks = call(
         second_kernel, (f32(2, 16, 16, 128), f32(8, 4, 8, 128)),
-        centre, lo, hi, far, near, scale, orbitals, occupation, odd,
-        scratch=[wide] * 5 + [pltpu.VMEM((16, 16, 128), jnp.float32)], smem=2,
+        centre, lo, hi, below, above, scale, orbitals, occupation,
+        scratch=[wide] * 5 + [pltpu.VMEM((16, 16, 128), jnp.float32)], smem=1,
     )
 
     blocks = blocks.reshape(4, 2, 4, 8, 128)
@@ -294,9 +282,11 @@
     def block_of(step):
         return lax.dynamic_index_in_dim(kept, chip ^ step, 0, keepdims=False)
 
-    two, one, three = (partner(block_of(step), 2 * step) for step in (2, 1, 3))
+    first, second = 1 + 2 * core, 3 - 2 * core
+    pair = jnp.stack([block_of(0), block_of(second)]) + partner(jnp.stack([block_of(first), block_of(2)]), 2, 6)
+    last = partner(pair[1], 6, 2)
     density, response = call(
-        final_kernel, (f32(16, 16, 16), f32(2, 16, 16, 128)), block_of(0), one, two, three, response
+        final_kernel, (f32(16, 16, 16), f32(2, 16, 16, 128)), pair[0], last, response
     )
     return response, density
 

time: 67.6 us -> 66.5 us (0.984)
  starting transfers between devices: 25.6 us -> 24.4 us
    ppermute x8 -> x7, starting transfers between devices: 15.2 us -> 10.6 us  [partner(): lax.ppermute(value, 'bands', [(i, i ^ steps[i % len(steps)]) for i in ran...]
    ppermute x4, waiting for transfers between devices: 10.8 us -> 7.2 us  [the longest x2 7.2 us: exchange_z(): lax.ppermute(tail, 'gz', ring('gz', 1))]
    ppermute x4, starting transfers between devices: 6.02 us -> 9.45 us  [the longest x2 8.4 us: exchange_z(): lax.ppermute(head, 'gz', ring('gz', -1))]
    ppermute x8 -> x7, waiting for transfers between devices: 13.3 us -> 16.6 us  [partner(): lax.ppermute(value, 'bands', [(i, i ^ steps[i % len(steps)]) for i in ran...]
  transfers between devices with their start and end apart: 16 -> 15, of which waited for: 14 -> 13; matrix products, arithmetic and copies ran while one was open for 0% -> 0% of each run, Pallas kernels for 0% -> 0%
where the time goes in v6:
time: 66.5 us; the launch traced here: 66 us
  waiting for transfers between devices  34.4 us (52%)
  starting transfers between devices  24.4 us (37%)
  Pallas kernels  5.1 us (8%)
  local copies, waits for them, and re-layouts  1.09 us (2%)
  between operations  0.86 us (1%)
    ppermute x7, waiting for transfers between devices, partner(): lax.ppermute(value, 'bands', [(i, i ^ steps[i % len(steps)]) for i in ran...  16.6 us
    ppermute x7, starting transfers between devices, partner(): lax.ppermute(value, 'bands', [(i, i ^ steps[i % len(steps)]) for i in ran...  10.6 us
    ppermute x2, starting transfers between devices, exchange_z(): lax.ppermute(head, 'gz', ring('gz', -1))  8.4 us
    ppermute x2, waiting for transfers between devices, exchange_z(): lax.ppermute(tail, 'gz', ring('gz', 1))  7.2 us
    ppermute x2, waiting for transfers between devices, exchange_y(): lax.ppermute(up, 'gy', ring('gy', 1))  5.86 us
    pallas_call x7, Pallas kernels, call(): pl.pallas_call(body, out_shape=outs, in_specs=[VMEM] * (len(args) - smem)...  5.1 us
    ppermute x2, waiting for transfers between devices, exchange_y(): lax.ppermute(down, 'gy', ring('gy', -1))  4.73 us
    ppermute x2, starting transfers between devices, exchange_y(): lax.ppermute(up, 'gy', ring('gy', 1))  2.5 us
  transfers between devices with their start and end apart: 15, of which 13 were waited for; matrix products, arithmetic and copies ran while one was open for 0% of the time, Pallas kernels for 0%

profile of v6, /device:TPU:6, one launch (start us, length us, event | category | flops | bytes accessed | tf_op | source)
XLA Modules:
  0.0 66.0 jit_solution(9283478099819805342)
XLA Ops:
  0.6 0.9 %slice_bitcast_fusion = (f32[4,16,128]{2,1,0:T(8,128)S(1)}, f32[4,16,128]{2,1,0:T(8,128)S(1)}, f32[4,16,128]{2,1,0:T(8,128)S(1)}, f32[4,16,128]{2,1,0:T(8,128)S(1)}) fusion(f32[2,16,16,128]{3,2,1,0:T(8,128)} %orb_ref.5), kind=kLoop, calls=%fused_computation.7 | loop fusion | bytes 262144 | tf_op jit(solution)/shard_map/slice | solution.py:248
  1.5 0.1 copy-done.5
  1.7 2.3 %collective-permute-start = (f32[3,4,16,128]{3,2,1,0:T(8,128)S(1)}, f32[3,4,16,128]{3,2,1,0:T(8,128)S(1)}, u32[]{:S(2)}, u32[]{:S(2)}) collective-permute-start(f32[3,4,16,128]{3,2,1,0:T(8,128)S(1)} %get-tuple-element.34), channel_id=1, source_target_pairs={{0,8},{8,16},{16,24},{24,0},{1,9},{9,17},{17,25},{25,1},{2,10},{10... | collective-permute-start | bytes 294920 | tf_op jit(solution)/shard_map/ppermute | solution.py:226
  4.1 2.3 %collective-permute-done.lo_ref = f32[3,4,16,128]{3,2,1,0:T(8,128)S(1)} collective-permute-done((f32[3,4,16,128]{3,2,1,0:T(8,128)S(1)}, f32[3,4,16,128]{3,2,1,0:T(8,128)S(1)}, u32[]{:S(2)}, u32[]{:S(2)}) %collective-permute-start) | collective-permute-done | bytes 98336 | tf_op jit(solution)/shard_map/ppermute | solution.py:226
  6.4 3.4 %collective-permute-done.1.hi_ref = f32[3,4,16,128]{3,2,1,0:T(8,128)S(1)} collective-permute-done((f32[3,4,16,128]{3,2,1,0:T(8,128)S(1)}, f32[3,4,16,128]{3,2,1,0:T(8,128)S(1)}, u32[]{:S(2)}, u32[]{:S(2)}) %collective-permute-start.1) | collective-permute-done | bytes 98336 | tf_op jit(solution)/shard_map/ppermute | solution.py:226
  9.9 0.1 collective-permute-start.2
  10.0 4.1 %collective-permute-start.3 = (f32[3,12,8,128]{3,2,1,0:T(8,128)S(1)}, f32[3,12,8,128]{3,2,1,0:T(8,128)S(1)}, u32[]{:S(2)}, u32[]{:S(2)}) collective-permute-start(f32[3,12,8,128]{3,2,1,0:T(8,128)S(1)} %get-tuple-element.37), channel_id=1, source_target_pairs={{0,7},{1,0},{2,1},{3,2},{4,3},{5,4},{6,5},{7,6},{8,15},{9,8},{10,9... | collective-permute-start | bytes 442376 | tf_op jit(solution)/shard_map/ppermute | solution.py:233
  14.1 3.1 %collective-permute-done.2.below_ref = f32[3,12,8,128]{3,2,1,0:T(8,128)S(1)} collective-permute-done((f32[3,12,8,128]{3,2,1,0:T(8,128)S(1)}, f32[3,12,8,128]{3,2,1,0:T(8,128)S(1)}, u32[]{:S(2)}, u32[]{:S(2)}) %collective-permute-start.2) | collective-permute-done | bytes 147488 | tf_op jit(solution)/shard_map/ppermute | solution.py:233
  17.2 1.8 %shard_map.79 = (f32[2,16,16,128]{3,2,1,0:T(8,128)S(1)}, f32[16,16,128]{2,1,0:T(8,128)S(1)}, f32[2,24,24,128]{3,2,1,0:T(8,128)S(1)}) custom-call(f32[3,16,16,128]{3,2,1,0:T(8,128)S(1)} %pad_maximum_fusion.centre_ref, f32[3,4,16,128]{3,2,1,0:T(8,128)S(1)} %collective-permute-done.lo_ref, f32[3,4,16,128]{3,2,1,0:T(8,128)S(1)} %collective-permute-done.1.hi_ref, ...), custom_call_target="tpu_custom_call" | custom-call | tf_op jit(solution)/shard_map/pallas_call | solution.py:15
  19.0 0.1 collective-permute-start.4
  19.1 1.2 %collective-permute-done.4 = f32[8,16,128]{2,1,0:T(8,128)S(1)} collective-permute-done((f32[8,16,128]{2,1,0:T(8,128)S(1)}, f32[8,16,128]{2,1,0:T(8,128)S(1)}, u32[]{:S(2)}, u32[]{:S(2)}) %collective-permute-start.4) | collective-permute-done | bytes 65568 | tf_op jit(solution)/shard_map/ppermute | solution.py:238
  20.4 1.9 %collective-permute-start.5 = (f32[8,16,128]{2,1,0:T(8,128)S(1)}, f32[8,16,128]{2,1,0:T(8,128)S(1)}, u32[]{:S(2)}, u32[]{:S(2)}) collective-permute-start(f32[8,16,128]{2,1,0:T(8,128)S(1)} %dynamic-slice_add_fusion), channel_id=1, source_target_pairs={{0,64},{32,224},{64,0},{96,160},{128,192},{160,96},{192,128},{224,... | collective-permute-start | bytes 196616 | tf_op jit(solution)/shard_map/ppermute | solution.py:238
  22.2 4.1 %collective-permute-done.5 = f32[8,16,128]{2,1,0:T(8,128)S(1)} collective-permute-done((f32[8,16,128]{2,1,0:T(8,128)S(1)}, f32[8,16,128]{2,1,0:T(8,128)S(1)}, u32[]{:S(2)}, u32[]{:S(2)}) %collective-permute-start.5) | collective-permute-done | bytes 65568 | tf_op jit(solution)/shard_map/ppermute | solution.py:238
  26.3 4.1 %collective-permute-start.6 = (f32[8,16,128]{2,1,0:T(8,128)S(1)}, f32[8,16,128]{2,1,0:T(8,128)S(1)}, u32[]{:S(2)}, u32[]{:S(2)}) collective-permute-start(f32[8,16,128]{2,1,0:T(8,128)S(1)} %add.54), channel_id=1, source_target_pairs={{0,192},{32,96},{64,128},{96,32},{128,64},{160,224},{192,0},{224,1... | collective-permute-start | bytes 196616 | tf_op jit(solution)/shard_map/ppermute | solution.py:238
  30.4 2.5 %collective-permute-done.6 = f32[8,16,128]{2,1,0:T(8,128)S(1)} collective-permute-done((f32[8,16,128]{2,1,0:T(8,128)S(1)}, f32[8,16,128]{2,1,0:T(8,128)S(1)}, u32[]{:S(2)}, u32[]{:S(2)}) %collective-permute-start.6) | collective-permute-done | bytes 65568 | tf_op jit(solution)/shard_map/ppermute | solution.py:238
  32.9 0.1 collective-permute-start.7
  33.0 1.2 %collective-permute-done.7.other_ref = f32[8,16,128]{2,1,0:T(8,128)S(1)} collective-permute-done((f32[8,16,128]{2,1,0:T(8,128)S(1)}, f32[8,16,128]{2,1,0:T(8,128)S(1)}, u32[]{:S(2)}, u32[]{:S(2)}) %collective-permute-start.7) | collective-permute-done | bytes 65568 | tf_op jit(solution)/shard_map/ppermute | solution.py:238
  34.3 0.2 collective-permute-start.8
  34.5 1.9 %collective-permute-start.9 = (f32[4,4,16,128]{3,2,1,0:T(8,128)S(1)}, f32[4,4,16,128]{3,2,1,0:T(8,128)S(1)}, u32[]{:S(2)}, u32[]{:S(2)}) collective-permute-start(f32[4,4,16,128]{3,2,1,0:T(8,128)S(1)} %get-tuple-element.42), channel_id=1, source_target_pairs={{0,24},{8,0},{16,8},{24,16},{1,25},{9,1},{17,9},{25,17},{2,26},{10... | collective-permute-start | bytes 393224 | tf_op jit(solution)/shard_map/ppermute | solution.py:226
  36.4 3.5 %collective-permute-done.8.lo_ref = f32[4,4,16,128]{3,2,1,0:T(8,128)S(1)} collective-permute-done((f32[4,4,16,128]{3,2,1,0:T(8,128)S(1)}, f32[4,4,16,128]{3,2,1,0:T(8,128)S(1)}, u32[]{:S(2)}, u32[]{:S(2)}) %collective-permute-start.8) | collective-permute-done | bytes 131104 | tf_op jit(solution)/shard_map/ppermute | solution.py:226
  39.9 1.3 %collective-permute-done.9.hi_ref = f32[4,4,16,128]{3,2,1,0:T(8,128)S(1)} collective-permute-done((f32[4,4,16,128]{3,2,1,0:T(8,128)S(1)}, f32[4,4,16,128]{3,2,1,0:T(8,128)S(1)}, u32[]{:S(2)}, u32[]{:S(2)}) %collective-permute-start.9) | collective-permute-done | bytes 131104 | tf_op jit(solution)/shard_map/ppermute | solution.py:226
  41.3 1.0 %collective-permute-start.10 = (f32[4,12,8,128]{3,2,1,0:T(8,128)S(1)}, f32[4,12,8,128]{3,2,1,0:T(8,128)S(1)}, u32[]{:S(2)}, u32[]{:S(2)}) collective-permute-start(f32[4,12,8,128]{3,2,1,0:T(8,128)S(1)} %get-tuple-element.43), channel_id=1, source_target_pairs={{0,1},{1,2},{2,3},{3,4},{4,5},{5,6},{6,7},{7,0},{8,9},{9,10},{10,1... | collective-permute-start | bytes 589832 | tf_op jit(solution)/shard_map/ppermute | solution.py:233
  42.2 4.3 %collective-permute-start.11 = (f32[4,12,8,128]{3,2,1,0:T(8,128)S(1)}, f32[4,12,8,128]{3,2,1,0:T(8,128)S(1)}, u32[]{:S(2)}, u32[]{:S(2)}) collective-permute-start(f32[4,12,8,128]{3,2,1,0:T(8,128)S(1)} %get-tuple-element.44), channel_id=1, source_target_pairs={{0,7},{1,0},{2,1},{3,2},{4,3},{5,4},{6,5},{7,6},{8,15},{9,8},{10,9... | collective-permute-start | bytes 589832 | tf_op jit(solution)/shard_map/ppermute | solution.py:233
  46.5 4.1 %collective-permute-done.10.below_ref = f32[4,12,8,128]{3,2,1,0:T(8,128)S(1)} collective-permute-done((f32[4,12,8,128]{3,2,1,0:T(8,128)S(1)}, f32[4,12,8,128]{3,2,1,0:T(8,128)S(1)}, u32[]{:S(2)}, u32[]{:S(2)}) %collective-permute-start.10) | collective-permute-done | bytes 196640 | tf_op jit(solution)/shard_map/ppermute | solution.py:233
  50.6 2.4 %shard_map.82 = (f32[2,16,16,128]{3,2,1,0:T(8,128)S(1)}, f32[8,4,8,128]{3,2,1,0:T(8,128)S(1)}) custom-call(f32[4,16,16,128]{3,2,1,0:T(8,128)S(1)} %get-tuple-element.40.centre_ref, f32[4,4,16,128]{3,2,1,0:T(8,128)S(1)} %collective-permute-done.8.lo_ref, f32[4,4,16,128]{3,2,1,0:T(8,128)S(1)} %collective-permute-done.9.hi_ref, ...), custom_call_target="tpu_custom_call" | custom-call | tf_op jit(solution)/shard_map/pallas_call | solution.py:15
  53.0 0.1 collective-permute-start.12
  53.2 1.2 %collective-permute-done.12 = f32[4,4,8,128]{3,2,1,0:T(8,128)S(1)} collective-permute-done((f32[4,4,8,128]{3,2,1,0:T(8,128)S(1)}, f32[4,4,8,128]{3,2,1,0:T(8,128)S(1)}, u32[]{:S(2)}, u32[]{:S(2)}) %collective-permute-start.12) | collective-permute-done | bytes 65568 | tf_op jit(solution)/shard_map/ppermute | solution.py:238
  54.4 0.7 %collective-permute-start.13 = (f32[2,4,8,128]{3,2,1,0:T(8,128)S(1)}, f32[2,4,8,128]{3,2,1,0:T(8,128)S(1)}, u32[]{:S(2)}, u32[]{:S(2)}) collective-permute-start(f32[2,4,8,128]{3,2,1,0:T(8,128)S(1)} %pad_maximum_fusion.1), channel_id=1, source_target_pairs={{0,64},{32,224},{64,0},{96,160},{128,192},{160,96},{192,128},{224,... | collective-permute-start | bytes 98312 | tf_op jit(solution)/shard_map/ppermute | solution.py:238
  55.1 4.2 %collective-permute-done.13 = f32[2,4,8,128]{3,2,1,0:T(8,128)S(1)} collective-permute-done((f32[2,4,8,128]{3,2,1,0:T(8,128)S(1)}, f32[2,4,8,128]{3,2,1,0:T(8,128)S(1)}, u32[]{:S(2)}, u32[]{:S(2)}) %collective-permute-start.13) | collective-permute-done | bytes 32800 | tf_op jit(solution)/shard_map/ppermute | solution.py:238
  59.3 3.7 %collective-permute-start.14 = (f32[4,8,128]{2,1,0:T(8,128)S(1)}, f32[4,8,128]{2,1,0:T(8,128)S(1)}, u32[]{:S(2)}, u32[]{:S(2)}) collective-permute-start(f32[4,8,128]{2,1,0:T(8,128)S(1)} %get-tuple-element.62), channel_id=1, source_target_pairs={{0,192},{32,96},{64,128},{96,32},{128,64},{160,224},{192,0},{224,1... | collective-permute-start | bytes 49160 | tf_op jit(solution)/shard_map/ppermute | solution.py:238
  63.0 2.3 %collective-permute-done.14.last_ref = f32[4,8,128]{2,1,0:T(8,128)S(1)} collective-permute-done((f32[4,8,128]{2,1,0:T(8,128)S(1)}, f32[4,8,128]{2,1,0:T(8,128)S(1)}, u32[]{:S(2)}, u32[]{:S(2)}) %collective-permute-start.14) | collective-permute-done | bytes 16416 | tf_op jit(solution)/shard_map/ppermute | solution.py:238
  65.3 0.8 %shard_map.83 = (f32[16,16,16]{2,1,0:T(8,128)}, f32[2,16,16,128]{3,2,1,0:T(8,128)}) custom-call(f32[4,8,128]{2,1,0:T(8,128)S(1)} %get-tuple-element.63.own_ref, f32[4,8,128]{2,1,0:T(8,128)S(1)} %collective-permute-done.14.last_ref, f32[2,16,16,128]{3,2,1,0:T(8,128)S(1)} %get-tuple-element.47.resp_ref), custom_call_target="tpu_custom_call" | custom-call | tf_op jit(solution)/shard_map/pallas_call | solution.py:15
  (31 shorter events, 0.4 us)
Async XLA Ops:
  0.6 0.9 %copy-start.1 = (f32[16,16,128]{2,1,0:T(8,128)S(1)}, f32[16,16,128]{2,1,0:T(8,128)}, u32[]{:S(2)}) copy-start(f32[16,16,128]{2,1,0:T(8,128)} %pert_ref.1) | copy-start | bytes 393220
  0.6 1.0 %copy-start.5 = (f32[16,16,128]{2,1,0:T(8,128)S(1)}, f32[16,16,128]{2,1,0:T(8,128)}, u32[]{:S(2)}) copy-start(f32[16,16,128]{2,1,0:T(8,128)} %param.9) | copy-start | bytes 393220
  1.7 2.3 %copy-start = (f32[2,16,16,128]{3,2,1,0:T(8,128)S(1)}, f32[2,16,16,128]{3,2,1,0:T(8,128)}, u32[]{:S(2)}) copy-start(f32[2,16,16,128]{3,2,1,0:T(8,128)} %orb_ref.5) | copy-start | bytes 786436
  1.7 4.7 %collective-permute-start = (f32[3,4,16,128]{3,2,1,0:T(8,128)S(1)}, f32[3,4,16,128]{3,2,1,0:T(8,128)S(1)}, u32[]{:S(2)}, u32[]{:S(2)}) collective-permute-start(f32[3,4,16,128]{3,2,1,0:T(8,128)S(1)} %get-tuple-element.34), channel_id=1, source_target_pairs={{0,8},{8,16},{16,24},{24,0},{1,9},{9,17},{17,25},{25,1},{2,10},{10... | collective-permute-start | bytes 294920 | tf_op jit(solution)/shard_map/ppermute | solution.py:226
  4.0 5.8 %collective-permute-start.1 = (f32[3,4,16,128]{3,2,1,0:T(8,128)S(1)}, f32[3,4,16,128]{3,2,1,0:T(8,128)S(1)}, u32[]{:S(2)}, u32[]{:S(2)}) collective-permute-start(f32[3,4,16,128]{3,2,1,0:T(8,128)S(1)} %get-tuple-element.35), channel_id=1, source_target_pairs={{0,24},{8,0},{16,8},{24,16},{1,25},{9,1},{17,9},{25,17},{2,26},{10... | collective-permute-start | bytes 294920 | tf_op jit(solution)/shard_map/ppermute | solution.py:226
  9.9 7.3 %collective-permute-start.2 = (f32[3,12,8,128]{3,2,1,0:T(8,128)S(1)}, f32[3,12,8,128]{3,2,1,0:T(8,128)S(1)}, u32[]{:S(2)}, u32[]{:S(2)}) collective-permute-start(f32[3,12,8,128]{3,2,1,0:T(8,128)S(1)} %get-tuple-element.36), channel_id=1, source_target_pairs={{0,1},{1,2},{2,3},{3,4},{4,5},{5,6},{6,7},{7,0},{8,9},{9,10},{10,1... | collective-permute-start | bytes 442376 | tf_op jit(solution)/shard_map/ppermute | solution.py:233
  10.0 7.2 %collective-permute-start.3 = (f32[3,12,8,128]{3,2,1,0:T(8,128)S(1)}, f32[3,12,8,128]{3,2,1,0:T(8,128)S(1)}, u32[]{:S(2)}, u32[]{:S(2)}) collective-permute-start(f32[3,12,8,128]{3,2,1,0:T(8,128)S(1)} %get-tuple-element.37), channel_id=1, source_target_pairs={{0,7},{1,0},{2,1},{3,2},{4,3},{5,4},{6,5},{7,6},{8,15},{9,8},{10,9... | collective-permute-start | bytes 442376 | tf_op jit(solution)/shard_map/ppermute | solution.py:233
  14.1 3.1 %copy-start.3 = (f32[2]{0:T(128)S(1)}, f32[2]{0:T(128)}, u32[]{:S(2)}) copy-start(f32[2]{0:T(128)} %occ_ref.3) | copy-start | bytes 28
  14.1 3.1 %copy-start.4 = (f32[2]{0:T(128)S(1)}, f32[2]{0:T(128)}, u32[]{:S(2)}) copy-start(f32[2]{0:T(128)} %shift_ref.1) | copy-start | bytes 28
  19.0 1.3 %collective-permute-start.4 = (f32[8,16,128]{2,1,0:T(8,128)S(1)}, f32[8,16,128]{2,1,0:T(8,128)S(1)}, u32[]{:S(2)}, u32[]{:S(2)}) collective-permute-start(f32[8,16,128]{2,1,0:T(8,128)S(1)} %constant_dynamic-slice_fusion.4), channel_id=1, source_target_pairs={{0,32},{32,0},{64,96},{96,64},{128,160},{160,128},{192,224},{224,1... | collective-permute-start | bytes 196616 | tf_op jit(solution)/shard_map/ppermute | solution.py:238
  20.4 5.9 %collective-permute-start.5 = (f32[8,16,128]{2,1,0:T(8,128)S(1)}, f32[8,16,128]{2,1,0:T(8,128)S(1)}, u32[]{:S(2)}, u32[]{:S(2)}) collective-permute-start(f32[8,16,128]{2,1,0:T(8,128)S(1)} %dynamic-slice_add_fusion), channel_id=1, source_target_pairs={{0,64},{32,224},{64,0},{96,160},{128,192},{160,96},{192,128},{224,... | collective-permute-start | bytes 196616 | tf_op jit(solution)/shard_map/ppermute | solution.py:238
  26.3 7.9 %copy-start.2 = (f32[16,16,128]{2,1,0:T(8,128)S(1)}, f32[16,16,128]{2,1,0:T(8,128)}, u32[]{:S(2)}) copy-start(f32[16,16,128]{2,1,0:T(8,128)} %kern_ref.1) | copy-start | bytes 393220
  26.3 6.5 %collective-permute-start.6 = (f32[8,16,128]{2,1,0:T(8,128)S(1)}, f32[8,16,128]{2,1,0:T(8,128)S(1)}, u32[]{:S(2)}, u32[]{:S(2)}) collective-permute-start(f32[8,16,128]{2,1,0:T(8,128)S(1)} %add.54), channel_id=1, source_target_pairs={{0,192},{32,96},{64,128},{96,32},{128,64},{160,224},{192,0},{224,1... | collective-permute-start | bytes 196616 | tf_op jit(solution)/shard_map/ppermute | solution.py:238
  32.9 1.3 %collective-permute-start.7 = (f32[8,16,128]{2,1,0:T(8,128)S(1)}, f32[8,16,128]{2,1,0:T(8,128)S(1)}, u32[]{:S(2)}, u32[]{:S(2)}) collective-permute-start(f32[8,16,128]{2,1,0:T(8,128)S(1)} %add.55.own_ref), channel_id=1, source_target_pairs={{0,32},{32,0},{64,96},{96,64},{128,160},{160,128},{192,224},{224,1... | collective-permute-start | bytes 196616 | tf_op jit(solution)/shard_map/ppermute | solution.py:238
  34.3 5.6 %collective-permute-start.8 = (f32[4,4,16,128]{3,2,1,0:T(8,128)S(1)}, f32[4,4,16,128]{3,2,1,0:T(8,128)S(1)}, u32[]{:S(2)}, u32[]{:S(2)}) collective-permute-start(f32[4,4,16,128]{3,2,1,0:T(8,128)S(1)} %get-tuple-element.41), channel_id=1, source_target_pairs={{0,8},{8,16},{16,24},{24,0},{1,9},{9,17},{17,25},{25,1},{2,10},{10... | collective-permute-start | bytes 393224 | tf_op jit(solution)/shard_map/ppermute | solution.py:226
  34.5 6.7 %collective-permute-start.9 = (f32[4,4,16,128]{3,2,1,0:T(8,128)S(1)}, f32[4,4,16,128]{3,2,1,0:T(8,128)S(1)}, u32[]{:S(2)}, u32[]{:S(2)}) collective-permute-start(f32[4,4,16,128]{3,2,1,0:T(8,128)S(1)} %get-tuple-element.42), channel_id=1, source_target_pairs={{0,24},{8,0},{16,8},{24,16},{1,25},{9,1},{17,9},{25,17},{2,26},{10... | collective-permute-start | bytes 393224 | tf_op jit(solution)/shard_map/ppermute | solution.py:226
  41.3 9.3 %collective-permute-start.10 = (f32[4,12,8,128]{3,2,1,0:T(8,128)S(1)}, f32[4,12,8,128]{3,2,1,0:T(8,128)S(1)}, u32[]{:S(2)}, u32[]{:S(2)}) collective-permute-start(f32[4,12,8,128]{3,2,1,0:T(8,128)S(1)} %get-tuple-element.43), channel_id=1, source_target_pairs={{0,1},{1,2},{2,3},{3,4},{4,5},{5,6},{6,7},{7,0},{8,9},{9,10},{10,1... | collective-permute-start | bytes 589832 | tf_op jit(solution)/shard_map/ppermute | solution.py:233
  42.2 8.4 %collective-permute-start.11 = (f32[4,12,8,128]{3,2,1,0:T(8,128)S(1)}, f32[4,12,8,128]{3,2,1,0:T(8,128)S(1)}, u32[]{:S(2)}, u32[]{:S(2)}) collective-permute-start(f32[4,12,8,128]{3,2,1,0:T(8,128)S(1)} %get-tuple-element.44), channel_id=1, source_target_pairs={{0,7},{1,0},{2,1},{3,2},{4,3},{5,4},{6,5},{7,6},{8,15},{9,8},{10,9... | collective-permute-start | bytes 589832 | tf_op jit(solution)/shard_map/ppermute | solution.py:233
  53.0 1.3 %collective-permute-start.12 = (f32[4,4,8,128]{3,2,1,0:T(8,128)S(1)}, f32[4,4,8,128]{3,2,1,0:T(8,128)S(1)}, u32[]{:S(2)}, u32[]{:S(2)}) collective-permute-start(f32[4,4,8,128]{3,2,1,0:T(8,128)S(1)} %dynamic-slice_bitcast_fusion), channel_id=1, source_target_pairs={{0,32},{32,0},{64,96},{96,64},{128,160},{160,128},{192,224},{224,1... | collective-permute-start | bytes 196616 | tf_op jit(solution)/shard_map/ppermute | solution.py:238
  54.4 4.9 %collective-permute-start.13 = (f32[2,4,8,128]{3,2,1,0:T(8,128)S(1)}, f32[2,4,8,128]{3,2,1,0:T(8,128)S(1)}, u32[]{:S(2)}, u32[]{:S(2)}) collective-permute-start(f32[2,4,8,128]{3,2,1,0:T(8,128)S(1)} %pad_maximum_fusion.1), channel_id=1, source_target_pairs={{0,64},{32,224},{64,0},{96,160},{128,192},{160,96},{192,128},{224,... | collective-permute-start | bytes 98312 | tf_op jit(solution)/shard_map/ppermute | solution.py:238
  59.3 5.9 %collective-permute-start.14 = (f32[4,8,128]{2,1,0:T(8,128)S(1)}, f32[4,8,128]{2,1,0:T(8,128)S(1)}, u32[]{:S(2)}, u32[]{:S(2)}) collective-permute-start(f32[4,8,128]{2,1,0:T(8,128)S(1)} %get-tuple-element.62), channel_id=1, source_target_pairs={{0,192},{32,96},{64,128},{96,32},{128,64},{160,224},{192,0},{224,1... | collective-permute-start | bytes 49160 | tf_op jit(solution)/shard_map/ppermute | solution.py:238

commit v7 on v6

--- a/solution.py
+++ b/solution.py
@@ -55,17 +55,19 @@
 
 
 def assemble(row, above_ref, below_ref, field, dest_ref, at):
-    low = low_half()
     for r in range(24):
-        dest_ref[at, r, 0:16] = row(r)
+        dest_ref[at, r, 8:24] = row(r)
     for j in range(12):
         above, below = above_ref[field, j], below_ref[field, j]
-        dest_ref[at, j, 16:24] = jnp.where(low, above, below)
-        dest_ref[at, j + 12, 16:24] = pltpu.roll(jnp.where(low, below, above), 4, 0)
-
-
-def shifts_z(u):
-    return pltpu.roll(u, 1, u.ndim - 2) + pltpu.roll(u, 23, u.ndim - 2)
+        dest_ref[at, j, 24:32] = above
+        dest_ref[at, j, 0:8] = below
+        dest_ref[at, j + 12, 24:32] = pltpu.roll(above, 4, 0)
+        dest_ref[at, j + 12, 0:8] = pltpu.roll(below, 4, 0)
+
+
+def window(zero, last=False):
+    first, count = (8, 16) if last else (4, 24)
+    return [pl.ds(zero + first + k, count) for k in (0, -1, 1)]
 
 
 def shifts_x(u):
@@ -80,21 +82,24 @@
         before, at = at, after
 
 
-def sources(p_ref, scale_ref, sc_ref, o):
+def sources(p_ref, scale_ref, sc_ref, o, zero):
+    here, down, up = window(zero)
+
     def load(r):
-        return p_ref[o, r]
+        return p_ref[o, r, here]
 
     def emit(r, before, at, after):
-        faces = shifts_x(at) + shifts_z(at) + (before + after)
-        sc_ref[o, r] = scale_ref[o, r] * (-30.0 * at - 5.0 * faces)
+        faces = shifts_x(at) + (p_ref[o, r, down] + p_ref[o, r, up]) + (before + after)
+        sc_ref[o, r, here] = scale_ref[o, r, here] * (-30.0 * at - 5.0 * faces)
 
     by_rows(1, 23, load, emit)
 
 
-def sweep(src_ref, scale_ref, sc_ref, o, margin, store):
+def sweep(src_ref, scale_ref, sc_ref, o, zero, margin, store):
+    here, down, up = window(zero, margin == 4)
+
     def load(r):
-        u = src_ref[o, r]
-        return u, shifts_z(u)
+        return src_ref[o, r, here], src_ref[o, r, down] + src_ref[o, r, up]
 
     def emit(r, before, at, after):
         u, along_z = at
@@ -102,34 +107,36 @@
         m = before[0] + after[0] + along_z
         n = 3.0 * m + across
         total = shifts_x(14.0 * u + n) + (3.0 * n + 5.0 * m)
-        store(r, 0.2 * u + sc_ref[o, r] + scale_ref[o, r] * total)
+        store(r, 0.2 * u + sc_ref[o, r, here] + scale_ref[o, r, here] * total)
 
     by_rows(margin, 24 - margin, load, emit)
 
 
-def into(dest_ref, o):
+def into(dest_ref, o, zero):
+    here = window(zero)[0]
+
     def store(r, new):
-        dest_ref[o, r] = new
+        dest_ref[o, r, here] = new
 
     return store
 
 
-def last_sweep(src_ref, scale_ref, sc_ref, o, orb_ref, occ_ref, resp_ref, dens_ref):
+def last_sweep(src_ref, scale_ref, sc_ref, o, zero, orb_ref, occ_ref, resp_ref, dens_ref):
     occupation = occ_ref[o]
 
     def store(r, new):
-        own = new[:16]
-        resp_ref[o, r - 4] = own
-        term = occupation * orb_ref[o, r - 4] * own
+        resp_ref[o, r - 4] = new
+        term = occupation * orb_ref[o, r - 4] * new
         dens_ref[r - 4] = term if o == 0 else dens_ref[r - 4] + term
 
-    sweep(src_ref, scale_ref, sc_ref, o, 4, store)
+    sweep(src_ref, scale_ref, sc_ref, o, zero, 4, store)
 
 
 def first_kernel(
-    centre_ref, lo_ref, hi_ref, below_ref, above_ref, orb_ref, shift_ref, occ_ref,
+    centre_ref, lo_ref, hi_ref, below_ref, above_ref, orb_ref, shift_ref, occ_ref, zero_ref,
     resp_ref, dens_ref, scale_ref, p_ref, sc_ref, a_ref, b_ref,
 ):
+    zero = zero_ref[0]
     for field in range(2):
         assemble(padded_row(centre_ref, lo_ref, hi_ref, field), above_ref, below_ref, field, p_ref, field)
     assemble(padded_row(centre_ref, lo_ref, hi_ref, 2), above_ref, below_ref, 2, a_ref, 0)
@@ -137,13 +144,13 @@
         base = 32.0 / 15.0 + shift_ref[o]
 
         for r in range(1, 23):
-            scale_ref[o, r] = (RELAX / 60.0) / (base + a_ref[0, r])
-    for o in range(2):
-        sources(p_ref, scale_ref, sc_ref, o)
-    for o in range(2):
-        sweep(sc_ref, scale_ref, sc_ref, o, 2, into(a_ref, o))
-        sweep(a_ref, scale_ref, sc_ref, o, 3, into(b_ref, o))
-        last_sweep(b_ref, scale_ref, sc_ref, o, orb_ref, occ_ref, resp_ref, dens_ref)
+            scale_ref[o, r, 0:32] = (RELAX / 60.0) / (base + a_ref[0, r, 0:32])
+    for o in range(2):
+        sources(p_ref, scale_ref, sc_ref, o, zero)
+    for o in range(2):
+        sweep(sc_ref, scale_ref, sc_ref, o, zero, 2, into(a_ref, o, zero))
+        sweep(a_ref, scale_ref, sc_ref, o, zero, 3, into(b_ref, o, zero))
+        last_sweep(b_ref, scale_ref, sc_ref, o, zero, orb_ref, occ_ref, resp_ref, dens_ref)
 
 
 def strips_kernel(*refs):
@@ -188,18 +195,19 @@
 
 
 def second_kernel(
-    centre_ref, lo_ref, hi_ref, below_ref, above_ref, scale_ref, orb_ref, occ_ref,
+    centre_ref, lo_ref, hi_ref, below_ref, above_ref, scale_ref, orb_ref, occ_ref, zero_ref,
     resp_ref, out_ref, p_ref, u_ref, sc_ref, a_ref, b_ref, dens_ref,
 ):
+    zero = zero_ref[0]
     for o in range(2):
         assemble(padded_row(centre_ref, lo_ref, hi_ref, o), above_ref, below_ref, o, p_ref, o)
         assemble(padded_row(centre_ref, lo_ref, hi_ref, 2 + o), above_ref, below_ref, 2 + o, u_ref, o)
     for o in range(2):
-        sources(p_ref, scale_ref, sc_ref, o)
-        sweep(u_ref, scale_ref, sc_ref, o, 1, into(a_ref, o))
-        sweep(a_ref, scale_ref, sc_ref, o, 2, into(b_ref, o))
-        sweep(b_ref, scale_ref, sc_ref, o, 3, into(a_ref, o))
-        last_sweep(a_ref, scale_ref, sc_ref, o, orb_ref, occ_ref, resp_ref, dens_ref)
+        sources(p_ref, scale_ref, sc_ref, o, zero)
+        sweep(u_ref, scale_ref, sc_ref, o, zero, 1, into(a_ref, o, zero))
+        sweep(a_ref, scale_ref, sc_ref, o, zero, 2, into(b_ref, o, zero))
+        sweep(b_ref, scale_ref, sc_ref, o, zero, 3, into(a_ref, o, zero))
+        last_sweep(a_ref, scale_ref, sc_ref, o, zero, orb_ref, occ_ref, resp_ref, dens_ref)
     for part in range(4):
         y, z = part // 2, 8 * (part % 2)
         blocks = swap_blocks([dens_ref[2 * k + y, z : z + 8] for k in range(8)])
@@ -241,8 +249,9 @@
 def on_device(orbitals, orbital_shift, occupation, potential, perturbation, kernel):
     group = lax.axis_index("bands")
     core, chip = group % 2, group // 2
-    padded = f32(2, 24, 24, 128)
-    wide = pltpu.VMEM((2, 24, 24, 128), jnp.float32)
+    padded = f32(2, 24, 32, 128)
+    wide = pltpu.VMEM((2, 24, 32, 128), jnp.float32)
+    zero = jnp.zeros((1,), jnp.int32)
 
     def ends(field):
         return field[12:16], field[0:4]
@@ -254,14 +263,14 @@
     above, below = exchange_z(centre, lo, hi)
     response, partial, scale = call(
         first_kernel, (f32(2, 16, 16, 128), f32(16, 16, 128), padded),
-        centre, lo, hi, below, above, orbitals, orbital_shift, occupation,
-        scratch=[wide] * 4, smem=2,
+        centre, lo, hi, below, above, orbitals, orbital_shift, occupation, zero,
+        scratch=[wide] * 4, smem=3,
     )
 
     own = lax.dynamic_slice_in_dim(partial, 8 * core, 8, 0)
     own = own + partner(lax.dynamic_slice_in_dim(partial, 8 * (1 - core), 8, 0), 1)
+    own = own + partner(own, 6, 2)
     own = own + partner(own, 2, 6)
-    own = own + partner(own, 6, 2)
     other = partner(own, 1)
     centre, up, down = call(
         change_kernel, (f32(4, 16, 16, 128), f32(4, 4, 16, 128), f32(4, 4, 16, 128)),
@@ -271,8 +280,8 @@
     above, below = exchange_z(centre, lo, hi)
     response, blocks = call(
         second_kernel, (f32(2, 16, 16, 128), f32(8, 4, 8, 128)),
-        centre, lo, hi, below, above, scale, orbitals, occupation,
-        scratch=[wide] * 5 + [pltpu.VMEM((16, 16, 128), jnp.float32)], smem=1,
+        centre, lo, hi, below, above, scale, orbitals, occupation, zero,
+        scratch=[wide] * 5 + [pltpu.VMEM((16, 16, 128), jnp.float32)], smem=2,
     )
 
     blocks = blocks.reshape(4, 2, 4, 8, 128)
@@ -282,9 +291,9 @@
     def block_of(step):
         return lax.dynamic_index_in_dim(kept, chip ^ step, 0, keepdims=False)
 
-    first, second = 1 + 2 * core, 3 - 2 * core
-    pair = jnp.stack([block_of(0), block_of(second)]) + partner(jnp.stack([block_of(first), block_of(2)]), 2, 6)
-    last = partner(pair[1], 6, 2)
+    first, second = 3 - 2 * core, 1 + 2 * core
+    pair = jnp.stack([block_of(0), block_of(second)]) + partner(jnp.stack([block_of(first), block_of(2)]), 6, 2)
+    last = partner(pair[1], 2, 6)
     density, response = call(
         final_kernel, (f32(16, 16, 16), f32(2, 16, 16, 128)), pair[0], last, response
     )

time: 66.5 us -> 65.8 us (0.989)
  waiting for transfers between devices: 34.4 us -> 33.1 us
  starting transfers between devices: 24.4 us -> 25.2 us
    ppermute x7, waiting for transfers between devices: 16.6 us -> 15.3 us  [partner(): lax.ppermute(value, 'bands', [(i, i ^ steps[i % len(steps)]) for i in ran...]
    ppermute x7, starting transfers between devices: 10.6 us -> 11.8 us  [partner(): lax.ppermute(value, 'bands', [(i, i ^ steps[i % len(steps)]) for i in ran...]
where the time goes in v7:
time: 65.8 us; the launch traced here: 65.3 us
  waiting for transfers between devices  33.1 us (50%)
  starting transfers between devices  25.2 us (38%)
  Pallas kernels  4.87 us (7%)
  local copies, waits for them, and re-layouts  1.09 us (2%)
  between operations  0.86 us (1%)
    ppermute x7, waiting for transfers between devices, partner(): lax.ppermute(value, 'bands', [(i, i ^ steps[i % len(steps)]) for i in ran...  15.3 us
    ppermute x7, starting transfers between devices, partner(): lax.ppermute(value, 'bands', [(i, i ^ steps[i % len(steps)]) for i in ran...  11.8 us
    ppermute x2, starting transfers between devices, exchange_z(): lax.ppermute(head, 'gz', ring('gz', -1))  7.81 us
    ppermute x2, waiting for transfers between devices, exchange_z(): lax.ppermute(tail, 'gz', ring('gz', 1))  7.2 us
    ppermute x2, waiting for transfers between devices, exchange_y(): lax.ppermute(up, 'gy', ring('gy', 1))  5.86 us
    pallas_call x7, Pallas kernels, call(): pl.pallas_call(body, out_shape=outs, in_specs=[VMEM] * (len(args) - smem)...  4.87 us
    ppermute x2, waiting for transfers between devices, exchange_y(): lax.ppermute(down, 'gy', ring('gy', -1))  4.73 us
    ppermute x2, starting transfers between devices, exchange_y(): lax.ppermute(up, 'gy', ring('gy', 1))  2.65 us
  transfers between devices with their start and end apart: 15, of which 13 were waited for; matrix products, arithmetic and copies ran while one was open for 0% of the time, Pallas kernels for 0%

profile of v7, /device:TPU:6, one launch (start us, length us, event | category | flops | bytes accessed | tf_op | source)
XLA Modules:
  0.0 65.3 jit_solution(2773629723404263984)
XLA Ops:
  0.6 0.9 %slice_bitcast_fusion = (f32[4,16,128]{2,1,0:T(8,128)S(1)}, f32[4,16,128]{2,1,0:T(8,128)S(1)}, f32[4,16,128]{2,1,0:T(8,128)S(1)}, f32[4,16,128]{2,1,0:T(8,128)S(1)}) fusion(f32[2,16,16,128]{3,2,1,0:T(8,128)} %orb_ref.5), kind=kLoop, calls=%fused_computation.7 | loop fusion | bytes 262144 | tf_op jit(solution)/shard_map/slice | solution.py:257
  1.5 0.1 copy-done.5
  1.7 2.3 %collective-permute-start = (f32[3,4,16,128]{3,2,1,0:T(8,128)S(1)}, f32[3,4,16,128]{3,2,1,0:T(8,128)S(1)}, u32[]{:S(2)}, u32[]{:S(2)}) collective-permute-start(f32[3,4,16,128]{3,2,1,0:T(8,128)S(1)} %get-tuple-element.34), channel_id=1, source_target_pairs={{0,8},{8,16},{16,24},{24,0},{1,9},{9,17},{17,25},{25,1},{2,10},{10... | collective-permute-start | bytes 294920 | tf_op jit(solution)/shard_map/ppermute | solution.py:234
  4.1 2.3 %collective-permute-done.lo_ref = f32[3,4,16,128]{3,2,1,0:T(8,128)S(1)} collective-permute-done((f32[3,4,16,128]{3,2,1,0:T(8,128)S(1)}, f32[3,4,16,128]{3,2,1,0:T(8,128)S(1)}, u32[]{:S(2)}, u32[]{:S(2)}) %collective-permute-start) | collective-permute-done | bytes 98336 | tf_op jit(solution)/shard_map/ppermute | solution.py:234
  6.4 3.4 %collective-permute-done.1.hi_ref = f32[3,4,16,128]{3,2,1,0:T(8,128)S(1)} collective-permute-done((f32[3,4,16,128]{3,2,1,0:T(8,128)S(1)}, f32[3,4,16,128]{3,2,1,0:T(8,128)S(1)}, u32[]{:S(2)}, u32[]{:S(2)}) %collective-permute-start.1) | collective-permute-done | bytes 98336 | tf_op jit(solution)/shard_map/ppermute | solution.py:234
  9.9 0.1 collective-permute-start.2
  10.0 4.1 %collective-permute-start.3 = (f32[3,12,8,128]{3,2,1,0:T(8,128)S(1)}, f32[3,12,8,128]{3,2,1,0:T(8,128)S(1)}, u32[]{:S(2)}, u32[]{:S(2)}) collective-permute-start(f32[3,12,8,128]{3,2,1,0:T(8,128)S(1)} %get-tuple-element.37), channel_id=1, source_target_pairs={{0,7},{1,0},{2,1},{3,2},{4,3},{5,4},{6,5},{7,6},{8,15},{9,8},{10,9... | collective-permute-start | bytes 442376 | tf_op jit(solution)/shard_map/ppermute | solution.py:241
  14.1 3.1 %collective-permute-done.2.below_ref = f32[3,12,8,128]{3,2,1,0:T(8,128)S(1)} collective-permute-done((f32[3,12,8,128]{3,2,1,0:T(8,128)S(1)}, f32[3,12,8,128]{3,2,1,0:T(8,128)S(1)}, u32[]{:S(2)}, u32[]{:S(2)}) %collective-permute-start.2) | collective-permute-done | bytes 147488 | tf_op jit(solution)/shard_map/ppermute | solution.py:241
  17.2 1.7 %shard_map.79 = (f32[2,16,16,128]{3,2,1,0:T(8,128)S(1)}, f32[16,16,128]{2,1,0:T(8,128)S(1)}, f32[2,24,32,128]{3,2,1,0:T(8,128)S(1)}) custom-call(f32[3,16,16,128]{3,2,1,0:T(8,128)S(1)} %pad_maximum_fusion.centre_ref, f32[3,4,16,128]{3,2,1,0:T(8,128)S(1)} %collective-permute-done.lo_ref, f32[3,4,16,128]{3,2,1,0:T(8,128)S(1)} %collective-permute-done.1.hi_ref, ...), custom_call_target="tpu_custom_call" | custom-call | tf_op jit(solution)/shard_map/pallas_call | solution.py:15
  18.9 0.1 collective-permute-start.4
  19.1 1.2 %collective-permute-done.4 = f32[8,16,128]{2,1,0:T(8,128)S(1)} collective-permute-done((f32[8,16,128]{2,1,0:T(8,128)S(1)}, f32[8,16,128]{2,1,0:T(8,128)S(1)}, u32[]{:S(2)}, u32[]{:S(2)}) %collective-permute-start.4) | collective-permute-done | bytes 65568 | tf_op jit(solution)/shard_map/ppermute | solution.py:246
  20.3 4.7 %collective-permute-start.5 = (f32[8,16,128]{2,1,0:T(8,128)S(1)}, f32[8,16,128]{2,1,0:T(8,128)S(1)}, u32[]{:S(2)}, u32[]{:S(2)}) collective-permute-start(f32[8,16,128]{2,1,0:T(8,128)S(1)} %dynamic-slice_add_fusion), channel_id=1, source_target_pairs={{0,192},{32,96},{64,128},{96,32},{128,64},{160,224},{192,0},{224,1... | collective-permute-start | bytes 196616 | tf_op jit(solution)/shard_map/ppermute | solution.py:246
  25.0 2.3 %collective-permute-done.5 = f32[8,16,128]{2,1,0:T(8,128)S(1)} collective-permute-done((f32[8,16,128]{2,1,0:T(8,128)S(1)}, f32[8,16,128]{2,1,0:T(8,128)S(1)}, u32[]{:S(2)}, u32[]{:S(2)}) %collective-permute-start.5) | collective-permute-done | bytes 65568 | tf_op jit(solution)/shard_map/ppermute | solution.py:246
  27.3 1.4 %collective-permute-start.6 = (f32[8,16,128]{2,1,0:T(8,128)S(1)}, f32[8,16,128]{2,1,0:T(8,128)S(1)}, u32[]{:S(2)}, u32[]{:S(2)}) collective-permute-start(f32[8,16,128]{2,1,0:T(8,128)S(1)} %add.54), channel_id=1, source_target_pairs={{0,64},{32,224},{64,0},{96,160},{128,192},{160,96},{192,128},{224,... | collective-permute-start | bytes 196616 | tf_op jit(solution)/shard_map/ppermute | solution.py:246
  28.8 3.9 %collective-permute-done.6 = f32[8,16,128]{2,1,0:T(8,128)S(1)} collective-permute-done((f32[8,16,128]{2,1,0:T(8,128)S(1)}, f32[8,16,128]{2,1,0:T(8,128)S(1)}, u32[]{:S(2)}, u32[]{:S(2)}) %collective-permute-start.6) | collective-permute-done | bytes 65568 | tf_op jit(solution)/shard_map/ppermute | solution.py:246
  32.7 0.1 collective-permute-start.7
  32.8 1.2 %collective-permute-done.7.other_ref = f32[8,16,128]{2,1,0:T(8,128)S(1)} collective-permute-done((f32[8,16,128]{2,1,0:T(8,128)S(1)}, f32[8,16,128]{2,1,0:T(8,128)S(1)}, u32[]{:S(2)}, u32[]{:S(2)}) %collective-permute-start.7) | collective-permute-done | bytes 65568 | tf_op jit(solution)/shard_map/ppermute | solution.py:246
  34.1 0.4 collective-permute-start.8
  34.5 1.7 %collective-permute-start.9 = (f32[4,4,16,128]{3,2,1,0:T(8,128)S(1)}, f32[4,4,16,128]{3,2,1,0:T(8,128)S(1)}, u32[]{:S(2)}, u32[]{:S(2)}) collective-permute-start(f32[4,4,16,128]{3,2,1,0:T(8,128)S(1)} %get-tuple-element.42), channel_id=1, source_target_pairs={{0,24},{8,0},{16,8},{24,16},{1,25},{9,1},{17,9},{25,17},{2,26},{10... | collective-permute-start | bytes 393224 | tf_op jit(solution)/shard_map/ppermute | solution.py:234
  36.2 3.5 %collective-permute-done.8.lo_ref = f32[4,4,16,128]{3,2,1,0:T(8,128)S(1)} collective-permute-done((f32[4,4,16,128]{3,2,1,0:T(8,128)S(1)}, f32[4,4,16,128]{3,2,1,0:T(8,128)S(1)}, u32[]{:S(2)}, u32[]{:S(2)}) %collective-permute-start.8) | collective-permute-done | bytes 131104 | tf_op jit(solution)/shard_map/ppermute | solution.py:234
  39.7 1.3 %collective-permute-done.9.hi_ref = f32[4,4,16,128]{3,2,1,0:T(8,128)S(1)} collective-permute-done((f32[4,4,16,128]{3,2,1,0:T(8,128)S(1)}, f32[4,4,16,128]{3,2,1,0:T(8,128)S(1)}, u32[]{:S(2)}, u32[]{:S(2)}) %collective-permute-start.9) | collective-permute-done | bytes 131104 | tf_op jit(solution)/shard_map/ppermute | solution.py:234
  41.1 1.1 %collective-permute-start.10 = (f32[4,12,8,128]{3,2,1,0:T(8,128)S(1)}, f32[4,12,8,128]{3,2,1,0:T(8,128)S(1)}, u32[]{:S(2)}, u32[]{:S(2)}) collective-permute-start(f32[4,12,8,128]{3,2,1,0:T(8,128)S(1)} %get-tuple-element.43), channel_id=1, source_target_pairs={{0,1},{1,2},{2,3},{3,4},{4,5},{5,6},{6,7},{7,0},{8,9},{9,10},{10,1... | collective-permute-start | bytes 589832 | tf_op jit(solution)/shard_map/ppermute | solution.py:241
  42.2 3.7 %collective-permute-start.11 = (f32[4,12,8,128]{3,2,1,0:T(8,128)S(1)}, f32[4,12,8,128]{3,2,1,0:T(8,128)S(1)}, u32[]{:S(2)}, u32[]{:S(2)}) collective-permute-start(f32[4,12,8,128]{3,2,1,0:T(8,128)S(1)} %get-tuple-element.44), channel_id=1, source_target_pairs={{0,7},{1,0},{2,1},{3,2},{4,3},{5,4},{6,5},{7,6},{8,15},{9,8},{10,9... | collective-permute-start | bytes 589832 | tf_op jit(solution)/shard_map/ppermute | solution.py:241
  45.9 4.1 %collective-permute-done.10.below_ref = f32[4,12,8,128]{3,2,1,0:T(8,128)S(1)} collective-permute-done((f32[4,12,8,128]{3,2,1,0:T(8,128)S(1)}, f32[4,12,8,128]{3,2,1,0:T(8,128)S(1)}, u32[]{:S(2)}, u32[]{:S(2)}) %collective-permute-start.10) | collective-permute-done | bytes 196640 | tf_op jit(solution)/shard_map/ppermute | solution.py:241
  50.0 2.2 %shard_map.82 = (f32[2,16,16,128]{3,2,1,0:T(8,128)S(1)}, f32[8,4,8,128]{3,2,1,0:T(8,128)S(1)}) custom-call(f32[4,16,16,128]{3,2,1,0:T(8,128)S(1)} %get-tuple-element.40.centre_ref, f32[4,4,16,128]{3,2,1,0:T(8,128)S(1)} %collective-permute-done.8.lo_ref, f32[4,4,16,128]{3,2,1,0:T(8,128)S(1)} %collective-permute-done.9.hi_ref, ...), custom_call_target="tpu_custom_call" | custom-call | tf_op jit(solution)/shard_map/pallas_call | solution.py:15
  52.2 0.1 collective-permute-start.12
  52.4 1.2 %collective-permute-done.12 = f32[4,4,8,128]{3,2,1,0:T(8,128)S(1)} collective-permute-done((f32[4,4,8,128]{3,2,1,0:T(8,128)S(1)}, f32[4,4,8,128]{3,2,1,0:T(8,128)S(1)}, u32[]{:S(2)}, u32[]{:S(2)}) %collective-permute-start.12) | collective-permute-done | bytes 65568 | tf_op jit(solution)/shard_map/ppermute | solution.py:246
  53.6 3.9 %collective-permute-start.13 = (f32[2,4,8,128]{3,2,1,0:T(8,128)S(1)}, f32[2,4,8,128]{3,2,1,0:T(8,128)S(1)}, u32[]{:S(2)}, u32[]{:S(2)}) collective-permute-start(f32[2,4,8,128]{3,2,1,0:T(8,128)S(1)} %pad_maximum_fusion.1), channel_id=1, source_target_pairs={{0,192},{32,96},{64,128},{96,32},{128,64},{160,224},{192,0},{224,1... | collective-permute-start | bytes 98312 | tf_op jit(solution)/shard_map/ppermute | solution.py:246
  57.6 2.2 %collective-permute-done.13 = f32[2,4,8,128]{3,2,1,0:T(8,128)S(1)} collective-permute-done((f32[2,4,8,128]{3,2,1,0:T(8,128)S(1)}, f32[2,4,8,128]{3,2,1,0:T(8,128)S(1)}, u32[]{:S(2)}, u32[]{:S(2)}) %collective-permute-start.13) | collective-permute-done | bytes 32800 | tf_op jit(solution)/shard_map/ppermute | solution.py:246
  59.8 1.5 %collective-permute-start.14 = (f32[4,8,128]{2,1,0:T(8,128)S(1)}, f32[4,8,128]{2,1,0:T(8,128)S(1)}, u32[]{:S(2)}, u32[]{:S(2)}) collective-permute-start(f32[4,8,128]{2,1,0:T(8,128)S(1)} %get-tuple-element.62), channel_id=1, source_target_pairs={{0,64},{32,224},{64,0},{96,160},{128,192},{160,96},{192,128},{224,... | collective-permute-start | bytes 49160 | tf_op jit(solution)/shard_map/ppermute | solution.py:246
  61.3 3.2 %collective-permute-done.14.last_ref = f32[4,8,128]{2,1,0:T(8,128)S(1)} collective-permute-done((f32[4,8,128]{2,1,0:T(8,128)S(1)}, f32[4,8,128]{2,1,0:T(8,128)S(1)}, u32[]{:S(2)}, u32[]{:S(2)}) %collective-permute-start.14) | collective-permute-done | bytes 16416 | tf_op jit(solution)/shard_map/ppermute | solution.py:246
  64.5 0.8 %shard_map.83 = (f32[16,16,16]{2,1,0:T(8,128)}, f32[2,16,16,128]{3,2,1,0:T(8,128)}) custom-call(f32[4,8,128]{2,1,0:T(8,128)S(1)} %get-tuple-element.63.own_ref, f32[4,8,128]{2,1,0:T(8,128)S(1)} %collective-permute-done.14.last_ref, f32[2,16,16,128]{3,2,1,0:T(8,128)S(1)} %get-tuple-element.47.resp_ref), custom_call_target="tpu_custom_call" | custom-call | tf_op jit(solution)/shard_map/pallas_call | solution.py:15
  (31 shorter events, 0.4 us)
Async XLA Ops:
  0.6 0.9 %copy-start.1 = (f32[16,16,128]{2,1,0:T(8,128)S(1)}, f32[16,16,128]{2,1,0:T(8,128)}, u32[]{:S(2)}) copy-start(f32[16,16,128]{2,1,0:T(8,128)} %pert_ref.1) | copy-start | bytes 393220
  0.6 1.0 %copy-start.5 = (f32[16,16,128]{2,1,0:T(8,128)S(1)}, f32[16,16,128]{2,1,0:T(8,128)}, u32[]{:S(2)}) copy-start(f32[16,16,128]{2,1,0:T(8,128)} %param.9) | copy-start | bytes 393220
  1.7 2.3 %copy-start = (f32[2,16,16,128]{3,2,1,0:T(8,128)S(1)}, f32[2,16,16,128]{3,2,1,0:T(8,128)}, u32[]{:S(2)}) copy-start(f32[2,16,16,128]{3,2,1,0:T(8,128)} %orb_ref.5) | copy-start | bytes 786436
  1.7 4.7 %collective-permute-start = (f32[3,4,16,128]{3,2,1,0:T(8,128)S(1)}, f32[3,4,16,128]{3,2,1,0:T(8,128)S(1)}, u32[]{:S(2)}, u32[]{:S(2)}) collective-permute-start(f32[3,4,16,128]{3,2,1,0:T(8,128)S(1)} %get-tuple-element.34), channel_id=1, source_target_pairs={{0,8},{8,16},{16,24},{24,0},{1,9},{9,17},{17,25},{25,1},{2,10},{10... | collective-permute-start | bytes 294920 | tf_op jit(solution)/shard_map/ppermute | solution.py:234
  4.0 5.8 %collective-permute-start.1 = (f32[3,4,16,128]{3,2,1,0:T(8,128)S(1)}, f32[3,4,16,128]{3,2,1,0:T(8,128)S(1)}, u32[]{:S(2)}, u32[]{:S(2)}) collective-permute-start(f32[3,4,16,128]{3,2,1,0:T(8,128)S(1)} %get-tuple-element.35), channel_id=1, source_target_pairs={{0,24},{8,0},{16,8},{24,16},{1,25},{9,1},{17,9},{25,17},{2,26},{10... | collective-permute-start | bytes 294920 | tf_op jit(solution)/shard_map/ppermute | solution.py:234
  9.9 7.3 %collective-permute-start.2 = (f32[3,12,8,128]{3,2,1,0:T(8,128)S(1)}, f32[3,12,8,128]{3,2,1,0:T(8,128)S(1)}, u32[]{:S(2)}, u32[]{:S(2)}) collective-permute-start(f32[3,12,8,128]{3,2,1,0:T(8,128)S(1)} %get-tuple-element.36), channel_id=1, source_target_pairs={{0,1},{1,2},{2,3},{3,4},{4,5},{5,6},{6,7},{7,0},{8,9},{9,10},{10,1... | collective-permute-start | bytes 442376 | tf_op jit(solution)/shard_map/ppermute | solution.py:241
  10.0 7.2 %collective-permute-start.3 = (f32[3,12,8,128]{3,2,1,0:T(8,128)S(1)}, f32[3,12,8,128]{3,2,1,0:T(8,128)S(1)}, u32[]{:S(2)}, u32[]{:S(2)}) collective-permute-start(f32[3,12,8,128]{3,2,1,0:T(8,128)S(1)} %get-tuple-element.37), channel_id=1, source_target_pairs={{0,7},{1,0},{2,1},{3,2},{4,3},{5,4},{6,5},{7,6},{8,15},{9,8},{10,9... | collective-permute-start | bytes 442376 | tf_op jit(solution)/shard_map/ppermute | solution.py:241
  14.1 3.1 %copy-start.3 = (f32[2]{0:T(128)S(1)}, f32[2]{0:T(128)}, u32[]{:S(2)}) copy-start(f32[2]{0:T(128)} %occ_ref.3) | copy-start | bytes 28
  14.1 3.1 %copy-start.4 = (f32[2]{0:T(128)S(1)}, f32[2]{0:T(128)}, u32[]{:S(2)}) copy-start(f32[2]{0:T(128)} %shift_ref.1) | copy-start | bytes 28
  18.9 1.3 %collective-permute-start.4 = (f32[8,16,128]{2,1,0:T(8,128)S(1)}, f32[8,16,128]{2,1,0:T(8,128)S(1)}, u32[]{:S(2)}, u32[]{:S(2)}) collective-permute-start(f32[8,16,128]{2,1,0:T(8,128)S(1)} %constant_dynamic-slice_fusion.4), channel_id=1, source_target_pairs={{0,32},{32,0},{64,96},{96,64},{128,160},{160,128},{192,224},{224,1... | collective-permute-start | bytes 196616 | tf_op jit(solution)/shard_map/ppermute | solution.py:246
  20.3 7.0 %collective-permute-start.5 = (f32[8,16,128]{2,1,0:T(8,128)S(1)}, f32[8,16,128]{2,1,0:T(8,128)S(1)}, u32[]{:S(2)}, u32[]{:S(2)}) collective-permute-start(f32[8,16,128]{2,1,0:T(8,128)S(1)} %dynamic-slice_add_fusion), channel_id=1, source_target_pairs={{0,192},{32,96},{64,128},{96,32},{128,64},{160,224},{192,0},{224,1... | collective-permute-start | bytes 196616 | tf_op jit(solution)/shard_map/ppermute | solution.py:246
  27.3 6.7 %copy-start.2 = (f32[16,16,128]{2,1,0:T(8,128)S(1)}, f32[16,16,128]{2,1,0:T(8,128)}, u32[]{:S(2)}) copy-start(f32[16,16,128]{2,1,0:T(8,128)} %kern_ref.1) | copy-start | bytes 393220
  27.3 5.4 %collective-permute-start.6 = (f32[8,16,128]{2,1,0:T(8,128)S(1)}, f32[8,16,128]{2,1,0:T(8,128)S(1)}, u32[]{:S(2)}, u32[]{:S(2)}) collective-permute-start(f32[8,16,128]{2,1,0:T(8,128)S(1)} %add.54), channel_id=1, source_target_pairs={{0,64},{32,224},{64,0},{96,160},{128,192},{160,96},{192,128},{224,... | collective-permute-start | bytes 196616 | tf_op jit(solution)/shard_map/ppermute | solution.py:246
  32.7 1.3 %collective-permute-start.7 = (f32[8,16,128]{2,1,0:T(8,128)S(1)}, f32[8,16,128]{2,1,0:T(8,128)S(1)}, u32[]{:S(2)}, u32[]{:S(2)}) collective-permute-start(f32[8,16,128]{2,1,0:T(8,128)S(1)} %add.55.own_ref), channel_id=1, source_target_pairs={{0,32},{32,0},{64,96},{96,64},{128,160},{160,128},{192,224},{224,1... | collective-permute-start | bytes 196616 | tf_op jit(solution)/shard_map/ppermute | solution.py:246
  34.1 5.6 %collective-permute-start.8 = (f32[4,4,16,128]{3,2,1,0:T(8,128)S(1)}, f32[4,4,16,128]{3,2,1,0:T(8,128)S(1)}, u32[]{:S(2)}, u32[]{:S(2)}) collective-permute-start(f32[4,4,16,128]{3,2,1,0:T(8,128)S(1)} %get-tuple-element.41), channel_id=1, source_target_pairs={{0,8},{8,16},{16,24},{24,0},{1,9},{9,17},{17,25},{25,1},{2,10},{10... | collective-permute-start | bytes 393224 | tf_op jit(solution)/shard_map/ppermute | solution.py:234
  34.5 6.6 %collective-permute-start.9 = (f32[4,4,16,128]{3,2,1,0:T(8,128)S(1)}, f32[4,4,16,128]{3,2,1,0:T(8,128)S(1)}, u32[]{:S(2)}, u32[]{:S(2)}) collective-permute-start(f32[4,4,16,128]{3,2,1,0:T(8,128)S(1)} %get-tuple-element.42), channel_id=1, source_target_pairs={{0,24},{8,0},{16,8},{24,16},{1,25},{9,1},{17,9},{25,17},{2,26},{10... | collective-permute-start | bytes 393224 | tf_op jit(solution)/shard_map/ppermute | solution.py:234
  41.1 8.9 %collective-permute-start.10 = (f32[4,12,8,128]{3,2,1,0:T(8,128)S(1)}, f32[4,12,8,128]{3,2,1,0:T(8,128)S(1)}, u32[]{:S(2)}, u32[]{:S(2)}) collective-permute-start(f32[4,12,8,128]{3,2,1,0:T(8,128)S(1)} %get-tuple-element.43), channel_id=1, source_target_pairs={{0,1},{1,2},{2,3},{3,4},{4,5},{5,6},{6,7},{7,0},{8,9},{9,10},{10,1... | collective-permute-start | bytes 589832 | tf_op jit(solution)/shard_map/ppermute | solution.py:241
  42.2 7.8 %collective-permute-start.11 = (f32[4,12,8,128]{3,2,1,0:T(8,128)S(1)}, f32[4,12,8,128]{3,2,1,0:T(8,128)S(1)}, u32[]{:S(2)}, u32[]{:S(2)}) collective-permute-start(f32[4,12,8,128]{3,2,1,0:T(8,128)S(1)} %get-tuple-element.44), channel_id=1, source_target_pairs={{0,7},{1,0},{2,1},{3,2},{4,3},{5,4},{6,5},{7,6},{8,15},{9,8},{10,9... | collective-permute-start | bytes 589832 | tf_op jit(solution)/shard_map/ppermute | solution.py:241
  52.2 1.3 %collective-permute-start.12 = (f32[4,4,8,128]{3,2,1,0:T(8,128)S(1)}, f32[4,4,8,128]{3,2,1,0:T(8,128)S(1)}, u32[]{:S(2)}, u32[]{:S(2)}) collective-permute-start(f32[4,4,8,128]{3,2,1,0:T(8,128)S(1)} %dynamic-slice_bitcast_fusion), channel_id=1, source_target_pairs={{0,32},{32,0},{64,96},{96,64},{128,160},{160,128},{192,224},{224,1... | collective-permute-start | bytes 196616 | tf_op jit(solution)/shard_map/ppermute | solution.py:246
  53.6 6.1 %collective-permute-start.13 = (f32[2,4,8,128]{3,2,1,0:T(8,128)S(1)}, f32[2,4,8,128]{3,2,1,0:T(8,128)S(1)}, u32[]{:S(2)}, u32[]{:S(2)}) collective-permute-start(f32[2,4,8,128]{3,2,1,0:T(8,128)S(1)} %pad_maximum_fusion.1), channel_id=1, source_target_pairs={{0,192},{32,96},{64,128},{96,32},{128,64},{160,224},{192,0},{224,1... | collective-permute-start | bytes 98312 | tf_op jit(solution)/shard_map/ppermute | solution.py:246
  59.8 4.7 %collective-permute-start.14 = (f32[4,8,128]{2,1,0:T(8,128)S(1)}, f32[4,8,128]{2,1,0:T(8,128)S(1)}, u32[]{:S(2)}, u32[]{:S(2)}) collective-permute-start(f32[4,8,128]{2,1,0:T(8,128)S(1)} %get-tuple-element.62), channel_id=1, source_target_pairs={{0,64},{32,224},{64,0},{96,160},{128,192},{160,96},{192,128},{224,... | collective-permute-start | bytes 49160 | tf_op jit(solution)/shard_map/ppermute | solution.py:246

commit v8 on v7

--- a/solution.py
+++ b/solution.py
@@ -1,3 +1,5 @@
+import functools
+
 import jax
 import jax.numpy as jnp
 from jax import lax
@@ -49,7 +51,10 @@
     return row
 
 
-def pack_kernel(centre_ref, lo_ref, hi_ref, tail_ref, head_ref):
+def pack_kernel(extras, centre_ref, lo_ref, hi_ref, *refs):
+    tail_ref, head_ref = refs[extras : extras + 2]
+    for source_ref, dest_ref in zip(refs[:extras], refs[extras + 2 :]):
+        dest_ref[...] = source_ref[...]
     for field in range(centre_ref.shape[0]):
         pack_z(padded_row(centre_ref, lo_ref, hi_ref, field), head_ref, tail_ref, field)
 
@@ -122,7 +127,7 @@
 
 
 def last_sweep(src_ref, scale_ref, sc_ref, o, zero, orb_ref, occ_ref, resp_ref, dens_ref):
-    occupation = occ_ref[o]
+    occupation = jnp.concatenate([occ_ref[o]] * 2, 0)
 
     def store(r, new):
         resp_ref[o, r - 4] = new
@@ -141,7 +146,7 @@
         assemble(padded_row(centre_ref, lo_ref, hi_ref, field), above_ref, below_ref, field, p_ref, field)
     assemble(padded_row(centre_ref, lo_ref, hi_ref, 2), above_ref, below_ref, 2, a_ref, 0)
     for o in range(2):
-        base = 32.0 / 15.0 + shift_ref[o]
+        base = 32.0 / 15.0 + jnp.concatenate([shift_ref[o]] * 4, 0)
 
         for r in range(1, 23):
             scale_ref[o, r, 0:32] = (RELAX / 60.0) / (base + a_ref[0, r, 0:32])
@@ -234,11 +239,13 @@
     return lax.ppermute(up, "gy", ring("gy", 1)), lax.ppermute(down, "gy", ring("gy", -1))
 
 
-def exchange_z(centre, lo, hi):
+def exchange_z(centre, lo, hi, *extras):
     fields = centre.shape[0]
     strip = f32(fields, 12, 8, 128)
-    tail, head = call(pack_kernel, (strip, strip), centre, lo, hi)
-    return lax.ppermute(head, "gz", ring("gz", -1)), lax.ppermute(tail, "gz", ring("gz", 1))
+    tail, head, *extras = call(
+        functools.partial(pack_kernel, len(extras)), (strip, strip, *(f32(*each.shape) for each in extras)), centre, lo, hi, *extras
+    )
+    return lax.ppermute(head, "gz", ring("gz", -1)), lax.ppermute(tail, "gz", ring("gz", 1)), *extras
 
 
 def partner(value, *steps):
@@ -251,7 +258,8 @@
     core, chip = group % 2, group // 2
     padded = f32(2, 24, 32, 128)
     wide = pltpu.VMEM((2, 24, 32, 128), jnp.float32)
-    zero = jnp.zeros((1,), jnp.int32)
+    zero = (lax.axis_index("gz") // 64)[None].astype(jnp.int32)
+    shifts, occupations = (jnp.broadcast_to(each[:, None, None], (2, 8, 128)) for each in (orbital_shift, occupation))
 
     def ends(field):
         return field[12:16], field[0:4]
@@ -260,11 +268,11 @@
     up, down = call(strips_kernel, (f32(3, 4, 16, 128), f32(3, 4, 16, 128)), *(end for pair in edges for end in pair))
     centre = jnp.concatenate([perturbation[None] * orbitals, potential[None]], 0)
     lo, hi = exchange_y(up, down)
-    above, below = exchange_z(centre, lo, hi)
+    above, below, shifts, occupations = exchange_z(centre, lo, hi, shifts, occupations)
     response, partial, scale = call(
         first_kernel, (f32(2, 16, 16, 128), f32(16, 16, 128), padded),
-        centre, lo, hi, below, above, orbitals, orbital_shift, occupation, zero,
-        scratch=[wide] * 4, smem=3,
+        centre, lo, hi, below, above, orbitals, shifts, occupations, zero,
+        scratch=[wide] * 4, smem=1,
     )
 
     own = lax.dynamic_slice_in_dim(partial, 8 * core, 8, 0)
@@ -280,8 +288,8 @@
     above, below = exchange_z(centre, lo, hi)
     response, blocks = call(
         second_kernel, (f32(2, 16, 16, 128), f32(8, 4, 8, 128)),
-        centre, lo, hi, below, above, scale, orbitals, occupation, zero,
-        scratch=[wide] * 5 + [pltpu.VMEM((16, 16, 128), jnp.float32)], smem=2,
+        centre, lo, hi, below, above, scale, orbitals, occupations, zero,
+        scratch=[wide] * 5 + [pltpu.VMEM((16, 16, 128), jnp.float32)], smem=1,
     )
 
     blocks = blocks.reshape(4, 2, 4, 8, 128)

time: 65.8 us -> 64.9 us (0.986)
  Pallas kernels: 4.87 us -> 3.79 us
    pallas_call x7, Pallas kernels: 4.87 us -> 3.79 us  [call(): pl.pallas_call(body, out_shape=outs, in_specs=[VMEM] * (len(args) - smem)...]
where the time goes in v8:
time: 64.9 us; the launch traced here: 64.3 us
  waiting for transfers between devices  33.1 us (51%)
  starting transfers between devices  25.2 us (39%)
  Pallas kernels  3.79 us (6%)
  local copies, waits for them, and re-layouts  1.24 us (2%)
  between operations  0.87 us (1%)
    ppermute x7, waiting for transfers between devices, partner(): lax.ppermute(value, 'bands', [(i, i ^ steps[i % len(steps)]) for i in ran...  15.3 us
    ppermute x7, starting transfers between devices, partner(): lax.ppermute(value, 'bands', [(i, i ^ steps[i % len(steps)]) for i in ran...  11.8 us
    ppermute x2, starting transfers between devices, exchange_z(): lax.ppermute(head, 'gz', ring('gz', -1))  7.81 us
    ppermute x2, waiting for transfers between devices, exchange_z(): lax.ppermute(tail, 'gz', ring('gz', 1))  7.2 us
    ppermute x2, waiting for transfers between devices, exchange_y(): lax.ppermute(up, 'gy', ring('gy', 1))  5.84 us
    ppermute x2, waiting for transfers between devices, exchange_y(): lax.ppermute(down, 'gy', ring('gy', -1))  4.73 us
    pallas_call x7, Pallas kernels, call(): pl.pallas_call(body, out_shape=outs, in_specs=[VMEM] * (len(args) - smem)...  3.79 us
    ppermute x2, starting transfers between devices, exchange_y(): lax.ppermute(up, 'gy', ring('gy', 1))  2.65 us
  transfers between devices with their start and end apart: 15, of which 13 were waited for; matrix products, arithmetic and copies ran while one was open for 0% of the time, Pallas kernels for 0%

profile of v8, /device:TPU:6, one launch (start us, length us, event | category | flops | bytes accessed | tf_op | source)
XLA Modules:
  0.0 64.3 jit_solution(18054188356722782069)
XLA Ops:
  0.6 0.9 %slice_bitcast_fusion = (f32[4,16,128]{2,1,0:T(8,128)S(1)}, f32[4,16,128]{2,1,0:T(8,128)S(1)}, f32[4,16,128]{2,1,0:T(8,128)S(1)}, f32[4,16,128]{2,1,0:T(8,128)S(1)}) fusion(f32[2,16,16,128]{3,2,1,0:T(8,128)} %orb_ref.5), kind=kLoop, calls=%fused_computation.7 | loop fusion | bytes 262144 | tf_op jit(solution)/shard_map/slice | solution.py:265
  1.5 0.1 copy-done.3
  1.7 2.3 %collective-permute-start = (f32[3,4,16,128]{3,2,1,0:T(8,128)S(1)}, f32[3,4,16,128]{3,2,1,0:T(8,128)S(1)}, u32[]{:S(2)}, u32[]{:S(2)}) collective-permute-start(f32[3,4,16,128]{3,2,1,0:T(8,128)S(1)} %get-tuple-element.36), channel_id=1, source_target_pairs={{0,8},{8,16},{16,24},{24,0},{1,9},{9,17},{17,25},{25,1},{2,10},{10... | collective-permute-start | bytes 294920 | tf_op jit(solution)/shard_map/ppermute | solution.py:239
  4.1 2.3 %collective-permute-done.lo_ref = f32[3,4,16,128]{3,2,1,0:T(8,128)S(1)} collective-permute-done((f32[3,4,16,128]{3,2,1,0:T(8,128)S(1)}, f32[3,4,16,128]{3,2,1,0:T(8,128)S(1)}, u32[]{:S(2)}, u32[]{:S(2)}) %collective-permute-start) | collective-permute-done | bytes 98336 | tf_op jit(solution)/shard_map/ppermute | solution.py:239
  6.4 3.4 %collective-permute-done.1.hi_ref = f32[3,4,16,128]{3,2,1,0:T(8,128)S(1)} collective-permute-done((f32[3,4,16,128]{3,2,1,0:T(8,128)S(1)}, f32[3,4,16,128]{3,2,1,0:T(8,128)S(1)}, u32[]{:S(2)}, u32[]{:S(2)}) %collective-permute-start.1) | collective-permute-done | bytes 98336 | tf_op jit(solution)/shard_map/ppermute | solution.py:239
  10.0 0.1 collective-permute-start.2
  10.1 4.1 %collective-permute-start.3 = (f32[3,12,8,128]{3,2,1,0:T(8,128)S(1)}, f32[3,12,8,128]{3,2,1,0:T(8,128)S(1)}, u32[]{:S(2)}, u32[]{:S(2)}) collective-permute-start(f32[3,12,8,128]{3,2,1,0:T(8,128)S(1)} %get-tuple-element.39), channel_id=1, source_target_pairs={{0,7},{1,0},{2,1},{3,2},{4,3},{5,4},{6,5},{7,6},{8,15},{9,8},{10,9... | collective-permute-start | bytes 442376 | tf_op jit(solution)/shard_map/ppermute | solution.py:248
  14.2 3.1 %collective-permute-done.2.below_ref = f32[3,12,8,128]{3,2,1,0:T(8,128)S(1)} collective-permute-done((f32[3,12,8,128]{3,2,1,0:T(8,128)S(1)}, f32[3,12,8,128]{3,2,1,0:T(8,128)S(1)}, u32[]{:S(2)}, u32[]{:S(2)}) %collective-permute-start.2) | collective-permute-done | bytes 147488 | tf_op jit(solution)/shard_map/ppermute | solution.py:248
  17.3 1.2 %shard_map.79 = (f32[2,16,16,128]{3,2,1,0:T(8,128)S(1)}, f32[16,16,128]{2,1,0:T(8,128)S(1)}, f32[2,24,32,128]{3,2,1,0:T(8,128)S(1)}) custom-call(f32[3,16,16,128]{3,2,1,0:T(8,128)S(1)} %pad_maximum_fusion.centre_ref, f32[3,4,16,128]{3,2,1,0:T(8,128)S(1)} %collective-permute-done.lo_ref, f32[3,4,16,128]{3,2,1,0:T(8,128)S(1)} %collective-permute-done.1.hi_ref, ...), custom_call_target="tpu_custom_call" | custom-call | tf_op jit(solution)/shard_map/pallas_call | solution.py:17
  18.6 0.1 collective-permute-start.4
  18.7 1.2 %collective-permute-done.4 = f32[8,16,128]{2,1,0:T(8,128)S(1)} collective-permute-done((f32[8,16,128]{2,1,0:T(8,128)S(1)}, f32[8,16,128]{2,1,0:T(8,128)S(1)}, u32[]{:S(2)}, u32[]{:S(2)}) %collective-permute-start.4) | collective-permute-done | bytes 65568 | tf_op jit(solution)/shard_map/ppermute | solution.py:253
  19.9 4.7 %collective-permute-start.5 = (f32[8,16,128]{2,1,0:T(8,128)S(1)}, f32[8,16,128]{2,1,0:T(8,128)S(1)}, u32[]{:S(2)}, u32[]{:S(2)}) collective-permute-start(f32[8,16,128]{2,1,0:T(8,128)S(1)} %dynamic-slice_add_fusion), channel_id=1, source_target_pairs={{0,192},{32,96},{64,128},{96,32},{128,64},{160,224},{192,0},{224,1... | collective-permute-start | bytes 196616 | tf_op jit(solution)/shard_map/ppermute | solution.py:253
  24.6 2.3 %collective-permute-done.5 = f32[8,16,128]{2,1,0:T(8,128)S(1)} collective-permute-done((f32[8,16,128]{2,1,0:T(8,128)S(1)}, f32[8,16,128]{2,1,0:T(8,128)S(1)}, u32[]{:S(2)}, u32[]{:S(2)}) %collective-permute-start.5) | collective-permute-done | bytes 65568 | tf_op jit(solution)/shard_map/ppermute | solution.py:253
  26.9 1.4 %collective-permute-start.6 = (f32[8,16,128]{2,1,0:T(8,128)S(1)}, f32[8,16,128]{2,1,0:T(8,128)S(1)}, u32[]{:S(2)}, u32[]{:S(2)}) collective-permute-start(f32[8,16,128]{2,1,0:T(8,128)S(1)} %add.55), channel_id=1, source_target_pairs={{0,64},{32,224},{64,0},{96,160},{128,192},{160,96},{192,128},{224,... | collective-permute-start | bytes 196616 | tf_op jit(solution)/shard_map/ppermute | solution.py:253
  28.4 3.9 %collective-permute-done.6 = f32[8,16,128]{2,1,0:T(8,128)S(1)} collective-permute-done((f32[8,16,128]{2,1,0:T(8,128)S(1)}, f32[8,16,128]{2,1,0:T(8,128)S(1)}, u32[]{:S(2)}, u32[]{:S(2)}) %collective-permute-start.6) | collective-permute-done | bytes 65568 | tf_op jit(solution)/shard_map/ppermute | solution.py:253
  32.3 0.1 collective-permute-start.7
  32.4 1.2 %collective-permute-done.7.other_ref = f32[8,16,128]{2,1,0:T(8,128)S(1)} collective-permute-done((f32[8,16,128]{2,1,0:T(8,128)S(1)}, f32[8,16,128]{2,1,0:T(8,128)S(1)}, u32[]{:S(2)}, u32[]{:S(2)}) %collective-permute-start.7) | collective-permute-done | bytes 65568 | tf_op jit(solution)/shard_map/ppermute | solution.py:253
  33.7 0.4 collective-permute-start.8
  34.1 1.7 %collective-permute-start.9 = (f32[4,4,16,128]{3,2,1,0:T(8,128)S(1)}, f32[4,4,16,128]{3,2,1,0:T(8,128)S(1)}, u32[]{:S(2)}, u32[]{:S(2)}) collective-permute-start(f32[4,4,16,128]{3,2,1,0:T(8,128)S(1)} %get-tuple-element.46), channel_id=1, source_target_pairs={{0,24},{8,0},{16,8},{24,16},{1,25},{9,1},{17,9},{25,17},{2,26},{10... | collective-permute-start | bytes 393224 | tf_op jit(solution)/shard_map/ppermute | solution.py:239
  35.8 3.5 %collective-permute-done.8.lo_ref = f32[4,4,16,128]{3,2,1,0:T(8,128)S(1)} collective-permute-done((f32[4,4,16,128]{3,2,1,0:T(8,128)S(1)}, f32[4,4,16,128]{3,2,1,0:T(8,128)S(1)}, u32[]{:S(2)}, u32[]{:S(2)}) %collective-permute-start.8) | collective-permute-done | bytes 131104 | tf_op jit(solution)/shard_map/ppermute | solution.py:239
  39.3 1.3 %collective-permute-done.9.hi_ref = f32[4,4,16,128]{3,2,1,0:T(8,128)S(1)} collective-permute-done((f32[4,4,16,128]{3,2,1,0:T(8,128)S(1)}, f32[4,4,16,128]{3,2,1,0:T(8,128)S(1)}, u32[]{:S(2)}, u32[]{:S(2)}) %collective-permute-start.9) | collective-permute-done | bytes 131104 | tf_op jit(solution)/shard_map/ppermute | solution.py:239
  40.7 1.1 %collective-permute-start.10 = (f32[4,12,8,128]{3,2,1,0:T(8,128)S(1)}, f32[4,12,8,128]{3,2,1,0:T(8,128)S(1)}, u32[]{:S(2)}, u32[]{:S(2)}) collective-permute-start(f32[4,12,8,128]{3,2,1,0:T(8,128)S(1)} %get-tuple-element.47), channel_id=1, source_target_pairs={{0,1},{1,2},{2,3},{3,4},{4,5},{5,6},{6,7},{7,0},{8,9},{9,10},{10,1... | collective-permute-start | bytes 589832 | tf_op jit(solution)/shard_map/ppermute | solution.py:248
  41.8 3.7 %collective-permute-start.11 = (f32[4,12,8,128]{3,2,1,0:T(8,128)S(1)}, f32[4,12,8,128]{3,2,1,0:T(8,128)S(1)}, u32[]{:S(2)}, u32[]{:S(2)}) collective-permute-start(f32[4,12,8,128]{3,2,1,0:T(8,128)S(1)} %get-tuple-element.48), channel_id=1, source_target_pairs={{0,7},{1,0},{2,1},{3,2},{4,3},{5,4},{6,5},{7,6},{8,15},{9,8},{10,9... | collective-permute-start | bytes 589832 | tf_op jit(solution)/shard_map/ppermute | solution.py:248
  45.5 4.1 %collective-permute-done.10.below_ref = f32[4,12,8,128]{3,2,1,0:T(8,128)S(1)} collective-permute-done((f32[4,12,8,128]{3,2,1,0:T(8,128)S(1)}, f32[4,12,8,128]{3,2,1,0:T(8,128)S(1)}, u32[]{:S(2)}, u32[]{:S(2)}) %collective-permute-start.10) | collective-permute-done | bytes 196640 | tf_op jit(solution)/shard_map/ppermute | solution.py:248
  49.6 1.7 %shard_map.82 = (f32[2,16,16,128]{3,2,1,0:T(8,128)S(1)}, f32[8,4,8,128]{3,2,1,0:T(8,128)S(1)}) custom-call(f32[4,16,16,128]{3,2,1,0:T(8,128)S(1)} %get-tuple-element.44.centre_ref, f32[4,4,16,128]{3,2,1,0:T(8,128)S(1)} %collective-permute-done.8.lo_ref, f32[4,4,16,128]{3,2,1,0:T(8,128)S(1)} %collective-permute-done.9.hi_ref, ...), custom_call_target="tpu_custom_call" | custom-call | tf_op jit(solution)/shard_map/pallas_call | solution.py:17
  51.3 0.1 collective-permute-start.12
  51.4 1.2 %collective-permute-done.12 = f32[4,4,8,128]{3,2,1,0:T(8,128)S(1)} collective-permute-done((f32[4,4,8,128]{3,2,1,0:T(8,128)S(1)}, f32[4,4,8,128]{3,2,1,0:T(8,128)S(1)}, u32[]{:S(2)}, u32[]{:S(2)}) %collective-permute-start.12) | collective-permute-done | bytes 65568 | tf_op jit(solution)/shard_map/ppermute | solution.py:253
  52.7 3.9 %collective-permute-start.13 = (f32[2,4,8,128]{3,2,1,0:T(8,128)S(1)}, f32[2,4,8,128]{3,2,1,0:T(8,128)S(1)}, u32[]{:S(2)}, u32[]{:S(2)}) collective-permute-start(f32[2,4,8,128]{3,2,1,0:T(8,128)S(1)} %pad_maximum_fusion.1), channel_id=1, source_target_pairs={{0,192},{32,96},{64,128},{96,32},{128,64},{160,224},{192,0},{224,1... | collective-permute-start | bytes 98312 | tf_op jit(solution)/shard_map/ppermute | solution.py:253
  56.6 2.2 %collective-permute-done.13 = f32[2,4,8,128]{3,2,1,0:T(8,128)S(1)} collective-permute-done((f32[2,4,8,128]{3,2,1,0:T(8,128)S(1)}, f32[2,4,8,128]{3,2,1,0:T(8,128)S(1)}, u32[]{:S(2)}, u32[]{:S(2)}) %collective-permute-start.13) | collective-permute-done | bytes 32800 | tf_op jit(solution)/shard_map/ppermute | solution.py:253
  58.8 1.5 %collective-permute-start.14 = (f32[4,8,128]{2,1,0:T(8,128)S(1)}, f32[4,8,128]{2,1,0:T(8,128)S(1)}, u32[]{:S(2)}, u32[]{:S(2)}) collective-permute-start(f32[4,8,128]{2,1,0:T(8,128)S(1)} %get-tuple-element.66), channel_id=1, source_target_pairs={{0,64},{32,224},{64,0},{96,160},{128,192},{160,96},{192,128},{224,... | collective-permute-start | bytes 49160 | tf_op jit(solution)/shard_map/ppermute | solution.py:253
  60.4 3.2 %collective-permute-done.14.last_ref = f32[4,8,128]{2,1,0:T(8,128)S(1)} collective-permute-done((f32[4,8,128]{2,1,0:T(8,128)S(1)}, f32[4,8,128]{2,1,0:T(8,128)S(1)}, u32[]{:S(2)}, u32[]{:S(2)}) %collective-permute-start.14) | collective-permute-done | bytes 16416 | tf_op jit(solution)/shard_map/ppermute | solution.py:253
  63.6 0.8 %shard_map.83 = (f32[16,16,16]{2,1,0:T(8,128)}, f32[2,16,16,128]{3,2,1,0:T(8,128)}) custom-call(f32[4,8,128]{2,1,0:T(8,128)S(1)} %get-tuple-element.67.own_ref, f32[4,8,128]{2,1,0:T(8,128)S(1)} %collective-permute-done.14.last_ref, f32[2,16,16,128]{3,2,1,0:T(8,128)S(1)} %get-tuple-element.51.resp_ref), custom_call_target="tpu_custom_call" | custom-call | tf_op jit(solution)/shard_map/pallas_call | solution.py:17
  (33 shorter events, 0.5 us)
Async XLA Ops:
  0.6 0.9 %copy-start.1 = (f32[16,16,128]{2,1,0:T(8,128)S(1)}, f32[16,16,128]{2,1,0:T(8,128)}, u32[]{:S(2)}) copy-start(f32[16,16,128]{2,1,0:T(8,128)} %pert_ref.1) | copy-start | bytes 393220
  0.6 1.0 %copy-start.3 = (f32[16,16,128]{2,1,0:T(8,128)S(1)}, f32[16,16,128]{2,1,0:T(8,128)}, u32[]{:S(2)}) copy-start(f32[16,16,128]{2,1,0:T(8,128)} %param.9) | copy-start | bytes 393220
  1.7 2.3 %copy-start = (f32[2,16,16,128]{3,2,1,0:T(8,128)S(1)}, f32[2,16,16,128]{3,2,1,0:T(8,128)}, u32[]{:S(2)}) copy-start(f32[2,16,16,128]{3,2,1,0:T(8,128)} %orb_ref.5) | copy-start | bytes 786436
  1.7 4.7 %collective-permute-start = (f32[3,4,16,128]{3,2,1,0:T(8,128)S(1)}, f32[3,4,16,128]{3,2,1,0:T(8,128)S(1)}, u32[]{:S(2)}, u32[]{:S(2)}) collective-permute-start(f32[3,4,16,128]{3,2,1,0:T(8,128)S(1)} %get-tuple-element.36), channel_id=1, source_target_pairs={{0,8},{8,16},{16,24},{24,0},{1,9},{9,17},{17,25},{25,1},{2,10},{10... | collective-permute-start | bytes 294920 | tf_op jit(solution)/shard_map/ppermute | solution.py:239
  4.0 5.8 %collective-permute-start.1 = (f32[3,4,16,128]{3,2,1,0:T(8,128)S(1)}, f32[3,4,16,128]{3,2,1,0:T(8,128)S(1)}, u32[]{:S(2)}, u32[]{:S(2)}) collective-permute-start(f32[3,4,16,128]{3,2,1,0:T(8,128)S(1)} %get-tuple-element.37), channel_id=1, source_target_pairs={{0,24},{8,0},{16,8},{24,16},{1,25},{9,1},{17,9},{25,17},{2,26},{10... | collective-permute-start | bytes 294920 | tf_op jit(solution)/shard_map/ppermute | solution.py:239
  4.0 5.8 %copy-start.4 = (f32[2]{0:T(128)S(1)}, f32[2]{0:T(128)}, u32[]{:S(2)}) copy-start(f32[2]{0:T(128)} %param.7) | copy-start | bytes 28
  4.1 5.8 %copy-start.5 = (f32[2]{0:T(128)S(1)}, f32[2]{0:T(128)}, u32[]{:S(2)}) copy-start(f32[2]{0:T(128)} %param.8) | copy-start | bytes 28
  10.0 7.3 %collective-permute-start.2 = (f32[3,12,8,128]{3,2,1,0:T(8,128)S(1)}, f32[3,12,8,128]{3,2,1,0:T(8,128)S(1)}, u32[]{:S(2)}, u32[]{:S(2)}) collective-permute-start(f32[3,12,8,128]{3,2,1,0:T(8,128)S(1)} %get-tuple-element.38), channel_id=1, source_target_pairs={{0,1},{1,2},{2,3},{3,4},{4,5},{5,6},{6,7},{7,0},{8,9},{9,10},{10,1... | collective-permute-start | bytes 442376 | tf_op jit(solution)/shard_map/ppermute | solution.py:248
  10.1 7.2 %collective-permute-start.3 = (f32[3,12,8,128]{3,2,1,0:T(8,128)S(1)}, f32[3,12,8,128]{3,2,1,0:T(8,128)S(1)}, u32[]{:S(2)}, u32[]{:S(2)}) collective-permute-start(f32[3,12,8,128]{3,2,1,0:T(8,128)S(1)} %get-tuple-element.39), channel_id=1, source_target_pairs={{0,7},{1,0},{2,1},{3,2},{4,3},{5,4},{6,5},{7,6},{8,15},{9,8},{10,9... | collective-permute-start | bytes 442376 | tf_op jit(solution)/shard_map/ppermute | solution.py:248
  18.6 1.3 %collective-permute-start.4 = (f32[8,16,128]{2,1,0:T(8,128)S(1)}, f32[8,16,128]{2,1,0:T(8,128)S(1)}, u32[]{:S(2)}, u32[]{:S(2)}) collective-permute-start(f32[8,16,128]{2,1,0:T(8,128)S(1)} %constant_dynamic-slice_fusion.4), channel_id=1, source_target_pairs={{0,32},{32,0},{64,96},{96,64},{128,160},{160,128},{192,224},{224,1... | collective-permute-start | bytes 196616 | tf_op jit(solution)/shard_map/ppermute | solution.py:253
  19.9 7.0 %collective-permute-start.5 = (f32[8,16,128]{2,1,0:T(8,128)S(1)}, f32[8,16,128]{2,1,0:T(8,128)S(1)}, u32[]{:S(2)}, u32[]{:S(2)}) collective-permute-start(f32[8,16,128]{2,1,0:T(8,128)S(1)} %dynamic-slice_add_fusion), channel_id=1, source_target_pairs={{0,192},{32,96},{64,128},{96,32},{128,64},{160,224},{192,0},{224,1... | collective-permute-start | bytes 196616 | tf_op jit(solution)/shard_map/ppermute | solution.py:253
  26.9 6.7 %copy-start.2 = (f32[16,16,128]{2,1,0:T(8,128)S(1)}, f32[16,16,128]{2,1,0:T(8,128)}, u32[]{:S(2)}) copy-start(f32[16,16,128]{2,1,0:T(8,128)} %kern_ref.1) | copy-start | bytes 393220
  26.9 5.4 %collective-permute-start.6 = (f32[8,16,128]{2,1,0:T(8,128)S(1)}, f32[8,16,128]{2,1,0:T(8,128)S(1)}, u32[]{:S(2)}, u32[]{:S(2)}) collective-permute-start(f32[8,16,128]{2,1,0:T(8,128)S(1)} %add.55), channel_id=1, source_target_pairs={{0,64},{32,224},{64,0},{96,160},{128,192},{160,96},{192,128},{224,... | collective-permute-start | bytes 196616 | tf_op jit(solution)/shard_map/ppermute | solution.py:253
  32.3 1.3 %collective-permute-start.7 = (f32[8,16,128]{2,1,0:T(8,128)S(1)}, f32[8,16,128]{2,1,0:T(8,128)S(1)}, u32[]{:S(2)}, u32[]{:S(2)}) collective-permute-start(f32[8,16,128]{2,1,0:T(8,128)S(1)} %add.56.own_ref), channel_id=1, source_target_pairs={{0,32},{32,0},{64,96},{96,64},{128,160},{160,128},{192,224},{224,1... | collective-permute-start | bytes 196616 | tf_op jit(solution)/shard_map/ppermute | solution.py:253
  33.7 5.6 %collective-permute-start.8 = (f32[4,4,16,128]{3,2,1,0:T(8,128)S(1)}, f32[4,4,16,128]{3,2,1,0:T(8,128)S(1)}, u32[]{:S(2)}, u32[]{:S(2)}) collective-permute-start(f32[4,4,16,128]{3,2,1,0:T(8,128)S(1)} %get-tuple-element.45), channel_id=1, source_target_pairs={{0,8},{8,16},{16,24},{24,0},{1,9},{9,17},{17,25},{25,1},{2,10},{10... | collective-permute-start | bytes 393224 | tf_op jit(solution)/shard_map/ppermute | solution.py:239
  34.1 6.6 %collective-permute-start.9 = (f32[4,4,16,128]{3,2,1,0:T(8,128)S(1)}, f32[4,4,16,128]{3,2,1,0:T(8,128)S(1)}, u32[]{:S(2)}, u32[]{:S(2)}) collective-permute-start(f32[4,4,16,128]{3,2,1,0:T(8,128)S(1)} %get-tuple-element.46), channel_id=1, source_target_pairs={{0,24},{8,0},{16,8},{24,16},{1,25},{9,1},{17,9},{25,17},{2,26},{10... | collective-permute-start | bytes 393224 | tf_op jit(solution)/shard_map/ppermute | solution.py:239
  40.7 8.9 %collective-permute-start.10 = (f32[4,12,8,128]{3,2,1,0:T(8,128)S(1)}, f32[4,12,8,128]{3,2,1,0:T(8,128)S(1)}, u32[]{:S(2)}, u32[]{:S(2)}) collective-permute-start(f32[4,12,8,128]{3,2,1,0:T(8,128)S(1)} %get-tuple-element.47), channel_id=1, source_target_pairs={{0,1},{1,2},{2,3},{3,4},{4,5},{5,6},{6,7},{7,0},{8,9},{9,10},{10,1... | collective-permute-start | bytes 589832 | tf_op jit(solution)/shard_map/ppermute | solution.py:248
  41.8 7.8 %collective-permute-start.11 = (f32[4,12,8,128]{3,2,1,0:T(8,128)S(1)}, f32[4,12,8,128]{3,2,1,0:T(8,128)S(1)}, u32[]{:S(2)}, u32[]{:S(2)}) collective-permute-start(f32[4,12,8,128]{3,2,1,0:T(8,128)S(1)} %get-tuple-element.48), channel_id=1, source_target_pairs={{0,7},{1,0},{2,1},{3,2},{4,3},{5,4},{6,5},{7,6},{8,15},{9,8},{10,9... | collective-permute-start | bytes 589832 | tf_op jit(solution)/shard_map/ppermute | solution.py:248
  51.3 1.3 %collective-permute-start.12 = (f32[4,4,8,128]{3,2,1,0:T(8,128)S(1)}, f32[4,4,8,128]{3,2,1,0:T(8,128)S(1)}, u32[]{:S(2)}, u32[]{:S(2)}) collective-permute-start(f32[4,4,8,128]{3,2,1,0:T(8,128)S(1)} %dynamic-slice_bitcast_fusion), channel_id=1, source_target_pairs={{0,32},{32,0},{64,96},{96,64},{128,160},{160,128},{192,224},{224,1... | collective-permute-start | bytes 196616 | tf_op jit(solution)/shard_map/ppermute | solution.py:253
  52.7 6.1 %collective-permute-start.13 = (f32[2,4,8,128]{3,2,1,0:T(8,128)S(1)}, f32[2,4,8,128]{3,2,1,0:T(8,128)S(1)}, u32[]{:S(2)}, u32[]{:S(2)}) collective-permute-start(f32[2,4,8,128]{3,2,1,0:T(8,128)S(1)} %pad_maximum_fusion.1), channel_id=1, source_target_pairs={{0,192},{32,96},{64,128},{96,32},{128,64},{160,224},{192,0},{224,1... | collective-permute-start | bytes 98312 | tf_op jit(solution)/shard_map/ppermute | solution.py:253
  58.8 4.7 %collective-permute-start.14 = (f32[4,8,128]{2,1,0:T(8,128)S(1)}, f32[4,8,128]{2,1,0:T(8,128)S(1)}, u32[]{:S(2)}, u32[]{:S(2)}) collective-permute-start(f32[4,8,128]{2,1,0:T(8,128)S(1)} %get-tuple-element.66), channel_id=1, source_target_pairs={{0,64},{32,224},{64,0},{96,160},{128,192},{160,96},{192,128},{224,... | collective-permute-start | bytes 49160 | tf_op jit(solution)/shard_map/ppermute | solution.py:253

commit v9 on v8

--- a/solution.py
+++ b/solution.py
@@ -220,11 +220,11 @@
             out_ref[b, part] = blocks[b]
 
 
-def final_kernel(own_ref, last_ref, resp_ref, dens_ref, response_ref):
+def final_kernel(own_ref, one_ref, two_ref, three_ref, resp_ref, dens_ref, response_ref):
     response_ref[...] = resp_ref[...]
     for part in range(4):
         y, z = part // 2, 8 * (part % 2)
-        total = own_ref[part] + last_ref[part]
+        total = (own_ref[part] + one_ref[part]) + (two_ref[part] + three_ref[part])
         for k in range(8):
             moved = total if k == 0 else pltpu.roll(total, 128 - 16 * k, 1)
             dens_ref[2 * k + y, z : z + 8, :] = moved[:, :16]
@@ -299,11 +299,9 @@
     def block_of(step):
         return lax.dynamic_index_in_dim(kept, chip ^ step, 0, keepdims=False)
 
-    first, second = 3 - 2 * core, 1 + 2 * core
-    pair = jnp.stack([block_of(0), block_of(second)]) + partner(jnp.stack([block_of(first), block_of(2)]), 6, 2)
-    last = partner(pair[1], 2, 6)
+    two, one, three = (partner(block_of(step), 2 * step) for step in (2, 1, 3))
     density, response = call(
-        final_kernel, (f32(16, 16, 16), f32(2, 16, 16, 128)), pair[0], last, response
+        final_kernel, (f32(16, 16, 16), f32(2, 16, 16, 128)), block_of(0), one, two, three, response
     )
     return response, density
 

time: 64.9 us -> 65.9 us (1.015)
  starting transfers between devices: 25.2 us -> 26.4 us
    ppermute x7 -> x8, starting transfers between devices: 11.8 us -> 13 us  [partner(): lax.ppermute(value, 'bands', [(i, i ^ steps[i % len(steps)]) for i in ran...]
    ppermute x7 -> x8, waiting for transfers between devices: 15.3 us -> 14.9 us  [partner(): lax.ppermute(value, 'bands', [(i, i ^ steps[i % len(steps)]) for i in ran...]
  transfers between devices with their start and end apart: 15 -> 16, of which waited for: 13 -> 12; matrix products, arithmetic and copies ran while one was open for 0% -> 0% of each run, Pallas kernels for 0% -> 0%
where the time goes in v9:
time: 65.9 us; the launch traced here: 65 us
  waiting for transfers between devices  32.7 us (50%)
  starting transfers between devices  26.4 us (40%)
  Pallas kernels  3.8 us (6%)
  local copies, waits for them, and re-layouts  1.23 us (2%)
  between operations  0.86 us (1%)
    ppermute x8, waiting for transfers between devices, partner(): lax.ppermute(value, 'bands', [(i, i ^ steps[i % len(steps)]) for i in ran...  14.9 us
    ppermute x8, starting transfers between devices, partner(): lax.ppermute(value, 'bands', [(i, i ^ steps[i % len(steps)]) for i in ran...  13 us
    ppermute x2, starting transfers between devices, exchange_z(): lax.ppermute(head, 'gz', ring('gz', -1))  7.81 us
    ppermute x2, waiting for transfers between devices, exchange_z(): lax.ppermute(tail, 'gz', ring('gz', 1))  7.2 us
    ppermute x2, waiting for transfers between devices, exchange_y(): lax.ppermute(up, 'gy', ring('gy', 1))  5.84 us
    ppermute x2, waiting for transfers between devices, exchange_y(): lax.ppermute(down, 'gy', ring('gy', -1))  4.73 us
    pallas_call x7, Pallas kernels, call(): pl.pallas_call(body, out_shape=outs, in_specs=[VMEM] * (len(args) - smem)...  3.8 us
    ppermute x2, starting transfers between devices, exchange_y(): lax.ppermute(up, 'gy', ring('gy', 1))  2.65 us
  transfers between devices with their start and end apart: 16, of which 12 were waited for; matrix products, arithmetic and copies ran while one was open for 0% of the time, Pallas kernels for 0%

profile of v9, /device:TPU:6, one launch (start us, length us, event | category | flops | bytes accessed | tf_op | source)
XLA Modules:
  0.0 65.0 jit_solution(11503264260050594715)
XLA Ops:
  0.6 0.9 %slice_bitcast_fusion = (f32[4,16,128]{2,1,0:T(8,128)S(1)}, f32[4,16,128]{2,1,0:T(8,128)S(1)}, f32[4,16,128]{2,1,0:T(8,128)S(1)}, f32[4,16,128]{2,1,0:T(8,128)S(1)}) fusion(f32[2,16,16,128]{3,2,1,0:T(8,128)} %orb_ref.5), kind=kLoop, calls=%fused_computation.5 | loop fusion | bytes 262144 | tf_op jit(solution)/shard_map/slice | solution.py:265
  1.5 0.1 copy-done.3
  1.7 2.3 %collective-permute-start = (f32[3,4,16,128]{3,2,1,0:T(8,128)S(1)}, f32[3,4,16,128]{3,2,1,0:T(8,128)S(1)}, u32[]{:S(2)}, u32[]{:S(2)}) collective-permute-start(f32[3,4,16,128]{3,2,1,0:T(8,128)S(1)} %get-tuple-element.36), channel_id=1, source_target_pairs={{0,8},{8,16},{16,24},{24,0},{1,9},{9,17},{17,25},{25,1},{2,10},{10... | collective-permute-start | bytes 294920 | tf_op jit(solution)/shard_map/ppermute | solution.py:239
  4.1 2.3 %collective-permute-done.lo_ref = f32[3,4,16,128]{3,2,1,0:T(8,128)S(1)} collective-permute-done((f32[3,4,16,128]{3,2,1,0:T(8,128)S(1)}, f32[3,4,16,128]{3,2,1,0:T(8,128)S(1)}, u32[]{:S(2)}, u32[]{:S(2)}) %collective-permute-start) | collective-permute-done | bytes 98336 | tf_op jit(solution)/shard_map/ppermute | solution.py:239
  6.4 3.4 %collective-permute-done.1.hi_ref = f32[3,4,16,128]{3,2,1,0:T(8,128)S(1)} collective-permute-done((f32[3,4,16,128]{3,2,1,0:T(8,128)S(1)}, f32[3,4,16,128]{3,2,1,0:T(8,128)S(1)}, u32[]{:S(2)}, u32[]{:S(2)}) %collective-permute-start.1) | collective-permute-done | bytes 98336 | tf_op jit(solution)/shard_map/ppermute | solution.py:239
  10.0 0.1 collective-permute-start.2
  10.1 4.1 %collective-permute-start.3 = (f32[3,12,8,128]{3,2,1,0:T(8,128)S(1)}, f32[3,12,8,128]{3,2,1,0:T(8,128)S(1)}, u32[]{:S(2)}, u32[]{:S(2)}) collective-permute-start(f32[3,12,8,128]{3,2,1,0:T(8,128)S(1)} %get-tuple-element.39), channel_id=1, source_target_pairs={{0,7},{1,0},{2,1},{3,2},{4,3},{5,4},{6,5},{7,6},{8,15},{9,8},{10,9... | collective-permute-start | bytes 442376 | tf_op jit(solution)/shard_map/ppermute | solution.py:248
  14.2 3.1 %collective-permute-done.2.below_ref = f32[3,12,8,128]{3,2,1,0:T(8,128)S(1)} collective-permute-done((f32[3,12,8,128]{3,2,1,0:T(8,128)S(1)}, f32[3,12,8,128]{3,2,1,0:T(8,128)S(1)}, u32[]{:S(2)}, u32[]{:S(2)}) %collective-permute-start.2) | collective-permute-done | bytes 147488 | tf_op jit(solution)/shard_map/ppermute | solution.py:248
  17.3 1.2 %shard_map.79 = (f32[2,16,16,128]{3,2,1,0:T(8,128)S(1)}, f32[16,16,128]{2,1,0:T(8,128)S(1)}, f32[2,24,32,128]{3,2,1,0:T(8,128)S(1)}) custom-call(f32[3,16,16,128]{3,2,1,0:T(8,128)S(1)} %pad_maximum_fusion.centre_ref, f32[3,4,16,128]{3,2,1,0:T(8,128)S(1)} %collective-permute-done.lo_ref, f32[3,4,16,128]{3,2,1,0:T(8,128)S(1)} %collective-permute-done.1.hi_ref, ...), custom_call_target="tpu_custom_call" | custom-call | tf_op jit(solution)/shard_map/pallas_call | solution.py:17
  18.6 0.1 collective-permute-start.4
  18.7 1.2 %collective-permute-done.4 = f32[8,16,128]{2,1,0:T(8,128)S(1)} collective-permute-done((f32[8,16,128]{2,1,0:T(8,128)S(1)}, f32[8,16,128]{2,1,0:T(8,128)S(1)}, u32[]{:S(2)}, u32[]{:S(2)}) %collective-permute-start.4) | collective-permute-done | bytes 65568 | tf_op jit(solution)/shard_map/ppermute | solution.py:253
  19.9 4.7 %collective-permute-start.5 = (f32[8,16,128]{2,1,0:T(8,128)S(1)}, f32[8,16,128]{2,1,0:T(8,128)S(1)}, u32[]{:S(2)}, u32[]{:S(2)}) collective-permute-start(f32[8,16,128]{2,1,0:T(8,128)S(1)} %dynamic-slice_add_fusion), channel_id=1, source_target_pairs={{0,192},{32,96},{64,128},{96,32},{128,64},{160,224},{192,0},{224,1... | collective-permute-start | bytes 196616 | tf_op jit(solution)/shard_map/ppermute | solution.py:253
  24.6 2.3 %collective-permute-done.5 = f32[8,16,128]{2,1,0:T(8,128)S(1)} collective-permute-done((f32[8,16,128]{2,1,0:T(8,128)S(1)}, f32[8,16,128]{2,1,0:T(8,128)S(1)}, u32[]{:S(2)}, u32[]{:S(2)}) %collective-permute-start.5) | collective-permute-done | bytes 65568 | tf_op jit(solution)/shard_map/ppermute | solution.py:253
  26.9 1.4 %collective-permute-start.6 = (f32[8,16,128]{2,1,0:T(8,128)S(1)}, f32[8,16,128]{2,1,0:T(8,128)S(1)}, u32[]{:S(2)}, u32[]{:S(2)}) collective-permute-start(f32[8,16,128]{2,1,0:T(8,128)S(1)} %add.49), channel_id=1, source_target_pairs={{0,64},{32,224},{64,0},{96,160},{128,192},{160,96},{192,128},{224,... | collective-permute-start | bytes 196616 | tf_op jit(solution)/shard_map/ppermute | solution.py:253
  28.4 3.9 %collective-permute-done.6 = f32[8,16,128]{2,1,0:T(8,128)S(1)} collective-permute-done((f32[8,16,128]{2,1,0:T(8,128)S(1)}, f32[8,16,128]{2,1,0:T(8,128)S(1)}, u32[]{:S(2)}, u32[]{:S(2)}) %collective-permute-start.6) | collective-permute-done | bytes 65568 | tf_op jit(solution)/shard_map/ppermute | solution.py:253
  32.3 0.1 collective-permute-start.7
  32.4 1.2 %collective-permute-done.7.other_ref = f32[8,16,128]{2,1,0:T(8,128)S(1)} collective-permute-done((f32[8,16,128]{2,1,0:T(8,128)S(1)}, f32[8,16,128]{2,1,0:T(8,128)S(1)}, u32[]{:S(2)}, u32[]{:S(2)}) %collective-permute-start.7) | collective-permute-done | bytes 65568 | tf_op jit(solution)/shard_map/ppermute | solution.py:253
  33.7 0.4 collective-permute-start.8
  34.1 1.7 %collective-permute-start.9 = (f32[4,4,16,128]{3,2,1,0:T(8,128)S(1)}, f32[4,4,16,128]{3,2,1,0:T(8,128)S(1)}, u32[]{:S(2)}, u32[]{:S(2)}) collective-permute-start(f32[4,4,16,128]{3,2,1,0:T(8,128)S(1)} %get-tuple-element.46), channel_id=1, source_target_pairs={{0,24},{8,0},{16,8},{24,16},{1,25},{9,1},{17,9},{25,17},{2,26},{10... | collective-permute-start | bytes 393224 | tf_op jit(solution)/shard_map/ppermute | solution.py:239
  35.8 3.5 %collective-permute-done.8.lo_ref = f32[4,4,16,128]{3,2,1,0:T(8,128)S(1)} collective-permute-done((f32[4,4,16,128]{3,2,1,0:T(8,128)S(1)}, f32[4,4,16,128]{3,2,1,0:T(8,128)S(1)}, u32[]{:S(2)}, u32[]{:S(2)}) %collective-permute-start.8) | collective-permute-done | bytes 131104 | tf_op jit(solution)/shard_map/ppermute | solution.py:239
  39.3 1.3 %collective-permute-done.9.hi_ref = f32[4,4,16,128]{3,2,1,0:T(8,128)S(1)} collective-permute-done((f32[4,4,16,128]{3,2,1,0:T(8,128)S(1)}, f32[4,4,16,128]{3,2,1,0:T(8,128)S(1)}, u32[]{:S(2)}, u32[]{:S(2)}) %collective-permute-start.9) | collective-permute-done | bytes 131104 | tf_op jit(solution)/shard_map/ppermute | solution.py:239
  40.7 1.1 %collective-permute-start.10 = (f32[4,12,8,128]{3,2,1,0:T(8,128)S(1)}, f32[4,12,8,128]{3,2,1,0:T(8,128)S(1)}, u32[]{:S(2)}, u32[]{:S(2)}) collective-permute-start(f32[4,12,8,128]{3,2,1,0:T(8,128)S(1)} %get-tuple-element.47), channel_id=1, source_target_pairs={{0,1},{1,2},{2,3},{3,4},{4,5},{5,6},{6,7},{7,0},{8,9},{9,10},{10,1... | collective-permute-start | bytes 589832 | tf_op jit(solution)/shard_map/ppermute | solution.py:248
  41.8 3.7 %collective-permute-start.11 = (f32[4,12,8,128]{3,2,1,0:T(8,128)S(1)}, f32[4,12,8,128]{3,2,1,0:T(8,128)S(1)}, u32[]{:S(2)}, u32[]{:S(2)}) collective-permute-start(f32[4,12,8,128]{3,2,1,0:T(8,128)S(1)} %get-tuple-element.48), channel_id=1, source_target_pairs={{0,7},{1,0},{2,1},{3,2},{4,3},{5,4},{6,5},{7,6},{8,15},{9,8},{10,9... | collective-permute-start | bytes 589832 | tf_op jit(solution)/shard_map/ppermute | solution.py:248
  45.5 4.1 %collective-permute-done.10.below_ref = f32[4,12,8,128]{3,2,1,0:T(8,128)S(1)} collective-permute-done((f32[4,12,8,128]{3,2,1,0:T(8,128)S(1)}, f32[4,12,8,128]{3,2,1,0:T(8,128)S(1)}, u32[]{:S(2)}, u32[]{:S(2)}) %collective-permute-start.10) | collective-permute-done | bytes 196640 | tf_op jit(solution)/shard_map/ppermute | solution.py:248
  49.6 1.7 %shard_map.82 = (f32[2,16,16,128]{3,2,1,0:T(8,128)S(1)}, f32[8,4,8,128]{3,2,1,0:T(8,128)S(1)}) custom-call(f32[4,16,16,128]{3,2,1,0:T(8,128)S(1)} %get-tuple-element.44.centre_ref, f32[4,4,16,128]{3,2,1,0:T(8,128)S(1)} %collective-permute-done.8.lo_ref, f32[4,4,16,128]{3,2,1,0:T(8,128)S(1)} %collective-permute-done.9.hi_ref, ...), custom_call_target="tpu_custom_call" | custom-call | tf_op jit(solution)/shard_map/pallas_call | solution.py:17
  51.3 0.1 collective-permute-start.12
  51.4 1.2 %collective-permute-done.12 = f32[4,4,8,128]{3,2,1,0:T(8,128)S(1)} collective-permute-done((f32[4,4,8,128]{3,2,1,0:T(8,128)S(1)}, f32[4,4,8,128]{3,2,1,0:T(8,128)S(1)}, u32[]{:S(2)}, u32[]{:S(2)}) %collective-permute-start.12) | collective-permute-done | bytes 65568 | tf_op jit(solution)/shard_map/ppermute | solution.py:253
  52.7 3.9 %collective-permute-start.15 = (f32[4,8,128]{2,1,0:T(8,128)S(1)}, f32[4,8,128]{2,1,0:T(8,128)S(1)}, u32[]{:S(2)}, u32[]{:S(2)}) collective-permute-start(f32[4,8,128]{2,1,0:T(8,128)S(1)} %get-tuple-element.62), channel_id=1, source_target_pairs={{0,192},{32,224},{64,128},{96,160},{128,64},{160,96},{192,0},{224,... | collective-permute-start | bytes 49160 | tf_op jit(solution)/shard_map/ppermute | solution.py:253
  56.6 1.3 %collective-permute-start.14 = (f32[4,8,128]{2,1,0:T(8,128)S(1)}, f32[4,8,128]{2,1,0:T(8,128)S(1)}, u32[]{:S(2)}, u32[]{:S(2)}) collective-permute-start(f32[4,8,128]{2,1,0:T(8,128)S(1)} %get-tuple-element.63), channel_id=1, source_target_pairs={{0,128},{32,160},{64,192},{96,224},{128,0},{160,32},{192,64},{224,... | collective-permute-start | bytes 49160 | tf_op jit(solution)/shard_map/ppermute | solution.py:253
  57.9 1.4 %collective-permute-start.13 = (f32[4,8,128]{2,1,0:T(8,128)S(1)}, f32[4,8,128]{2,1,0:T(8,128)S(1)}, u32[]{:S(2)}, u32[]{:S(2)}) collective-permute-start(f32[4,8,128]{2,1,0:T(8,128)S(1)} %get-tuple-element.64), channel_id=1, source_target_pairs={{0,64},{32,96},{64,0},{96,32},{128,192},{160,224},{192,128},{224,1... | collective-permute-start | bytes 49160 | tf_op jit(solution)/shard_map/ppermute | solution.py:253
  59.3 5.0 %collective-permute-done.14.two_ref = f32[4,8,128]{2,1,0:T(8,128)S(1)} collective-permute-done((f32[4,8,128]{2,1,0:T(8,128)S(1)}, f32[4,8,128]{2,1,0:T(8,128)S(1)}, u32[]{:S(2)}, u32[]{:S(2)}) %collective-permute-start.14) | collective-permute-done | bytes 16416 | tf_op jit(solution)/shard_map/ppermute | solution.py:253
  64.3 0.8 %shard_map.83 = (f32[16,16,16]{2,1,0:T(8,128)}, f32[2,16,16,128]{3,2,1,0:T(8,128)}) custom-call(f32[4,8,128]{2,1,0:T(8,128)S(1)} %get-tuple-element.65.own_ref, f32[4,8,128]{2,1,0:T(8,128)S(1)} %collective-permute-done.13.one_ref, f32[4,8,128]{2,1,0:T(8,128)S(1)} %collective-permute-done.14.two_ref, f32[4,8,128]{2,1,0:T(8,128)S(1)} %collective-permute-done.15.three_ref, ...), custom_call_target="tpu_custom_call" | custom-call | tf_op jit(solution)/shard_map/pallas_call | solution.py:17
  (32 shorter events, 0.5 us)
Async XLA Ops:
  0.6 0.9 %copy-start.1 = (f32[16,16,128]{2,1,0:T(8,128)S(1)}, f32[16,16,128]{2,1,0:T(8,128)}, u32[]{:S(2)}) copy-start(f32[16,16,128]{2,1,0:T(8,128)} %pert_ref.1) | copy-start | bytes 393220
  0.6 1.0 %copy-start.3 = (f32[16,16,128]{2,1,0:T(8,128)S(1)}, f32[16,16,128]{2,1,0:T(8,128)}, u32[]{:S(2)}) copy-start(f32[16,16,128]{2,1,0:T(8,128)} %param.9) | copy-start | bytes 393220
  1.7 2.3 %copy-start = (f32[2,16,16,128]{3,2,1,0:T(8,128)S(1)}, f32[2,16,16,128]{3,2,1,0:T(8,128)}, u32[]{:S(2)}) copy-start(f32[2,16,16,128]{3,2,1,0:T(8,128)} %orb_ref.5) | copy-start | bytes 786436
  1.7 4.7 %collective-permute-start = (f32[3,4,16,128]{3,2,1,0:T(8,128)S(1)}, f32[3,4,16,128]{3,2,1,0:T(8,128)S(1)}, u32[]{:S(2)}, u32[]{:S(2)}) collective-permute-start(f32[3,4,16,128]{3,2,1,0:T(8,128)S(1)} %get-tuple-element.36), channel_id=1, source_target_pairs={{0,8},{8,16},{16,24},{24,0},{1,9},{9,17},{17,25},{25,1},{2,10},{10... | collective-permute-start | bytes 294920 | tf_op jit(solution)/shard_map/ppermute | solution.py:239
  4.0 5.8 %collective-permute-start.1 = (f32[3,4,16,128]{3,2,1,0:T(8,128)S(1)}, f32[3,4,16,128]{3,2,1,0:T(8,128)S(1)}, u32[]{:S(2)}, u32[]{:S(2)}) collective-permute-start(f32[3,4,16,128]{3,2,1,0:T(8,128)S(1)} %get-tuple-element.37), channel_id=1, source_target_pairs={{0,24},{8,0},{16,8},{24,16},{1,25},{9,1},{17,9},{25,17},{2,26},{10... | collective-permute-start | bytes 294920 | tf_op jit(solution)/shard_map/ppermute | solution.py:239
  4.0 5.8 %copy-start.4 = (f32[2]{0:T(128)S(1)}, f32[2]{0:T(128)}, u32[]{:S(2)}) copy-start(f32[2]{0:T(128)} %param.7) | copy-start | bytes 28
  4.1 5.8 %copy-start.5 = (f32[2]{0:T(128)S(1)}, f32[2]{0:T(128)}, u32[]{:S(2)}) copy-start(f32[2]{0:T(128)} %param.8) | copy-start | bytes 28
  10.0 7.3 %collective-permute-start.2 = (f32[3,12,8,128]{3,2,1,0:T(8,128)S(1)}, f32[3,12,8,128]{3,2,1,0:T(8,128)S(1)}, u32[]{:S(2)}, u32[]{:S(2)}) collective-permute-start(f32[3,12,8,128]{3,2,1,0:T(8,128)S(1)} %get-tuple-element.38), channel_id=1, source_target_pairs={{0,1},{1,2},{2,3},{3,4},{4,5},{5,6},{6,7},{7,0},{8,9},{9,10},{10,1... | collective-permute-start | bytes 442376 | tf_op jit(solution)/shard_map/ppermute | solution.py:248
  10.1 7.2 %collective-permute-start.3 = (f32[3,12,8,128]{3,2,1,0:T(8,128)S(1)}, f32[3,12,8,128]{3,2,1,0:T(8,128)S(1)}, u32[]{:S(2)}, u32[]{:S(2)}) collective-permute-start(f32[3,12,8,128]{3,2,1,0:T(8,128)S(1)} %get-tuple-element.39), channel_id=1, source_target_pairs={{0,7},{1,0},{2,1},{3,2},{4,3},{5,4},{6,5},{7,6},{8,15},{9,8},{10,9... | collective-permute-start | bytes 442376 | tf_op jit(solution)/shard_map/ppermute | solution.py:248
  18.6 1.3 %collective-permute-start.4 = (f32[8,16,128]{2,1,0:T(8,128)S(1)}, f32[8,16,128]{2,1,0:T(8,128)S(1)}, u32[]{:S(2)}, u32[]{:S(2)}) collective-permute-start(f32[8,16,128]{2,1,0:T(8,128)S(1)} %constant_dynamic-slice_fusion), channel_id=1, source_target_pairs={{0,32},{32,0},{64,96},{96,64},{128,160},{160,128},{192,224},{224,1... | collective-permute-start | bytes 196616 | tf_op jit(solution)/shard_map/ppermute | solution.py:253
  19.9 7.0 %collective-permute-start.5 = (f32[8,16,128]{2,1,0:T(8,128)S(1)}, f32[8,16,128]{2,1,0:T(8,128)S(1)}, u32[]{:S(2)}, u32[]{:S(2)}) collective-permute-start(f32[8,16,128]{2,1,0:T(8,128)S(1)} %dynamic-slice_add_fusion), channel_id=1, source_target_pairs={{0,192},{32,96},{64,128},{96,32},{128,64},{160,224},{192,0},{224,1... | collective-permute-start | bytes 196616 | tf_op jit(solution)/shard_map/ppermute | solution.py:253
  26.9 6.7 %copy-start.2 = (f32[16,16,128]{2,1,0:T(8,128)S(1)}, f32[16,16,128]{2,1,0:T(8,128)}, u32[]{:S(2)}) copy-start(f32[16,16,128]{2,1,0:T(8,128)} %kern_ref.1) | copy-start | bytes 393220
  26.9 5.4 %collective-permute-start.6 = (f32[8,16,128]{2,1,0:T(8,128)S(1)}, f32[8,16,128]{2,1,0:T(8,128)S(1)}, u32[]{:S(2)}, u32[]{:S(2)}) collective-permute-start(f32[8,16,128]{2,1,0:T(8,128)S(1)} %add.49), channel_id=1, source_target_pairs={{0,64},{32,224},{64,0},{96,160},{128,192},{160,96},{192,128},{224,... | collective-permute-start | bytes 196616 | tf_op jit(solution)/shard_map/ppermute | solution.py:253
  32.3 1.3 %collective-permute-start.7 = (f32[8,16,128]{2,1,0:T(8,128)S(1)}, f32[8,16,128]{2,1,0:T(8,128)S(1)}, u32[]{:S(2)}, u32[]{:S(2)}) collective-permute-start(f32[8,16,128]{2,1,0:T(8,128)S(1)} %add.50.own_ref), channel_id=1, source_target_pairs={{0,32},{32,0},{64,96},{96,64},{128,160},{160,128},{192,224},{224,1... | collective-permute-start | bytes 196616 | tf_op jit(solution)/shard_map/ppermute | solution.py:253
  33.7 5.6 %collective-permute-start.8 = (f32[4,4,16,128]{3,2,1,0:T(8,128)S(1)}, f32[4,4,16,128]{3,2,1,0:T(8,128)S(1)}, u32[]{:S(2)}, u32[]{:S(2)}) collective-permute-start(f32[4,4,16,128]{3,2,1,0:T(8,128)S(1)} %get-tuple-element.45), channel_id=1, source_target_pairs={{0,8},{8,16},{16,24},{24,0},{1,9},{9,17},{17,25},{25,1},{2,10},{10... | collective-permute-start | bytes 393224 | tf_op jit(solution)/shard_map/ppermute | solution.py:239
  34.1 6.6 %collective-permute-start.9 = (f32[4,4,16,128]{3,2,1,0:T(8,128)S(1)}, f32[4,4,16,128]{3,2,1,0:T(8,128)S(1)}, u32[]{:S(2)}, u32[]{:S(2)}) collective-permute-start(f32[4,4,16,128]{3,2,1,0:T(8,128)S(1)} %get-tuple-element.46), channel_id=1, source_target_pairs={{0,24},{8,0},{16,8},{24,16},{1,25},{9,1},{17,9},{25,17},{2,26},{10... | collective-permute-start | bytes 393224 | tf_op jit(solution)/shard_map/ppermute | solution.py:239
  40.7 8.9 %collective-permute-start.10 = (f32[4,12,8,128]{3,2,1,0:T(8,128)S(1)}, f32[4,12,8,128]{3,2,1,0:T(8,128)S(1)}, u32[]{:S(2)}, u32[]{:S(2)}) collective-permute-start(f32[4,12,8,128]{3,2,1,0:T(8,128)S(1)} %get-tuple-element.47), channel_id=1, source_target_pairs={{0,1},{1,2},{2,3},{3,4},{4,5},{5,6},{6,7},{7,0},{8,9},{9,10},{10,1... | collective-permute-start | bytes 589832 | tf_op jit(solution)/shard_map/ppermute | solution.py:248
  41.8 7.8 %collective-permute-start.11 = (f32[4,12,8,128]{3,2,1,0:T(8,128)S(1)}, f32[4,12,8,128]{3,2,1,0:T(8,128)S(1)}, u32[]{:S(2)}, u32[]{:S(2)}) collective-permute-start(f32[4,12,8,128]{3,2,1,0:T(8,128)S(1)} %get-tuple-element.48), channel_id=1, source_target_pairs={{0,7},{1,0},{2,1},{3,2},{4,3},{5,4},{6,5},{7,6},{8,15},{9,8},{10,9... | collective-permute-start | bytes 589832 | tf_op jit(solution)/shard_map/ppermute | solution.py:248
  51.3 1.3 %collective-permute-start.12 = (f32[4,4,8,128]{3,2,1,0:T(8,128)S(1)}, f32[4,4,8,128]{3,2,1,0:T(8,128)S(1)}, u32[]{:S(2)}, u32[]{:S(2)}) collective-permute-start(f32[4,4,8,128]{3,2,1,0:T(8,128)S(1)} %dynamic-slice_bitcast_fusion), channel_id=1, source_target_pairs={{0,32},{32,0},{64,96},{96,64},{128,160},{160,128},{192,224},{224,1... | collective-permute-start | bytes 196616 | tf_op jit(solution)/shard_map/ppermute | solution.py:253
  52.7 6.6 %collective-permute-start.15 = (f32[4,8,128]{2,1,0:T(8,128)S(1)}, f32[4,8,128]{2,1,0:T(8,128)S(1)}, u32[]{:S(2)}, u32[]{:S(2)}) collective-permute-start(f32[4,8,128]{2,1,0:T(8,128)S(1)} %get-tuple-element.62), channel_id=1, source_target_pairs={{0,192},{32,224},{64,128},{96,160},{128,64},{160,96},{192,0},{224,... | collective-permute-start | bytes 49160 | tf_op jit(solution)/shard_map/ppermute | solution.py:253
  56.6 7.6 %collective-permute-start.14 = (f32[4,8,128]{2,1,0:T(8,128)S(1)}, f32[4,8,128]{2,1,0:T(8,128)S(1)}, u32[]{:S(2)}, u32[]{:S(2)}) collective-permute-start(f32[4,8,128]{2,1,0:T(8,128)S(1)} %get-tuple-element.63), channel_id=1, source_target_pairs={{0,128},{32,160},{64,192},{96,224},{128,0},{160,32},{192,64},{224,... | collective-permute-start | bytes 49160 | tf_op jit(solution)/shard_map/ppermute | solution.py:253
  57.9 6.4 %collective-permute-start.13 = (f32[4,8,128]{2,1,0:T(8,128)S(1)}, f32[4,8,128]{2,1,0:T(8,128)S(1)}, u32[]{:S(2)}, u32[]{:S(2)}) collective-permute-start(f32[4,8,128]{2,1,0:T(8,128)S(1)} %get-tuple-element.64), channel_id=1, source_target_pairs={{0,64},{32,96},{64,0},{96,32},{128,192},{160,224},{192,128},{224,1... | collective-permute-start | bytes 49160 | tf_op jit(solution)/shard_map/ppermute | solution.py:253
